TPU v7x, 32 devices: a whole 2x2x4 slice. The times are simulated.
32 devices in a mesh: frame: 8 (over z, x), head: 4 (over y, core).
Axes of the slice: x: 2, y: 2, z: 4, core: 2. Of those that a mesh axis runs over, the one named last changes fastest.
Arguments:
- features: bfloat16 [8, 96, 256, 1536], P(None, 'frame', None, 'head'), may hold values from -6 to 6
- lengths: int32 [8, 96], P(None, 'frame'), may hold values from 64 to 256, as said below
- loss_mask: int32 [8, 96, 256], P(None, 'frame'), may hold values from 0 to 1, as said below
- sq_weight: float32 [5, 1536, 1536], P(None, 'frame', 'head')
- sq_first: float32 [5, 1536, 1536], P(None, 'frame', 'head'), may hold values from -5.340576e-05 to 5.340576e-05
- sq_second: float32 [5, 1536, 1536], P(None, 'frame', 'head'), may hold values from 5.3897747e-11 to 2.1559099e-10
- ffn_weight: float32 [2, 1536, 6144], P(None, 'frame', 'head'), may hold values from -0.15625 to 0.15625
- ffn_first: float32 [2, 1536, 6144], P(None, 'frame', 'head'), may hold values from -5.340576e-05 to 5.340576e-05
- ffn_second: float32 [2, 1536, 6144], P(None, 'frame', 'head'), may hold values from 5.3897747e-11 to 2.1559099e-10
- left_bases: float32 [7, 32, 48, 48], P(None, 'frame'), may hold values from -1 to 1, as said below
- right_sq: float32 [5, 12, 128, 128], P(None, 'head'), may hold values from -1 to 1, as said below
- right_ffn: float32 [2, 48, 128, 128], P(None, 'head'), may hold values from -1 to 1, as said below
- latents: float32 [64, 1536], replicated, may hold values from -6 to 6
- lat_first: float32 [64, 1536], replicated, may hold values from -5.340576e-05 to 5.340576e-05
- lat_second: float32 [64, 1536], replicated, may hold values from 3.3686092e-12 to 1.3474437e-11
- time_embed: float32 [96, 1536], P('frame', 'head'), may hold values from -3 to 3
- time_first: float32 [96, 1536], P('frame', 'head'), may hold values from -5.340576e-05 to 5.340576e-05
- time_second: float32 [96, 1536], P('frame', 'head'), may hold values from 5.3897747e-11 to 2.1559099e-10
- gains: float32 [4, 1536], replicated, may hold values from 0.3 to 2.5
- gain_first: float32 [4, 1536], P(None, 'head'), may hold values from -5.340576e-05 to 5.340576e-05
- gain_second: float32 [4, 1536], P(None, 'head'), may hold values from 5.3897747e-11 to 2.1559099e-10
Outputs:
- loss_sum: float32 [], replicated
- masked_count: float32 [], replicated
- grad_norm: float32 [], replicated
- sq_new: float32 [5, 1536, 1536], P(None, 'frame', 'head')
- sq_first_new: float32 [5, 1536, 1536], P(None, 'frame', 'head')
- sq_second_new: float32 [5, 1536, 1536], P(None, 'frame', 'head')
- sq_low: bfloat16 [5, 1536, 1536], P(None, 'frame', 'head')
- ffn_new: float32 [2, 1536, 6144], P(None, 'frame', 'head')
- ffn_first_new: float32 [2, 1536, 6144], P(None, 'frame', 'head')
- ffn_second_new: float32 [2, 1536, 6144], P(None, 'frame', 'head')
- ffn_low: bfloat16 [2, 1536, 6144], P(None, 'frame', 'head')
- lat_new: float32 [64, 1536], replicated
- lat_first_new: float32 [64, 1536], replicated
- lat_second_new: float32 [64, 1536], replicated
- time_new: float32 [96, 1536], P('frame', 'head')
- time_first_new: float32 [96, 1536], P('frame', 'head')
- time_second_new: float32 [96, 1536], P('frame', 'head')
- gain_new: float32 [4, 1536], P(None, 'head')
- gain_first_new: float32 [4, 1536], P(None, 'head')
- gain_second_new: float32 [4, 1536], P(None, 'head')
Inputs may be any that keep to these rules, and one draw needn't show every extreme that they name: `lengths`: some frame has all 256 patches as keys. `loss_mask`: the first patch of every frame counts. `left_bases`: every block is an orthogonal matrix. `right_sq`: every block is an orthogonal matrix. `right_ffn`: every block is an orthogonal matrix.
All inputs are finite; a program needn't handle non-finite values.
Results may differ from a plain program's by a relative error of at most 0.015.
Values may be sent and summed in bfloat16 or wider, within the bound.
No kernel may reach another device: no remote copies, remote signals or barrier semaphores. Data moves between devices by JAX's collectives and lax.ppermute only.
A program may use at most 1 GiB of HBM per device.

v0:
```python
import jax
import jax.numpy as jnp
from jax import lax
from jax.sharding import PartitionSpec as P

HEAD_SIZE = 96
LATENTS = 64
PATCH = 256
FRAMES = 96
STEP = 5


HIGH_ACCURACY = lax.Precision.HIGHEST
clip_max = 0.05
beta_one = 0.5
beta_two = 0.6
adam_eps = 1e-08


def combined_all(value, axis, join):
    gathered = jax.tree.map(
        lambda a, kind: lax.all_gather(a.astype(kind), axis),
        value,
        (jnp.bfloat16, jnp.bfloat16, jnp.bfloat16),
    )

    def take(source):
        return jax.tree.map(
            lambda a, own: lax.dynamic_index_in_dim(a, source, 0, False).astype(own.dtype),
            gathered,
            value,
        )

    return lax.fori_loop(
        1, lax.axis_size(axis), lambda source, state: join(state, take(source)), take(0)
    )


def matmul(a, b):
    return jnp.dot(a, b, preferred_element_type=jnp.float32)


def left_tmul(a, b):
    return lax.dot_general(a, b, (((0,), (0,)), ((), ())), preferred_element_type=jnp.float32)


def right_tmul(a, b):
    return lax.dot_general(a, b, (((1,), (1,)), ((), ())), preferred_element_type=jnp.float32)


def normalize_rows(v):
    cent = v - jnp.mean(v, -1, keepdims=True)
    reciprocal_deviation = lax.rsqrt(jnp.mean(cent * cent, -1, keepdims=True) + 1e-05)
    return (cent * reciprocal_deviation, reciprocal_deviation)


def norm_reverse(gradient_tensor, centered_input, reciprocal_deviation, norm_gain):
    scaled_values = gradient_tensor * norm_gain
    running_mean_first = jnp.mean(scaled_values, -1, keepdims=True)
    running_mean_second = jnp.mean(scaled_values * centered_input, -1, keepdims=True)
    return reciprocal_deviation * (
        scaled_values - running_mean_first - centered_input * running_mean_second
    )


def rotate(gradient_tensor, left_basis, right_basis, inverse):
    slabs, row_count, col_count = gradient_tensor.shape
    bl = left_basis.shape[-1]
    br = right_basis.shape[-1]
    blocks = gradient_tensor.reshape(slabs, row_count // bl, bl, col_count // br, br)
    if inverse:
        out = jnp.einsum(
            "maij,majcl,mckl->maick", left_basis, blocks, right_basis, precision=HIGH_ACCURACY
        )
    else:
        out = jnp.einsum(
            "maij,maick,mckl->majcl", left_basis, blocks, right_basis, precision=HIGH_ACCURACY
        )
    return out.reshape(slabs, row_count, col_count)


def adam_moments(gradient_tensor, moment_one, moment_two):
    moment_one = beta_one * moment_one + (1.0 - beta_one) * gradient_tensor
    moment_two = beta_two * moment_two + (1.0 - beta_two) * gradient_tensor * gradient_tensor
    adam_step = (
        moment_one
        / (1.0 - beta_one**STEP)
        / (jnp.sqrt(moment_two / (1.0 - beta_two**STEP)) + adam_eps)
    )
    return (moment_one, moment_two, adam_step)


def soap_update(weight, gradient_tensor, moment_one, moment_two, left_basis, right_basis, rates):
    moment_one, moment_two, adam_step = adam_moments(
        rotate(gradient_tensor, left_basis, right_basis, False), moment_one, moment_two
    )
    updated = weight - rates[:, None, None] * (
        rotate(adam_step, left_basis, right_basis, True) + 0.01 * weight
    )
    return (updated, moment_one, moment_two, updated.astype(jnp.bfloat16))


def adamw_update(weight, gradient_tensor, moment_one, moment_two, decay):
    moment_one, moment_two, adam_step = adam_moments(gradient_tensor, moment_one, moment_two)
    return (weight - 0.3 * (adam_step + decay * weight), moment_one, moment_two)


def combine(earlier, later):
    peak_a, sums_a, outs_a = earlier
    peak_b, sums_b, outs_b = later
    highest = jnp.maximum(peak_a, peak_b)
    fac_a = jnp.exp(peak_a - highest)
    fac_b = jnp.exp(peak_b - highest)
    return (
        highest,
        sums_a * fac_a + sums_b * fac_b,
        outs_a * fac_a[..., None] + outs_b * fac_b[..., None],
    )


def per_device(
    features,
    lengths,
    loss_mask,
    sq_weight,
    sq_first,
    sq_second,
    ffn_weight,
    ffn_first,
    ffn_second,
    left_bases,
    right_sq,
    right_ffn,
    latents,
    lat_first,
    lat_second,
    time_embed,
    time_first,
    time_second,
    gains,
    gain_first,
    gain_second,
):
    videos, frames_dev, patches, cols = features.shape
    lat_count, feature_width = latents.shape
    heads_dev = cols // HEAD_SIZE
    rows_dev = sq_weight.shape[1]
    inv_root = HEAD_SIZE ** (-0.5)
    frame_idx = lax.axis_index("frame")
    head_idx = lax.axis_index("head")
    first_frame = (frame_idx == 0).astype(jnp.float32)
    first_head = (head_idx == 0).astype(jnp.float32)
    row_count = videos * lat_count
    row_weight = first_head * first_frame
    sq_full, ffn_full = (
        lax.all_gather(sq_weight.astype(jnp.bfloat16), "frame", axis=1, tiled=True),
        lax.all_gather(ffn_weight.astype(jnp.bfloat16), "frame", axis=1, tiled=True),
    )
    w_query, w_outt, w_dec = (sq_full[0], sq_full[3], sq_full[4])
    w_keyval = jnp.concatenate([sq_full[1], sq_full[2]], 1)
    w_up, w_downt = (ffn_full[0], ffn_full[1])
    local_rows = features.astype(jnp.float32) + time_embed[None, :, None, :]
    collected_rows = lax.all_gather(local_rows.astype(jnp.bfloat16), "head", axis=3, tiled=True)
    centered_input, input_reciprocal_deviation = normalize_rows(
        collected_rows.reshape(-1, feature_width).astype(jnp.float32)
    )
    normalized_input = (centered_input * gains[0]).astype(jnp.bfloat16)
    keyvals = matmul(normalized_input, w_keyval).astype(jnp.bfloat16)
    key_x = keyvals[:, :cols].reshape(videos, -1, heads_dev, HEAD_SIZE)
    val_x = keyvals[:, cols:].reshape(videos, -1, heads_dev, HEAD_SIZE)
    zhat_zero, zrstd_zero = normalize_rows(latents)
    normed_lat = (zhat_zero * gains[1]).astype(jnp.bfloat16)
    query = matmul(normed_lat, w_query).astype(jnp.bfloat16)
    keyval_lat = matmul(normed_lat, w_keyval).astype(jnp.bfloat16)
    query_by_head = query.reshape(lat_count, heads_dev, HEAD_SIZE)
    latent_key = keyval_lat[:, :cols].reshape(lat_count, heads_dev, HEAD_SIZE).astype(jnp.float32)
    latent_value = keyval_lat[:, cols:].reshape(lat_count, heads_dev, HEAD_SIZE).astype(jnp.float32)
    valid_key = (
        lax.broadcasted_iota(jnp.int32, (videos, frames_dev, patches), 2) < lengths[:, :, None]
    ).reshape(videos, -1)

    def patch_scores(keys_now):
        scores = (
            jnp.einsum(
                "lhd,vphd->vhlp", query_by_head, keys_now, preferred_element_type=jnp.float32
            )
            * inv_root
        )
        return jnp.where(valid_key[:, None, None, :], scores, -1e30)

    scores = patch_scores(key_x)
    peak = jnp.max(scores, -1)
    expo = jnp.exp(scores - peak[..., None])
    partial_value = jnp.einsum(
        "vhlp,vphd->vhld", expo, val_x.astype(jnp.float32), precision=HIGH_ACCURACY
    )
    peak, sums, partial_value = combined_all(
        (peak, jnp.sum(expo, -1), partial_value), "frame", combine
    )
    lat_scores = (
        jnp.einsum(
            "qrn,trn->rqt", query_by_head.astype(jnp.float32), latent_key, precision=HIGH_ACCURACY
        )
        * inv_root
    )
    highest = jnp.maximum(peak, jnp.max(lat_scores, -1)[None])
    latent_exponent = jnp.exp(lat_scores[None] - highest[..., None])
    shrink = jnp.exp(peak - highest)
    lat_total = sums * shrink + jnp.sum(latent_exponent, -1)
    outs = partial_value * shrink[..., None] + jnp.einsum(
        "caws,sax->cawx", latent_exponent, latent_value, precision=HIGH_ACCURACY
    )
    attn = outs / lat_total[..., None]
    lse = highest + jnp.log(lat_total)
    attn_low = attn.transpose(0, 2, 1, 3).reshape(videos * lat_count, cols).astype(jnp.bfloat16)
    lat_rows = jnp.broadcast_to(latents[None], (videos, lat_count, feature_width)).reshape(
        videos * lat_count, feature_width
    )
    z_one = lat_rows + lax.psum(right_tmul(attn_low, w_outt).astype(jnp.bfloat16), "head").astype(
        jnp.float32
    )
    z1hat, z1rstd = normalize_rows(z_one)
    ffn_in = (z1hat * gains[2]).astype(jnp.bfloat16)
    pre = matmul(ffn_in, w_up)
    hidden = jax.nn.gelu(pre).astype(jnp.bfloat16)
    z_two = z_one + lax.psum(right_tmul(hidden, w_downt).astype(jnp.bfloat16), "head").astype(
        jnp.float32
    )
    z2hat, z2rstd = normalize_rows(z_two)
    final = (z2hat * gains[3]).astype(jnp.bfloat16)
    dec_query = matmul(final, w_query).astype(jnp.bfloat16)
    dec_value = matmul(final, w_dec).astype(jnp.bfloat16)
    dec_query = dec_query.reshape(videos, lat_count, heads_dev, HEAD_SIZE)
    dec_value = dec_value.reshape(videos, lat_count, heads_dev, HEAD_SIZE)
    dscores = (
        jnp.einsum("vphd,vlhd->vphl", key_x, dec_query, preferred_element_type=jnp.float32)
        * inv_root
    )
    dprobs = jax.nn.softmax(dscores, -1)
    dec_value_f = dec_value.astype(jnp.float32)
    pred = jnp.einsum("vphl,vlhd->vphd", dprobs, dec_value_f, precision=HIGH_ACCURACY).reshape(
        features.shape
    )
    mask_float = loss_mask.astype(jnp.float32)[..., None]
    error_pred = pred - features.astype(jnp.float32)
    loss_part = jnp.sum(mask_float * error_pred * error_pred)
    count_part = jnp.sum(loss_mask.astype(jnp.float32)) * first_head
    dpred = (2.0 * mask_float * error_pred).reshape(videos, -1, heads_dev, HEAD_SIZE)
    dprob_grad = jnp.einsum("vphd,vlhd->vphl", dpred, dec_value_f, precision=HIGH_ACCURACY)
    dscore_grad = dprobs * (dprob_grad - jnp.sum(dprobs * dprob_grad, -1, keepdims=True)) * inv_root
    ddv_part = jnp.einsum("vphl,vphd->vlhd", dprobs, dpred, precision=HIGH_ACCURACY).reshape(
        videos * lat_count, cols
    )
    ddq_part = jnp.einsum(
        "vphl,vphd->vlhd", dscore_grad, key_x.astype(jnp.float32), precision=HIGH_ACCURACY
    ).reshape(videos * lat_count, cols)
    dkey_dec = jnp.einsum(
        "vphl,vlhd->vphd", dscore_grad, dec_query.astype(jnp.float32), precision=HIGH_ACCURACY
    )
    ddq, ddv = (
        lax.psum(ddq_part.astype(jnp.bfloat16), "frame").astype(jnp.float32),
        lax.psum(ddv_part.astype(jnp.bfloat16), "frame").astype(jnp.float32),
    )
    ddq_low = ddq.astype(jnp.bfloat16)
    ddv_low = ddv.astype(jnp.bfloat16)
    dfinal = lax.psum(
        (right_tmul(ddq_low, w_query) + right_tmul(ddv_low, w_dec)).astype(jnp.bfloat16), "head"
    ).astype(jnp.float32)
    dz_two = norm_reverse(dfinal, z2hat, z2rstd, gains[3])
    dz2_low = dz_two.astype(jnp.bfloat16)
    _, gelu_back = jax.vjp(jax.nn.gelu, pre)
    dpre = gelu_back(matmul(dz2_low, w_downt))[0].astype(jnp.bfloat16)
    dffn_in = lax.psum(right_tmul(dpre, w_up).astype(jnp.bfloat16), "head").astype(jnp.float32)
    dz_one = dz_two + norm_reverse(dffn_in, z1hat, z1rstd, gains[2])
    dz1_low = dz_one.astype(jnp.bfloat16)
    row_ids = lax.broadcasted_iota(jnp.int32, (row_count, lat_count), 0) % lat_count
    onehot = (row_ids == lax.broadcasted_iota(jnp.int32, (row_count, lat_count), 1)).astype(
        jnp.float32
    )
    lat_direct = lax.dot_general(onehot, dz_one, (((0,), (0,)), ((), ())), precision=HIGH_ACCURACY)
    row_part = (
        jnp.concatenate(
            [lat_direct, jnp.sum(dffn_in * z1hat, 0)[None], jnp.sum(dfinal * z2hat, 0)[None]], 0
        )
        * row_weight
    )
    grad_downt = left_tmul(dz2_low, hidden)
    grad_up = left_tmul(ffn_in, dpre)
    grad_outt = left_tmul(dz1_low, attn_low)
    attention_gradient = (
        matmul(dz1_low, w_outt)
        .reshape(videos, lat_count, heads_dev, HEAD_SIZE)
        .transpose(0, 2, 1, 3)
    )
    delta = jnp.sum(attention_gradient * attn, -1)
    probs = jnp.exp(patch_scores(key_x) - lse[..., None])
    dprob_x = jnp.einsum(
        "vhld,vphd->vhlp", attention_gradient, val_x.astype(jnp.float32), precision=HIGH_ACCURACY
    )
    dscore_x = probs * (dprob_x - delta[..., None]) * inv_root
    dval_x = jnp.einsum("vhlp,vhld->vphd", probs, attention_gradient, precision=HIGH_ACCURACY)
    query_wide_float = query_by_head.astype(jnp.float32)
    dkey_att = jnp.einsum("vhlp,lhd->vphd", dscore_x, query_wide_float, precision=HIGH_ACCURACY)
    dq_part = jnp.einsum(
        "vhlp,vphd->lhd", dscore_x, key_x.astype(jnp.float32), precision=HIGH_ACCURACY
    )
    latent_probabilities = jnp.exp(lat_scores[None] - lse[..., None])
    latent_prob_gradient = jnp.einsum(
        "oawn,tan->oawt", attention_gradient, latent_value, precision=HIGH_ACCURACY
    )
    latent_score_gradient = (
        latent_probabilities * (latent_prob_gradient - delta[..., None]) * inv_root
    )
    dq_part = dq_part + first_frame * jnp.einsum(
        "iepx,xeu->peu", latent_score_gradient, latent_key, precision=HIGH_ACCURACY
    )
    latent_key_gradient = jnp.einsum(
        "onbc,bns->cns", latent_score_gradient, query_wide_float, precision=HIGH_ACCURACY
    ).reshape(lat_count, cols)
    latent_value_gradient = jnp.einsum(
        "qugr,qugc->ruc", latent_probabilities, attention_gradient, precision=HIGH_ACCURACY
    ).reshape(lat_count, cols)
    dkv_lat = jnp.concatenate([latent_key_gradient, latent_value_gradient], 1).astype(jnp.bfloat16)
    dquery = (
        lax.psum(dq_part.astype(jnp.bfloat16), "frame")
        .astype(jnp.float32)
        .reshape(lat_count, cols)
        .astype(jnp.bfloat16)
    )
    dkv_x = jnp.concatenate(
        [(dkey_att + dkey_dec).reshape(-1, cols), dval_x.reshape(-1, cols)], 1
    ).astype(jnp.bfloat16)
    grad_kv_part = left_tmul(normalized_input, dkv_x) + first_frame * left_tmul(normed_lat, dkv_lat)
    dzn_part = right_tmul(dquery, w_query) + right_tmul(dkv_lat, w_keyval)
    normalized_gradient = right_tmul(dkv_x, w_keyval)
    flattened_gradient = norm_reverse(
        normalized_gradient, centered_input, input_reciprocal_deviation, gains[0]
    )
    time_part = jnp.sum(
        flattened_gradient.reshape(videos, frames_dev, patches, feature_width), (0, 2)
    )
    time_pad = lax.dynamic_update_slice_in_dim(
        jnp.zeros((FRAMES, feature_width), jnp.float32), time_part, frame_idx * frames_dev, 0
    )
    gain0_portion = jnp.sum(normalized_gradient * centered_input, 0)
    dzn, time_grad, grad_gain0, row_sum = lax.psum(
        (dzn_part * first_frame, time_pad, gain0_portion, row_part), ("frame", "head")
    )
    grad_gain1 = jnp.sum(dzn * zhat_zero, 0)
    lat_grad = row_sum[:lat_count] + norm_reverse(dzn, zhat_zero, zrstd_zero, gains[1])
    grad_gain2 = row_sum[lat_count]
    grad_gain3 = row_sum[lat_count + 1]
    grad_query = left_tmul(normed_lat, dquery) + left_tmul(final, ddq_low)
    grad_dec = left_tmul(final, ddv_low)
    stacked_kv = grad_kv_part.reshape(feature_width, 2, cols).transpose(1, 0, 2)
    grad_kv = lax.psum_scatter(
        stacked_kv.astype(jnp.bfloat16), "frame", scatter_dimension=1, tiled=True
    ).astype(jnp.float32)

    def own_rows(matrix):
        return lax.dynamic_slice_in_dim(matrix, frame_idx * rows_dev, rows_dev, 0)

    sq_grad = jnp.stack(
        [own_rows(grad_query), grad_kv[0], grad_kv[1], own_rows(grad_outt), own_rows(grad_dec)]
    )
    ffn_grad = jnp.stack([own_rows(grad_up), own_rows(grad_downt)])
    time_own = lax.dynamic_slice(
        time_grad, (frame_idx * frames_dev, head_idx * cols), (frames_dev, cols)
    )
    gain_grad = lax.dynamic_slice_in_dim(
        jnp.stack([grad_gain0, grad_gain1, grad_gain2, grad_gain3]), head_idx * cols, cols, 1
    )
    squares = (
        jnp.sum(sq_grad * sq_grad) + jnp.sum(ffn_grad * ffn_grad) + jnp.sum(time_own * time_own)
    )
    squares = (
        squares
        + first_frame * first_head * jnp.sum(lat_grad * lat_grad)
        + first_frame * jnp.sum(gain_grad * gain_grad)
    )
    loss_sum, masked_count, squares = lax.psum((loss_part, count_part, squares), ("frame", "head"))
    grad_norm = jnp.sqrt(squares) / masked_count
    factor = jnp.minimum(1.0, clip_max / grad_norm) / masked_count
    out_rate = ((FRAMES * PATCH + LATENTS) / 64.0) ** 0.5
    sq_rates = jnp.array([1.0, 1.0, 1.0, out_rate, 1.0], jnp.float32) * 0.02
    ffn_rates = jnp.array([0.02, 0.02], jnp.float32)
    sq_out = soap_update(
        sq_weight, sq_grad * factor, sq_first, sq_second, left_bases[:5], right_sq, sq_rates
    )
    ffn_out = soap_update(
        ffn_weight, ffn_grad * factor, ffn_first, ffn_second, left_bases[5:], right_ffn, ffn_rates
    )
    lat_out = adamw_update(latents, lat_grad * factor, lat_first, lat_second, 0.01)
    time_out = adamw_update(time_embed, time_own * factor, time_first, time_second, 0.01)
    gain_own = lax.dynamic_slice_in_dim(gains, head_idx * cols, cols, 1)
    gain_out = adamw_update(gain_own, gain_grad * factor, gain_first, gain_second, 0.0)
    return (
        loss_sum,
        masked_count,
        grad_norm,
        sq_out[0],
        sq_out[1],
        sq_out[2],
        sq_out[3],
        ffn_out[0],
        ffn_out[1],
        ffn_out[2],
        ffn_out[3],
        lat_out[0],
        lat_out[1],
        lat_out[2],
        time_out[0],
        time_out[1],
        time_out[2],
        gain_out[0],
        gain_out[1],
        gain_out[2],
    )


def solution(mesh):
    placed = (
        P(None, "frame", None, "head"),
        P(None, "frame"),
        P(None, "frame", None),
        P(None, "frame", "head"),
        P(None, "frame", "head"),
        P(None, "frame", "head"),
        P(None, "frame", "head"),
        P(None, "frame", "head"),
        P(None, "frame", "head"),
        P(None, "frame", None, None),
        P(None, "head", None, None),
        P(None, "head", None, None),
        P(),
        P(),
        P(),
        P("frame", "head"),
        P("frame", "head"),
        P("frame", "head"),
        P(),
        P(None, "head"),
        P(None, "head"),
    )
    return jax.shard_map(
        per_device,
        mesh=mesh,
        in_specs=placed,
        out_specs=(
            P(),
            P(),
            P(),
            P(None, "frame", "head"),
            P(None, "frame", "head"),
            P(None, "frame", "head"),
            P(None, "frame", "head"),
            P(None, "frame", "head"),
            P(None, "frame", "head"),
            P(None, "frame", "head"),
            P(None, "frame", "head"),
            P(),
            P(),
            P(),
            P("frame", "head"),
            P("frame", "head"),
            P("frame", "head"),
            P(None, "head"),
            P(None, "head"),
            P(None, "head"),
        ),
        check_vma=False,
    )
```

profile of v0, /device:TPU:0, one launch (start us, length us, event | category | flops | bytes accessed | tf_op | source)
XLA Modules:
  0.0 3189.5 jit_solution(8663634521941728638)
XLA Ops:
  66.7 41.0 %all-gather.10.cloned.1.call-done = bf16[5,1536,384]{2,1,0:T(8,128)(2,1)} async-done(((bf16[5,192,384]{2,1,0:T(8,128)(2,1)}), bf16[5,1536,384]{2,1,0:T(8,128)(2,1)}) %all-gather.10.cloned.1.call-update) | async-done | bytes 5898256 | tf_op jit(solution)/shard_map/all_gather | solution.py:156
  114.1 577.5 %all-gather.8.cloned.1.call-done = bf16[8,12,256,1536]{2,1,3,0:T(8,128)(2,1)} async-done(((bf16[8,12,256,384]{2,1,3,0:T(8,128)(2,1)}), bf16[8,12,256,1536]{2,1,3,0:T(8,128)(2,1)}) %all-gather.8.cloned.1.call-update) | async-done | bytes 75497488 | tf_op jit(solution)/shard_map/all_gather | solution.py:163
  722.5 38.0 %multiply_reduce_fusion = f32[8,12,256]{2,1,0:T(8,128)S(1)} fusion(bf16[8,12,256,1536]{2,1,3,0:T(8,128)(2,1)} %all-gather.8.cloned.1.call-done, f32[8,12,256]{2,1,0:T(8,128)S(1)} %broadcast_multiply_fusion.3), kind=kLoop, calls=%fused_computation.9 | loop fusion | flops 150970368 | bytes 75694080 | tf_op jit(solution)/shard_map/reduce_sum | solution.py:53
  760.6 142.6 %copy.156 = f32[8,12,256,1536]{3,2,1,0:T(8,128)} copy(bf16[8,12,256,1536]{2,1,3,0:T(8,128)(2,1)} %all-gather.8.cloned.1.call-done) | data formatting | bytes 226492416 | tf_op jit(solution)/shard_map/convert_element_type | solution.py:165
  903.3 72.5 %multiply_convert_fusion = bf16[24576,1536]{1,0:T(8,128)(2,1)} fusion(f32[8,12,256,1536]{3,2,1,0:T(8,128)} %copy.156, f32[1536]{0:T(1024)S(1)} %get-tuple-element.215, f32[24576]{0:T(1024)S(1)} %rsqrt.36, f32[24576]{0:T(1024)S(1)} %div.151), kind=kLoop, calls=%fused_computation.15 | loop fusion | flops 150994944 | bytes 226695168 | tf_op jit(solution)/shard_map/convert_element_type | solution.py:167
  975.8 67.7 %convolution_convert_fusion = bf16[24576,768]{1,0:T(8,128)(2,1)} fusion(bf16[24576,1536]{1,0:T(8,128)(2,1)} %multiply_convert_fusion, bf16[1536,384]{1,0:T(8,128)(2,1)S(1)} %copy-done.39, bf16[1536,384]{1,0:T(8,128)(2,1)} %get-tuple-element.274), kind=kOutput, calls=%fused_computation.23 | convolution fusion | flops 58005651456 | bytes 115605504 | tf_op jit(solution)/shard_map/dot_general | solution.py:40
  1209.2 51.5 %fusion.111 = bf16[8,4,64,96]{3,2,1,0:T(8,128)(2,1)} fusion(bf16[8,3072,4,96]{1,0,3,2:T(8,128)(2,1)} %bitcast.328, f32[8,4,64,3072]{3,2,0,1:T(8,128)} %get-tuple-element.267), kind=kOutput, calls=%fused_computation.168 | convolution fusion | flops 7247953920 | bytes 44433408 | tf_op jit(solution)/shard_map/vhlp,vphd->vhld/dot_general | solution.py:194
  1294.0 31.1 all-gather.1
  1361.9 38.5 %all-reduce.10.cloned.1.call-done = bf16[512,1536]{1,0:T(8,128)(2,1)} async-done(((bf16[512,1536]{1,0:T(8,128)(2,1)}), bf16[512,1536]{1,0:T(8,128)(2,1)}) %all-reduce.10.cloned.1.call-update) | async-done | bytes 1572880 | tf_op jit(solution)/shard_map/psum | solution.py:219
  1406.7 134.4 %all-gather.12.cloned.1.call-done = bf16[2,1536,1536]{2,1,0:T(8,128)(2,1)} async-done(((bf16[2,192,1536]{2,1,0:T(8,128)(2,1)}), bf16[2,1536,1536]{2,1,0:T(8,128)(2,1)}) %all-gather.12.cloned.1.call-update) | async-done | bytes 9437200 | tf_op jit(solution)/shard_map/all_gather | solution.py:157
  1555.7 37.3 %all-reduce.12.cloned.1.call-done = bf16[512,1536]{1,0:T(8,128)(2,1)} async-done(((bf16[512,1536]{1,0:T(8,128)(2,1)}), bf16[512,1536]{1,0:T(8,128)(2,1)}) %all-reduce.12.cloned.1.call-update) | async-done | bytes 1572880 | tf_op jit(solution)/shard_map/psum | solution.py:226
  1604.0 38.1 %fusion.37 = f32[8,4,64,3072]{3,2,0,1:T(8,128)} fusion(bf16[8,3072,4,96]{1,0,3,2:T(8,128)(2,1)} %bitcast.325, bf16[8,64,4,96]{3,2,1,0:T(4,128)(2,1)S(1)} %reshape.308), kind=kOutput, calls=%fused_computation.63 | convolution fusion | flops 1207959552 | bytes 44433408 | tf_op jit(solution)/shard_map/vphd,vlhd->vphl/dot_general | solution.py:236
  1697.9 45.2 %reshape.309 = f32[8,12,256,384]{2,1,3,0:T(8,128)} reshape(f32[8,3072,4,96]{1,3,2,0:T(8,128)} %fusion.41) | data formatting | bytes 75497472 | tf_op jit(solution)/shard_map/reshape | solution.py:241
  1743.1 41.1 %fusion.10 = (f32[8,12,256,384]{2,1,3,0:T(8,128)}, f32[]{:T(128)}) fusion(f32[8,12,256,384]{2,1,3,0:T(8,128)} %reshape.309, bf16[8,12,256,384]{2,1,3,0:T(8,128)(2,1)} %copy.154, f32[8,12,256]{2,1,0:T(8,128)S(1)} %copy-done.53, f32[8,12,256]{2,1,0:T(8,128)S(1)} %copy-done.52), kind=kLoop, calls=%fused_computation.28 | loop fusion | flops 56623104 | bytes 94568448 | tf_op jit(solution)/shard_map/mul | solution.py:248
  1784.2 45.1 %reshape.310 = f32[8,3072,4,96]{1,3,2,0:T(8,128)} reshape(f32[8,12,256,384]{2,1,3,0:T(8,128)} %get-tuple-element.268) | data formatting | bytes 75497472 | tf_op jit(solution)/shard_map/reshape | solution.py:248
  1829.3 46.8 %fusion.127 = bf16[8,64,4,96]{3,1,2,0:T(8,128)(2,1)S(1)} fusion(f32[8,3072,4,96]{1,3,2,0:T(8,128)} %reshape.310, f32[8,3072,4,64]{1,3,0,2:T(8,128)} %get-tuple-element.289, f32[8,3072,4]{1,0,2:T(8,128)S(1)} %get-tuple-element.288), kind=kOutput, calls=%fused_computation.174 | convolution fusion | flops 7254245376 | bytes 63700992 | tf_op jit(solution)/shard_map/vphl,vphd->vlhd/dot_general | solution.py:251
  1876.0 34.8 %fusion.11 = (f32[8,3072,4]{1,0,2:T(8,128)}, f32[8,4,64,3072]{3,2,0,1:T(8,128)}) fusion(f32[8,3072,4,96]{1,3,2,0:T(8,128)} %reshape.310, bf16[8,64,4,96]{3,2,1,0:T(4,128)(2,1)S(1)} %reshape.307, f32[8,3072,4,64]{1,3,0,2:T(8,128)} %get-tuple-element.289, f32[8,3072,4]{1,0,2:T(8,128)S(1)} %get-tuple-element.288), kind=kOutput, calls=%fused_computation.31 | convolution fusion | flops 7266533376 | bytes 89260032 | tf_op jit(solution)/shard_map/vphd,vlhd->vphl/dot_general | solution.py:249
  1938.3 50.7 %fusion.122 = bf16[8,64,4,96]{3,1,2,0:T(8,128)(2,1)S(1)} fusion(f32[8,3072,4,64]{1,3,0,2:T(8,128)} %fusion.13, bf16[8,3072,4,96]{1,0,3,2:T(8,128)(2,1)} %bitcast.326), kind=kOutput, calls=%fused_computation.173 | convolution fusion | flops 7247953920 | bytes 44433408 | tf_op jit(solution)/shard_map/vphl,vphd->vlhd/dot_general | solution.py:254
  1990.6 75.0 %all-reduce.20.cloned.1.call-done = (bf16[512,384]{1,0:T(8,128)(2,1)}, bf16[512,384]{1,0:T(8,128)(2,1)}) async-done(((bf16[512,384]{1,0:T(8,128)(2,1)}, bf16[512,384]{1,0:T(8,128)(2,1)}), (bf16[512,384]{1,0:T(8,128)(2,1)}, bf16[512,384]{1,0:T(8,128)(2,1)})) %all-reduce.20.cloned.1.call-update) | async-done | bytes 786448 | tf_op jit(solution)/shard_map/psum | solution.py:262
  2071.8 42.0 %all-reduce.14.cloned.1.call-done = bf16[512,1536]{1,0:T(8,128)(2,1)} async-done(((bf16[512,1536]{1,0:T(8,128)(2,1)}), bf16[512,1536]{1,0:T(8,128)(2,1)}) %all-reduce.14.cloned.1.call-update) | async-done | bytes 1572880 | tf_op jit(solution)/shard_map/psum | solution.py:266
  2138.0 38.2 %all-reduce.16.cloned.1.call-done = bf16[512,1536]{1,0:T(8,128)(2,1)} async-done(((bf16[512,1536]{1,0:T(8,128)(2,1)}), bf16[512,1536]{1,0:T(8,128)(2,1)}) %all-reduce.16.cloned.1.call-update) | async-done | bytes 1572880 | tf_op jit(solution)/shard_map/psum | solution.py:273
  2188.0 49.3 %multiply_multiply_fusion.1 = f32[8,4,64,3072]{3,2,0,1:T(8,128)} fusion(f32[8,4,64]{2,0,1:T(8,128)S(1)} %get-tuple-element.292, f32[8,4,64,96]{3,2,0,1:T(8,128)S(1)} %get-tuple-element.293, bf16[8,3072,4,96]{1,0,3,2:T(8,128)(2,1)} %bitcast.329, f32[8,4,64]{2,0,1:T(8,128)S(1)} %copy-done.38, f32[4,8,3072,64]{2,3,1,0:T(8,128)} %get-tuple-element.285, ...), kind=kOutput, calls=%fused_computation.49 | convolution fusion | flops 7285506048 | bytes 70033408 | tf_op jit(solution)/shard_map/vhld,vphd->vhlp/dot_general | solution.py:297
  2237.3 40.3 %convert_bitcast_fusion = bf16[8,3072,4,96]{1,3,2,0:T(8,128)(2,1)} fusion(f32[8,4,64,96]{3,2,0,1:T(8,128)S(1)} %get-tuple-element.293, f32[4,8,3072,64]{2,3,1,0:T(8,128)} %get-tuple-element.285, f32[8,4,64]{2,0,1:T(8,128)S(1)} %copy-done.38, pred[8,3072]{1,0:T(8,128)(4,1)S(1)} %copy-done.20), kind=kOutput, calls=%fused_computation.60 | convolution fusion | flops 7276068864 | bytes 44859392 | tf_op jit(solution)/shard_map/vhlp,vhld->vphd/dot_general | solution.py:301
  2277.6 50.8 %fusion.133 = f32[4,96,64]{1,2,0:T(8,128)S(1)} fusion(f32[8,4,64,3072]{3,2,0,1:T(8,128)} %multiply_multiply_fusion.1, bf16[8,3072,4,96]{1,0,3,2:T(8,128)(2,1)} %bitcast.327), kind=kOutput, calls=%fused_computation.186 | convolution fusion | flops 7247757312 | bytes 44138496 | tf_op jit(solution)/shard_map/vhlp,vphd->lhd/dot_general | solution.py:304
  2359.6 38.1 %psum.106 = bf16[64,384]{1,0:T(8,128)(2,1)} all-reduce(bf16[64,384]{1,0:T(8,128)(2,1)S(1)} %convert_element_type.308), channel_id=1, replica_groups=mesh['frame'=8,'head'=4] {'frame'}, use_global_device_ids=true, to_apply=%region_33.34 | all-reduce | flops 24576 | bytes 98304 | tf_op jit(solution)/shard_map/psum | solution.py:325
  2524.2 128.5 %multiply_reduce_fusion.1 = (f32[1536]{0:T(1024)}, f32[24576]{0:T(1024)S(1)}, f32[24576]{0:T(1024)S(1)}, f32[24576,1536]{1,0:T(8,128)}) fusion(f32[8,12,256,1536]{3,2,1,0:T(8,128)} %copy.156, f32[24576]{0:T(1024)S(1)} %copy-done.49, f32[24576]{0:T(1024)S(1)} %copy-done.47, f32[1536]{0:T(1024)S(1)} %copy-done.70, ...), kind=kOutput, calls=%fused_computation.12 | convolution fusion | flops 58288717824 | bytes 342503424 | tf_op jit(solution)/shard_map/dot_general | solution.py:48
  2652.8 142.1 %subtract_multiply_fusion = f32[24576,1536]{1,0:T(8,128)} fusion(f32[24576,1536]{1,0:T(8,128)} %get-tuple-element.294, f32[8,12,256,1536]{3,2,1,0:T(8,128)} %copy.156, f32[24576]{0:T(1024)S(1)} %broadcast_multiply_fusion.4, f32[24576]{0:T(1024)S(1)} %broadcast_multiply_fusion.5, f32[1536]{0:T(1024)S(1)} %copy-done.70, f32[24576]{0:T(1024)S(1)} %copy-done.49, ...), kind=kLoop, calls=%fused_computation.13 | loop fusion | flops 264241152 | bytes 453384192 | tf_op jit(solution)/shard_map/mul | solution.py:61
  2794.9 45.5 %reduce_sum.334 = f32[12,1536]{1,0:T(8,128)S(1)} reduce(f32[8,12,256,1536]{3,2,1,0:T(8,128)} %bitcast.54, f32[]{:T(128)} %constant.178.clone.1), dimensions={0,2}, to_apply=%region_39.40 | reduce | flops 37730304 | bytes 151068672 | tf_op jit(solution)/shard_map/reduce_sum | solution.py:339
  2850.5 65.4 %fusion.218 = f32[1536,768]{0,1:T(8,128)S(1)} fusion(bf16[24576,768]{0,1:T(8,128)(2,1)} %constant_dynamic-update-slice_fusion, bf16[24576,1536]{1,0:T(8,128)(2,1)} %multiply_convert_fusion), kind=kOutput, calls=%fused_computation.336 | convolution fusion | flops 57982058496 | bytes 117964800 | tf_op jit(solution)/shard_map/dot_general | solution.py:44
  2960.0 37.3 %psum.110 = f32[1,1536]{1,0:T(1,128)S(1)} all-reduce(f32[1,1536]{1,0:T(1,128)S(1)} %stack.55), channel_id=1, replica_groups=mesh['frame'=8,'head'=4] {'frame','head'}, use_global_device_ids=true, to_apply=%region_50.51 | all-reduce | flops 1536 | bytes 12288 | tf_op jit(solution)/shard_map/psum | solution.py:346
  3007.2 45.4 %reduce-scatter.2.cloned.1.call-done = bf16[2,192,384]{2,1,0:T(8,128)(2,1)} async-done(((bf16[2,1536,384]{2,1,0:T(8,128)(2,1)}), bf16[2,192,384]{2,1,0:T(8,128)(2,1)}) %reduce-scatter.2.cloned.1.call-update) | async-done | bytes 294928 | tf_op jit(solution)/shard_map/reduce_scatter | solution.py:356
  3059.9 39.9 %all-reduce = (f32[]{:T(128)}, f32[]{:T(128)}, f32[]{:T(128)}) all-reduce(f32[]{:T(128)} %get-tuple-element.269, f32[]{:T(128)S(6)} %mul.691, f32[]{:T(128)S(6)} %add.331), channel_id=1, replica_groups=mesh['frame'=8,'head'=4] {'frame','head'}, use_global_device_ids=true, to_apply=%region_19.20 | all-reduce | flops 3 | bytes 24 | tf_op jit(solution)/shard_map/psum | solution.py:381
  (453 shorter events, 808.6 us)
Async XLA Ops:
  7.2 3108.5 %copy-start = (f32[2,12,128,128]{3,2,1,0:T(8,128)S(1)}, f32[2,12,128,128]{3,2,1,0:T(8,128)}, u32[]{:S(2)}) copy-start(f32[2,12,128,128]{3,2,1,0:T(8,128)} %param.36) | copy-start | bytes 4718596
  7.2 100.6 %all-gather.10.cloned.1.call-start = ((), (), s32[]{:S(2)}) async-start(), calls=%async_computation.2 | async-start | bytes 6635520 | tf_op jit(solution)/shard_map/all_gather | solution.py:156
  9.7 681.9 %all-gather.8.cloned.1.call-start = ((), (), s32[]{:S(2)}) async-start(), calls=%async_computation.1 | async-start | bytes 125829120 | tf_op jit(solution)/shard_map/all_gather | solution.py:163
  63.6 1271.8 %all-gather.14.cloned.1.call-start = ((), (), s32[]{:S(2)}) async-start(), calls=%async_computation.9 | async-start | bytes 4718592 | tf_op jit(solution)/shard_map/all_gather | solution.py:22
  65.4 837.8 %copy-start.69 = (f32[1536]{0:T(1024)}, f32[1536]{0:T(1024)S(1)}, u32[]{:S(2)}) copy-start(f32[1536]{0:T(1024)S(1)} %get-tuple-element.215) | copy-start | bytes 18436
  65.4 48.6 %copy-start.87 = (f32[64]{0:T(128)}, f32[64]{0:T(128)S(1)}, u32[]{:S(2)}) copy-start(f32[64]{0:T(128)S(1)} %broadcast_multiply_fusion.17) | copy-start | bytes 772
  65.6 48.4 %copy-start.94 = (f32[64]{0:T(128)}, f32[64]{0:T(128)S(1)}, u32[]{:S(2)}) copy-start(f32[64]{0:T(128)S(1)} %add_rsqrt_fusion.3) | copy-start | bytes 772
  66.0 48.1 %copy-start.28 = (bf16[64,1536]{1,0:T(8,128)(2,1)}, bf16[64,1536]{1,0:T(8,128)(2,1)S(1)}, u32[]{:S(2)}) copy-start(bf16[64,1536]{1,0:T(8,128)(2,1)S(1)} %multiply_convert_fusion.4) | copy-start | bytes 589828
  722.5 180.7 %copy-start.46 = (f32[24576]{0:T(1024)}, f32[24576]{0:T(1024)S(1)}, u32[]{:S(2)}) copy-start(f32[24576]{0:T(1024)S(1)} %div.151) | copy-start | bytes 294916
  760.6 142.7 %copy-start.48 = (f32[24576]{0:T(1024)}, f32[24576]{0:T(1024)S(1)}, u32[]{:S(2)}) copy-start(f32[24576]{0:T(1024)S(1)} %rsqrt.36) | copy-start | bytes 294916
  903.3 72.5 %copy-start.39 = (bf16[1536,384]{1,0:T(8,128)(2,1)S(1)}, bf16[1536,384]{1,0:T(8,128)(2,1)}, u32[]{:S(2)}) copy-start(bf16[1536,384]{1,0:T(8,128)(2,1)} %get-tuple-element.273) | copy-start | bytes 3538948
  1209.2 51.6 %copy-start.29 = (bf16[64,1536]{1,0:T(8,128)(2,1)S(1)}, bf16[64,1536]{1,0:T(8,128)(2,1)}, u32[]{:S(2)}) copy-start(bf16[64,1536]{1,0:T(8,128)(2,1)} %copy-done.28) | copy-start | bytes 589828
  1260.7 139.6 %all-reduce.10.cloned.1.call-start = ((), (), s32[]{:S(2)}) async-start(), calls=%async_computation.3 | async-start | bytes 3145728 | tf_op jit(solution)/shard_map/psum | solution.py:219
  1262.7 89.2 %copy-start.71 = (bf16[64,4,96]{2,1,0:T(4,128)(2,1)}, bf16[64,4,96]{2,1,0:T(4,128)(2,1)S(1)}, u32[]{:S(2)}) copy-start(bf16[64,4,96]{2,1,0:T(4,128)(2,1)S(1)} %reshape.306) | copy-start | bytes 147460
  1262.8 62.3 %copy-start.50 = (bf16[64,4,96]{2,1,0:T(4,128)(2,1)}, bf16[64,4,96]{2,1,0:T(4,128)(2,1)S(1)}, u32[]{:S(2)}) copy-start(bf16[64,4,96]{2,1,0:T(4,128)(2,1)S(1)} %reshape.305) | copy-start | bytes 147460
  1263.0 88.9 %copy-start.54 = (f32[4,64,64]{1,2,0:T(8,128)}, f32[4,64,64]{1,2,0:T(8,128)S(1)}, u32[]{:S(2)}) copy-start(f32[4,64,64]{1,2,0:T(8,128)S(1)} %get-tuple-element.287) | copy-start | bytes 196612
  1358.9 182.2 %all-gather.12.cloned.1.call-start = ((), (), s32[]{:S(2)}) async-start(), calls=%async_computation.4 | async-start | bytes 10616832 | tf_op jit(solution)/shard_map/all_gather | solution.py:157
  1361.8 231.2 %all-reduce.12.cloned.1.call-start = ((), (), s32[]{:S(2)}) async-start(), calls=%async_computation.5 | async-start | bytes 3145728 | tf_op jit(solution)/shard_map/psum | solution.py:226
  1551.9 513.8 %all-reduce.20.cloned.1.call-start = ((), (), s32[]{:S(2)}) async-start(), calls=%async_computation.11 | async-start | bytes 1572864 | tf_op jit(solution)/shard_map/psum | solution.py:262
  1990.6 123.2 %all-reduce.14.cloned.1.call-start = ((), (), s32[]{:S(2)}) async-start(), calls=%async_computation.6 | async-start | bytes 3145728 | tf_op jit(solution)/shard_map/psum | solution.py:266
  2068.1 45.7 %copy-start.2 = (bf16[512,1536]{1,0:T(8,128)(2,1)S(1)}, bf16[512,1536]{1,0:T(8,128)(2,1)}, u32[]{:S(2)}) copy-start(bf16[512,1536]{1,0:T(8,128)(2,1)} %all-reduce.10.cloned.1.call-done) | copy-start | bytes 4718596
  2068.1 45.7 %copy-start.5 = (f32[64,1536]{1,0:T(8,128)S(1)}, f32[64,1536]{1,0:T(8,128)}, u32[]{:S(2)}) copy-start(f32[64,1536]{1,0:T(8,128)} %param.37) | copy-start | bytes 1179652
  2068.1 45.6 %copy-start.67 = (f32[1536]{0:T(1024)S(1)}, f32[1536]{0:T(1024)}, u32[]{:S(2)}) copy-start(f32[1536]{0:T(1024)} %get-tuple-element.216) | copy-start | bytes 18436
  2068.2 45.6 %copy-start.74 = (f32[512]{0:T(512)S(1)}, f32[512]{0:T(512)}, u32[]{:S(2)}) copy-start(f32[512]{0:T(512)} %copy-done.73) | copy-start | bytes 6148
  2071.8 104.4 %all-reduce.16.cloned.1.call-start = ((), (), s32[]{:S(2)}) async-start(), calls=%async_computation.7 | async-start | bytes 3145728 | tf_op jit(solution)/shard_map/psum | solution.py:273
  2133.1 865.8 %all-reduce.18.cloned.1.call-start = ((), (), s32[]{:S(2)}) async-start(), calls=%async_computation.10 | async-start | bytes 2850816 | tf_op jit(solution)/shard_map/psum | solution.py:346
  2277.6 50.8 %copy-start.32 = (bf16[64,4,96]{2,1,0:T(4,128)(2,1)S(1)}, bf16[64,4,96]{2,1,0:T(4,128)(2,1)}, u32[]{:S(2)}) copy-start(bf16[64,4,96]{2,1,0:T(4,128)(2,1)} %reshape.303) | copy-start | bytes 147460
  2794.9 47.4 %copy-start.41 = (bf16[1536,384]{1,0:T(8,128)(2,1)S(1)}, bf16[1536,384]{1,0:T(8,128)(2,1)}, u32[]{:S(2)}) copy-start(bf16[1536,384]{1,0:T(8,128)(2,1)} %get-tuple-element.273) | copy-start | bytes 3538948
  2850.5 65.4 %copy-start.30 = (bf16[64,1536]{1,0:T(8,128)(2,1)S(1)}, bf16[64,1536]{1,0:T(8,128)(2,1)}, u32[]{:S(2)}) copy-start(bf16[64,1536]{1,0:T(8,128)(2,1)} %copy-done.28) | copy-start | bytes 589828
  2850.5 202.1 %reduce-scatter.2.cloned.1.call-start = ((), (), s32[]{:S(2)}) async-start(), calls=%async_computation.8 | async-start | bytes 2654208 | tf_op jit(solution)/shard_map/reduce_scatter | solution.py:356
  3001.1 101.4 %copy-start.42 = (f32[1,4,48,3,128]{4,2,1,3,0:T(8,128)S(1)}, f32[1,4,48,3,128]{4,2,1,3,0:T(8,128)}, u32[]{:S(2)}) copy-start(f32[1,4,48,3,128]{4,2,1,3,0:T(8,128)} %copy.212) | copy-start | bytes 884740
  3054.8 50.6 %copy-start.25 = (f32[5,3,128,128]{3,2,1,0:T(8,128)S(1)}, f32[5,3,128,128]{3,2,1,0:T(8,128)}, u32[]{:S(2)}) copy-start(f32[5,3,128,128]{3,2,1,0:T(8,128)} %param.35) | copy-start | bytes 2949124
  (92 other events, 1221.0 us)
Sparse Core Ops, SparseCore 0:
  10.8 96.9 all-gather.9
  109.3 582.1 all-gather.7
  1260.9 74.5 all-gather.13
  1359.0 41.2 all-reduce.9
  1403.0 138.1 all-gather.11
  1552.0 41.0 all-reduce.11
  1990.7 74.8 all-reduce.19
  2071.9 41.8 all-reduce.13
  2133.3 42.8 all-reduce.15
  2850.6 129.1 all-reduce.17
  2984.3 68.2 reduce-scatter.1
where the time goes:
time: 3210 us; the launch traced here: 3190 us
  waiting for transfers between devices  1040 us (32%)
  matrix products  833 us (26%)
  local copies, waits for them, and re-layouts  566 us (18%)
  other arithmetic  549 us (17%)
  blocking collectives  177 us (6%)
    all_gather x1, waiting for transfers between devices, per_device(): lax.all_gather(local_rows.astype(jnp.bfloat16), 'head', axis=3, tiled=True)  577 us
    dot_general x8, matrix products, right_tmul(): lax.dot_general(a, b, (((1,), (1,)), ((), ())), preferred_element_type=jn...  150 us
    mul x2, other arithmetic, norm_reverse(): reciprocal_deviation * (scaled_values - running_mean_first - centered_inp...  144 us
    convert_element_type x1, local copies, waits for them, and re-layouts, per_device(): collected_rows.reshape(-1, feature_width).astype(jnp.float32)  143 us
    unnamed x235, local copies, waits for them, and re-layouts  138 us
    all_gather x1, waiting for transfers between devices, per_device(): lax.all_gather(ffn_weight.astype(jnp.bfloat16), 'frame', axis=1, tiled=True)  134 us
    dot_general x8, matrix products, matmul(): return jnp.dot(a, b, preferred_element_type=jnp.float32)  90.5 us
    dot_general x8, matrix products, left_tmul(): lax.dot_general(a, b, (((0,), (0,)), ((), ())), preferred_element_type=jn...  80.1 us
  transfers between devices with their start and end apart: 11, of which 10 were waited for; matrix products, arithmetic and copies ran while one was open for 6% of the time, Pallas kernels for 0%

commit v1 on v0

v1 whole, which is shorter than its diff:
```python
import functools

import jax
import jax.numpy as jnp
from jax import lax
from jax.experimental import pallas as pl
from jax.experimental.pallas import tpu as pltpu
from jax.sharding import PartitionSpec as P

HEAD_SIZE = 96
LATENTS = 64
PATCH = 256
FRAMES = 96
STEP = 5
GROUP = 4
EXTRA = 128
TAIL = 16
VMEM_BYTES = 58 * 1024 * 1024

HIGH_ACCURACY = lax.Precision.HIGHEST
clip_max = 0.05
beta_one = 0.5
beta_two = 0.6
adam_eps = 1e-08
f32 = jnp.float32
bf16 = jnp.bfloat16


def nn(a, b):
    return lax.dot_general(a, b, (((1,), (0,)), ((), ())), preferred_element_type=f32)


def nt(a, b):
    return lax.dot_general(a, b, (((1,), (1,)), ((), ())), preferred_element_type=f32)


def tn(a, b):
    return lax.dot_general(a, b, (((0,), (0,)), ((), ())), preferred_element_type=f32)


def normalize_rows(v):
    cent = v - jnp.mean(v, -1, keepdims=True)
    rstd = lax.rsqrt(jnp.mean(cent * cent, -1, keepdims=True) + 1e-05)
    return (cent * rstd, rstd)


def norm_reverse(dy, xhat, rstd, gain):
    scaled = dy * gain
    first = jnp.mean(scaled, -1, keepdims=True)
    second = jnp.mean(scaled * xhat, -1, keepdims=True)
    return rstd * (scaled - first - xhat * second)


def rotate(grad, left, right, inverse):
    slabs, rows, cols = grad.shape
    bl = left.shape[-1]
    br = right.shape[-1]
    blocks = grad.reshape(slabs, rows // bl, bl, cols // br, br)
    if inverse:
        out = jnp.einsum("maij,majcl,mckl->maick", left, blocks, right, precision=HIGH_ACCURACY)
    else:
        out = jnp.einsum("maij,maick,mckl->majcl", left, blocks, right, precision=HIGH_ACCURACY)
    return out.reshape(slabs, rows, cols)


def adam_moments(grad, one, two):
    one = beta_one * one + (1.0 - beta_one) * grad
    two = beta_two * two + (1.0 - beta_two) * grad * grad
    step = one / (1.0 - beta_one**STEP) / (jnp.sqrt(two / (1.0 - beta_two**STEP)) + adam_eps)
    return (one, two, step)


def soap_update(weight, grad, one, two, left, right, rates):
    one, two, step = adam_moments(rotate(grad, left, right, False), one, two)
    updated = weight - rates[:, None, None] * (rotate(step, left, right, True) + 0.01 * weight)
    return (updated, one, two, updated.astype(bf16))


def adamw_update(weight, grad, one, two, decay):
    one, two, step = adam_moments(grad, one, two)
    return (weight - 0.3 * (step + decay * weight), one, two)


def swap(x, axis, bit):
    size = lax.axis_size(axis)
    return lax.ppermute(x, axis, [(i, i ^ bit) for i in range(size)])


def sum_over(x, axis):
    bit = 1
    while bit < lax.axis_size(axis):
        x = x + swap(x, axis, bit)
        bit *= 2
    return x


def sum_head(x):
    x = x + swap(x, "head", 1)
    x = lax.reduce_precision(x, 8, 7)
    return x + swap(x.astype(bf16), "head", 2).astype(f32)


def split_three(x):
    high = lax.reduce_precision(x, 8, 7)
    rest = x - high
    mid = lax.reduce_precision(rest, 8, 7)
    return jnp.concatenate([high, mid, rest - mid], -1).astype(bf16)


def join_three(x):
    n = x.shape[-1] // 3
    x = x.astype(f32)
    return x[..., :n] + x[..., n : 2 * n] + x[..., 2 * n :]


def head_of_lane(rows, cols):
    return lax.broadcasted_iota(jnp.int32, (rows, cols), 1) // HEAD_SIZE


def spread(x):
    owner = head_of_lane(*x.shape)
    x = x.astype(f32)
    return jnp.concatenate([jnp.where(owner == j, x, 0.0) for j in range(GROUP)], 0).astype(bf16)


def collect(r):
    rows = r.shape[0] // GROUP
    owner = head_of_lane(rows, r.shape[1])
    out = jnp.where(owner == 0, r[:rows], 0.0)
    for j in range(1, GROUP):
        out = out + jnp.where(owner == j, r[j * rows : (j + 1) * rows], 0.0)
    return out


def whole(shape):
    return pl.BlockSpec(shape, lambda *_: (0,) * len(shape), pipeline_mode=pl.Buffered(1))


def kernel_absorb(scale, x_ref, w_ref, out_ref):
    out_ref[...] = (nt(spread(x_ref[...]), w_ref[...]) * scale).astype(bf16)


def absorb(x, w, scale):
    depth, width = w.shape
    cols = GROUP * HEAD_SIZE
    groups = width // cols
    rows = GROUP * LATENTS
    return pl.pallas_call(
        functools.partial(kernel_absorb, scale),
        grid=(groups,),
        in_specs=[
            pl.BlockSpec((LATENTS, cols), lambda g: (0, g)),
            pl.BlockSpec((depth, cols), lambda g: (0, g)),
        ],
        out_specs=pl.BlockSpec((rows, depth), lambda g: (g, 0)),
        out_shape=jax.ShapeDtypeStruct((groups * rows, depth), bf16),
        compiler_params=pltpu.CompilerParams(vmem_limit_bytes=VMEM_BYTES),
        name="absorb",
    )(x, w)


def kernel_read(
    nf, place, own, ra, rb, rc, time_ref, g0, qw, wv, xn_in, e_in, px_in, st_in, o_in,
    xn_o, e_o, px_o, st_o, o_o, xs, acc, run,
):
    del xn_in, e_in, px_in, st_in, o_in
    i = pl.program_id(0)
    tokens, depth = xs.shape
    cols = own.shape[1]
    heads_rows = GROUP * LATENTS
    groups = qw.shape[0] // heads_rows

    @pl.when(i == 0)
    def _():
        acc[...] = jnp.zeros_like(acc)
        run[0] = jnp.full(run.shape[1:], -1e30, f32)
        run[1] = jnp.zeros(run.shape[1:], f32)
        st_o[...] = jnp.zeros_like(st_o)

    for k, part in enumerate((own, ra, rb, rc)):
        off = pl.multiple_of((place[0] ^ k) * cols, 128)
        for f in range(nf):
            rows = slice(f * PATCH, (f + 1) * PATCH)
            moved = part[rows, :].astype(f32) + time_ref[pl.ds(i * nf + f, 1), pl.ds(off, cols)]
            xs[rows, pl.ds(off, cols)] = moved.astype(bf16)
    x = xs[...].astype(f32)
    cent = x - jnp.sum(x, -1, keepdims=True) * (1.0 / depth)
    rstd = lax.rsqrt(jnp.sum(cent * cent, -1, keepdims=True) * (1.0 / depth) + 1e-05)
    xn_o[:, :depth] = (cent * rstd * g0[...]).astype(bf16)
    lane = lax.broadcasted_iota(jnp.int32, (tokens, EXTRA), 1)
    frame = lax.broadcasted_iota(jnp.int32, (tokens, EXTRA), 0) // PATCH + i * nf
    xn_o[:, depth:] = jnp.where(lane == frame, rstd, 0.0).astype(bf16)
    key = lax.broadcasted_iota(jnp.int32, (1, tokens), 1)
    limit = place[1 + i * nf]
    for f in range(1, nf):
        limit = jnp.where(key >= f * PATCH, f * PATCH + place[1 + i * nf + f], limit)
    valid = key < limit
    block = lax.broadcasted_iota(jnp.int32, (heads_rows, 128), 1)
    last = i == pl.num_programs(0) - 1
    for g in range(groups):
        rows = slice(g * heads_rows, (g + 1) * heads_rows)
        scores = jnp.where(valid, nt(qw[rows, :], xn_o[:, :depth]), -1e30)
        old = run[0, rows, :]
        new = jnp.maximum(old, jnp.max(scores, -1, keepdims=True))
        expo = jnp.exp(scores - new[:, :1])
        shrink = jnp.exp(old - new)
        total = run[1, rows, :] * shrink + jnp.sum(expo, -1, keepdims=True)
        run[0, rows, :] = new
        run[1, rows, :] = total
        low = expo.astype(bf16)
        e_o[rows, :] = low
        stats = jnp.where(block == i, new, st_o[rows, :])
        stats = jnp.where(last & (block == 126), new, stats)
        st_o[rows, :] = jnp.where(last & (block == 127), total, stats)
        acc[rows, :] = acc[rows, :] * shrink[:, :1] + nn(low, xn_o[...])

    @pl.when(last)
    def _():
        for g in range(groups):
            rows = slice(g * heads_rows, (g + 1) * heads_rows)
            wide = slice(g * cols, (g + 1) * cols)
            held = acc[rows, :].astype(bf16)
            px_o[rows, :] = held
            mixed = nn(held[:, :depth], wv[:, wide]) / run[1, rows, :1]
            o_o[:, wide] = collect(mixed)


def read_pass(j, prev, feat, got, time_full, gain, lens, qw, wv, h, videos_dev):
    count, tokens_video, cols = feat.shape
    depth = wv.shape[0]
    frames_dev = tokens_video // PATCH
    nf = 2 if frames_dev % 2 == 0 else 1
    tokens = nf * PATCH
    blocks = frames_dev // nf
    rows = qw.shape[0]
    place = jnp.concatenate([h[None], lens]).astype(jnp.int32)
    feat2 = feat.reshape(count * tokens_video, cols)
    shapes = (
        jax.ShapeDtypeStruct((videos_dev * tokens_video, depth + EXTRA), bf16),
        jax.ShapeDtypeStruct((videos_dev * rows, tokens_video), bf16),
        jax.ShapeDtypeStruct((videos_dev * rows, depth + EXTRA), bf16),
        jax.ShapeDtypeStruct((videos_dev * rows, 128), f32),
        jax.ShapeDtypeStruct((videos_dev * LATENTS, depth), f32),
    )
    aliases = {}
    if prev is None:
        prev = [jnp.zeros((8, 128), s.dtype) for s in shapes]
    else:
        aliases = {9 + n: n for n in range(5)}
    anyspec = pl.BlockSpec(memory_space=pl.ANY)
    return pl.pallas_call(
        functools.partial(kernel_read, nf),
        grid_spec=pltpu.PrefetchScalarGridSpec(
            num_scalar_prefetch=1,
            grid=(blocks,),
            in_specs=[
                pl.BlockSpec((tokens, cols), lambda i, p: ((p[0] * videos_dev + j) * blocks + i, 0)),
                pl.BlockSpec((tokens, cols), lambda i, p: (i, 0)),
                pl.BlockSpec((tokens, cols), lambda i, p: (i, 0)),
                pl.BlockSpec((tokens, cols), lambda i, p: (i, 0)),
                whole(time_full.shape),
                whole(gain.shape),
                whole(qw.shape),
                whole(wv.shape),
                anyspec, anyspec, anyspec, anyspec, anyspec,
            ],
            out_specs=[
                pl.BlockSpec((tokens, depth + EXTRA), lambda i, p: (j * blocks + i, 0)),
                pl.BlockSpec((rows, tokens), lambda i, p: (j, i)),
                pl.BlockSpec((rows, depth + EXTRA), lambda i, p: (j, 0), pipeline_mode=pl.Buffered(1)),
                pl.BlockSpec((rows, 128), lambda i, p: (j, 0), pipeline_mode=pl.Buffered(1)),
                pl.BlockSpec((LATENTS, depth), lambda i, p: (j, 0), pipeline_mode=pl.Buffered(1)),
            ],
            scratch_shapes=[
                pltpu.VMEM((tokens, depth), bf16),
                pltpu.VMEM((rows, depth + EXTRA), f32),
                pltpu.VMEM((2, rows, 128), f32),
            ],
        ),
        out_shape=shapes,
        input_output_aliases=aliases,
        compiler_params=pltpu.CompilerParams(vmem_limit_bytes=VMEM_BYTES),
        cost_estimate=pl.CostEstimate(
            flops=4 * rows * tokens_video * depth,
            bytes_accessed=tokens_video * depth * 8,
            transcendentals=rows * tokens_video,
        ),
        name="read_pass",
    )(place, feat2, *got, time_full, gain, qw, wv, *prev)


def kernel_decode(
    nf, scale, place, xn, own, ra, rb, rc, msk, dq, dv, wk,
    ddq_o, ddv_o, dx_o, side_o, loss_o, dqw, dvd, sc, zs, acc, dacc, loss,
):
    i = pl.program_id(0)
    tokens = xn.shape[0]
    depth = wk.shape[0]
    cols = own.shape[1]
    heads_rows = GROUP * LATENTS
    groups = dqw.shape[0] // heads_rows
    total_rows = dqw.shape[0]

    @pl.when(i == 0)
    def _():
        acc[...] = jnp.zeros_like(acc)
        dacc[...] = jnp.zeros_like(dacc)
        loss[...] = jnp.zeros_like(loss)
        for g in range(groups):
            rows = slice(g * heads_rows, (g + 1) * heads_rows)
            wide = slice(g * cols, (g + 1) * cols)
            dqw[rows, :] = (nt(spread(dq[:, wide]), wk[:, wide]) * scale).astype(bf16)
            dvd[g] = spread(dv[:, wide])

    sc[...] = nt(dqw[...], xn[:, :depth]).reshape(groups, heads_rows, tokens)
    counts = msk[...]
    second = jnp.zeros((1, tokens), f32)
    for k, part in enumerate((own, ra, rb, rc)):
        g = place[0] ^ k
        s = sc[g].reshape(GROUP, LATENTS, tokens)
        a = jnp.exp(s - jnp.max(s, 1, keepdims=True))
        a = a / jnp.sum(a, 1, keepdims=True)
        low = a.reshape(heads_rows, tokens).astype(bf16)
        error = tn(low, dvd[g]) - part[...].astype(f32)
        kept = counts * error
        loss[...] += jnp.sum((kept * error).reshape(tokens // 8, 8, cols), 0)
        dp = (2.0 * kept).astype(bf16)
        dacc[g] += nn(low, dp)
        da = nt(dvd[g], dp).reshape(GROUP, LATENTS, tokens)
        z = a * (da - jnp.sum(a * da, 1, keepdims=True))
        second = second + jnp.sum((z * s).reshape(heads_rows, tokens), 0, keepdims=True)
        zs[pl.ds(pl.multiple_of(g * heads_rows, heads_rows), heads_rows), :] = z.reshape(
            heads_rows, tokens
        ).astype(bf16)
    zs[pl.ds(total_rows, TAIL), :] = tail_rows(nf, i, second, xn, depth)
    acc[...] += nn(zs[...], xn[...])

    @pl.when(i == pl.num_programs(0) - 1)
    def _():
        gain = jnp.zeros((8, depth), f32)
        for g in range(groups):
            rows = slice(g * heads_rows, (g + 1) * heads_rows)
            wide = slice(g * cols, (g + 1) * cols)
            held = acc[rows, :depth]
            low = held.astype(bf16)
            dx_o[rows, :] = low
            ddq_o[:, wide] = collect(nn(low, wk[:, wide])) * scale
            ddv_o[:, wide] = collect(dacc[g])
            gain = gain + jnp.sum(
                (held * dqw[rows, :].astype(f32)).reshape(heads_rows // 8, 8, depth), 0
            )
        side_o[0:TAIL, :] = tn(acc[:total_rows, depth:].astype(bf16), dqw[...])[:TAIL]
        side_o[TAIL : 2 * TAIL, :] = acc[total_rows:, :depth]
        side_o[2 * TAIL :, :] = gain
        loss_o[...] = loss[...]


def tail_rows(nf, i, second, xn, depth):
    tokens = xn.shape[0]
    rstd = nt(jnp.ones((TAIL, EXTRA), bf16), xn[:, depth:])
    row = lax.broadcasted_iota(jnp.int32, (TAIL, tokens), 0)
    frame = lax.broadcasted_iota(jnp.int32, (TAIL, tokens), 1) // PATCH + i * nf
    return jnp.where(row == frame, rstd * second * (1.0 / depth), 0.0).astype(bf16)


def decode_pass(j, xn_all, feat, got, counts, dq_all, dv_all, wk, h, scale, videos_dev):
    count, tokens_video, cols = feat.shape
    depth = wk.shape[0]
    frames_dev = tokens_video // PATCH
    nf = 2 if frames_dev % 2 == 0 else 1
    tokens = nf * PATCH
    blocks = frames_dev // nf
    groups = depth // cols
    heads_rows = GROUP * LATENTS
    rows = groups * heads_rows
    feat2 = feat.reshape(count * tokens_video, cols)
    return pl.pallas_call(
        functools.partial(kernel_decode, nf, scale),
        grid_spec=pltpu.PrefetchScalarGridSpec(
            num_scalar_prefetch=1,
            grid=(blocks,),
            in_specs=[
                pl.BlockSpec((tokens, depth + EXTRA), lambda i, p: (j * blocks + i, 0)),
                pl.BlockSpec((tokens, cols), lambda i, p: ((p[0] * videos_dev + j) * blocks + i, 0)),
                pl.BlockSpec((tokens, cols), lambda i, p: (i, 0)),
                pl.BlockSpec((tokens, cols), lambda i, p: (i, 0)),
                pl.BlockSpec((tokens, cols), lambda i, p: (i, 0)),
                pl.BlockSpec((tokens, 1), lambda i, p: (j * blocks + i, 0)),
                pl.BlockSpec((LATENTS, depth), lambda i, p: (j, 0), pipeline_mode=pl.Buffered(1)),
                pl.BlockSpec((LATENTS, depth), lambda i, p: (j, 0), pipeline_mode=pl.Buffered(1)),
                whole(wk.shape),
            ],
            out_specs=[
                whole((LATENTS, depth)),
                whole((LATENTS, depth)),
                whole((rows, depth)),
                whole((2 * TAIL + 8, depth)),
                whole((8, cols)),
            ],
            scratch_shapes=[
                pltpu.VMEM((rows, depth), bf16),
                pltpu.VMEM((groups, heads_rows, cols), bf16),
                pltpu.VMEM((groups, heads_rows, tokens), f32),
                pltpu.VMEM((rows + TAIL, tokens), bf16),
                pltpu.VMEM((rows + TAIL, depth + EXTRA), f32),
                pltpu.VMEM((groups, heads_rows, cols), f32),
                pltpu.VMEM((8, cols), f32),
            ],
        ),
        out_shape=(
            jax.ShapeDtypeStruct((LATENTS, depth), f32),
            jax.ShapeDtypeStruct((LATENTS, depth), f32),
            jax.ShapeDtypeStruct((rows, depth), bf16),
            jax.ShapeDtypeStruct((2 * TAIL + 8, depth), f32),
            jax.ShapeDtypeStruct((8, cols), f32),
        ),
        compiler_params=pltpu.CompilerParams(vmem_limit_bytes=VMEM_BYTES),
        cost_estimate=pl.CostEstimate(
            flops=6 * rows * tokens_video * depth,
            bytes_accessed=tokens_video * depth * 4,
            transcendentals=rows * tokens_video,
        ),
        name="decode_pass",
    )(jnp.full((1,), h, jnp.int32), xn_all, feat2, *got, counts, dq_all, dv_all, wk)


def kernel_value(do, wv, px, st, ld, ow_o, dwv_o, side_o, acc):
    g = pl.program_id(0)
    v = pl.program_id(1)
    depth = wv.shape[0]

    @pl.when((g == 0) & (v == 0))
    def _():
        side_o[...] = jnp.zeros_like(side_o)

    diag = spread(do[...])
    ow = nt(diag, wv[...]).astype(bf16)
    ow_o[...] = ow
    norm = px[...].astype(f32) * jnp.exp(st[:, 126:127] - ld[:, 0:1])
    low = norm.astype(bf16)
    part = tn(diag, low[:, :depth])

    @pl.when(v == 0)
    def _():
        acc[...] = part

    @pl.when(v > 0)
    def _():
        acc[...] += part

    dwv_o[...] = acc[...].astype(bf16)
    side_o[0:TAIL, :] += tn(low[:, depth:], ow)[:TAIL]
    rows = ow.shape[0]
    side_o[TAIL:, :] += jnp.sum((ow.astype(f32) * norm[:, :depth]).reshape(rows // 8, 8, depth), 0)


def value_pass(do_all, wv, px_all, st_all, ld, videos_dev):
    depth = wv.shape[0]
    cols = GROUP * HEAD_SIZE
    groups = depth // cols
    rows = GROUP * LATENTS
    return pl.pallas_call(
        kernel_value,
        grid=(groups, videos_dev),
        in_specs=[
            pl.BlockSpec((LATENTS, cols), lambda g, v: (v, g)),
            pl.BlockSpec((depth, cols), lambda g, v: (0, g)),
            pl.BlockSpec((rows, depth + EXTRA), lambda g, v: (v * groups + g, 0)),
            pl.BlockSpec((rows, 128), lambda g, v: (v * groups + g, 0)),
            pl.BlockSpec((rows, 128), lambda g, v: (v * groups + g, 0)),
        ],
        out_specs=[
            pl.BlockSpec((rows, depth), lambda g, v: (v * groups + g, 0)),
            pl.BlockSpec((cols, depth), lambda g, v: (g, 0)),
            pl.BlockSpec((TAIL + 8, depth), lambda g, v: (0, 0)),
        ],
        out_shape=(
            jax.ShapeDtypeStruct((videos_dev * groups * rows, depth), bf16),
            jax.ShapeDtypeStruct((depth, depth), bf16),
            jax.ShapeDtypeStruct((TAIL + 8, depth), f32),
        ),
        scratch_shapes=[pltpu.VMEM((cols, depth), f32)],
        compiler_params=pltpu.CompilerParams(vmem_limit_bytes=VMEM_BYTES),
        name="value_pass",
    )(do_all, wv, px_all, st_all, ld)


def kernel_back(nf, scale, videos_dev, xn, e, st, ld, ow, qw, q, wk, *rest):
    dqs = rest[:videos_dev]
    dxs = rest[videos_dev : 2 * videos_dev]
    dq_o, dwk_o, side_o, zs, acc = rest[2 * videos_dev :]
    v = pl.program_id(0)
    i = pl.program_id(1)
    tokens = xn.shape[0]
    depth = wk.shape[0]
    heads_rows = GROUP * LATENTS
    total_rows = qw.shape[0]
    groups = total_rows // heads_rows
    cols = GROUP * HEAD_SIZE

    @pl.when((v == 0) & (i == 0))
    def _():
        acc[...] = jnp.zeros_like(acc)

    second = jnp.zeros((1, tokens), f32)
    block = lax.broadcasted_iota(jnp.int32, (heads_rows, 128), 1)
    for g in range(groups):
        rows = slice(g * heads_rows, (g + 1) * heads_rows)
        peak = jnp.sum(jnp.where(block == i, st[rows, :], 0.0), -1, keepdims=True)
        lse = ld[rows, 0:1]
        dp = nt(ow[rows, :], xn[:, :depth])
        expo = e[rows, :].astype(f32)
        prob = expo * jnp.exp(peak - lse)
        z = prob * (dp - ld[rows, 1:2])
        score = jnp.log(jnp.maximum(expo, 1e-37)) + peak
        second = second + jnp.sum(z * score + prob * dp, 0, keepdims=True)
        zs[rows, :] = z.astype(bf16)
    zs[total_rows:, :] = tail_rows(nf, i, second, xn, depth)
    acc[...] += nn(zs[...], xn[...])

    @pl.when((v == videos_dev - 1) & (i == pl.num_programs(1) - 1))
    def _():
        gain = jnp.zeros((8, depth), f32)
        for g in range(groups):
            rows = slice(g * heads_rows, (g + 1) * heads_rows)
            wide = slice(g * cols, (g + 1) * cols)
            held = acc[rows, :depth]
            low = held.astype(bf16)
            dq_o[:, wide] = collect(nn(low, wk[:, wide])) * scale
            grad = tn(spread(q[:, wide]), low)
            for one, dx in zip(dqs, dxs):
                grad = grad + tn(spread(one[:, wide]), dx[rows, :])
            dwk_o[wide, :] = (grad * scale).astype(bf16)
            gain = gain + jnp.sum(
                (held * qw[rows, :].astype(f32)).reshape(heads_rows // 8, 8, depth), 0
            )
        side_o[0:TAIL, :] = tn(acc[:total_rows, depth:].astype(bf16), qw[...])[:TAIL]
        side_o[TAIL : 2 * TAIL, :] = acc[total_rows:, :depth]
        side_o[2 * TAIL :, :] = gain


def back_pass(xn_all, e_all, st_all, ld, ow, qw, q_all, wk, dq_all, dxs, scale, videos_dev):
    depth = wk.shape[0]
    tokens_video = e_all.shape[1]
    frames_dev = tokens_video // PATCH
    nf = 2 if frames_dev % 2 == 0 else 1
    tokens = nf * PATCH
    blocks = frames_dev // nf
    rows = qw.shape[0]
    dqs = [dq_all[v * LATENTS : (v + 1) * LATENTS] for v in range(videos_dev)]
    return pl.pallas_call(
        functools.partial(kernel_back, nf, scale, videos_dev),
        grid=(videos_dev, blocks),
        in_specs=[
            pl.BlockSpec((tokens, depth + EXTRA), lambda v, i: (v * blocks + i, 0)),
            pl.BlockSpec((rows, tokens), lambda v, i: (v, i)),
            pl.BlockSpec((rows, 128), lambda v, i: (v, 0)),
            pl.BlockSpec((rows, 128), lambda v, i: (v, 0)),
            pl.BlockSpec((rows, depth), lambda v, i: (v, 0)),
            whole(qw.shape),
            whole(q_all.shape),
            whole(wk.shape),
        ]
        + [whole(a.shape) for a in dqs]
        + [whole(a.shape) for a in dxs],
        out_specs=[
            whole((LATENTS, depth)),
            whole((depth, depth)),
            whole((2 * TAIL + 8, depth)),
        ],
        out_shape=(
            jax.ShapeDtypeStruct((LATENTS, depth), f32),
            jax.ShapeDtypeStruct((depth, depth), bf16),
            jax.ShapeDtypeStruct((2 * TAIL + 8, depth), f32),
        ),
        scratch_shapes=[
            pltpu.VMEM((rows + TAIL, tokens), bf16),
            pltpu.VMEM((rows + TAIL, depth + EXTRA), f32),
        ],
        compiler_params=pltpu.CompilerParams(vmem_limit_bytes=VMEM_BYTES),
        cost_estimate=pl.CostEstimate(
            flops=4 * videos_dev * rows * tokens_video * depth,
            bytes_accessed=videos_dev * tokens_video * depth * 4,
            transcendentals=videos_dev * rows * tokens_video,
        ),
        name="back_pass",
    )(xn_all, e_all, st_all, ld, ow, qw, q_all, wk, *dqs, *dxs)


def scatter_head(x):
    me = lax.axis_index("head")
    core, side = (me & 1, me >> 1)
    x = x.reshape((2, 2) + x.shape[1:])
    away = lax.dynamic_index_in_dim(x, 1 - core, 1, False)
    near = lax.dynamic_index_in_dim(x, core, 1, False)
    x = near.astype(f32) + swap(away, "head", 1).astype(f32)
    away = lax.dynamic_index_in_dim(x, 1 - side, 0, False)
    near = lax.dynamic_index_in_dim(x, side, 0, False)
    return near, swap(away.astype(bf16), "head", 2)


def per_device(
    features, lengths, loss_mask, sq_weight, sq_first, sq_second, ffn_weight, ffn_first,
    ffn_second, left_bases, right_sq, right_ffn, latents, lat_first, lat_second, time_embed,
    time_first, time_second, gains, gain_first, gain_second,
):
    videos, frames_dev, patches, cols = features.shape
    lat_count, depth = latents.shape
    heads_dev = cols // HEAD_SIZE
    head_size = lax.axis_size("head")
    frame_size = lax.axis_size("frame")
    videos_dev = videos // head_size
    rows_dev = sq_weight.shape[1]
    scale = HEAD_SIZE ** (-0.5)
    f = lax.axis_index("frame")
    h = lax.axis_index("head")
    first_frame = (f == 0).astype(f32)
    first_head = (h == 0).astype(f32)
    share = videos_dev * lat_count // frame_size
    tokens_video = frames_dev * patches

    with jax.named_scope("exchange"):
        feat = features.reshape(videos, tokens_video, cols)
        got = [
            [
                swap(lax.dynamic_index_in_dim(feat, videos_dev * (h ^ k) + j, 0, False), "head", k)
                for k in range(1, head_size)
            ]
            for j in range(videos_dev)
        ]

    with jax.named_scope("weights"):
        sq_low = sq_weight.astype(bf16)
        kv_rows = lax.all_gather(sq_low[1:3], "head", axis=2, tiled=True)
        w_key = lax.all_gather(kv_rows[0], "frame", axis=0, tiled=True)
        w_value = lax.all_gather(kv_rows[1], "frame", axis=0, tiled=True)
        w_query, w_outt, w_dec = (
            lax.all_gather(sq_low[n], "frame", axis=0, tiled=True) for n in (0, 3, 4)
        )
        ffn_low = ffn_weight.astype(bf16)
        w_up, w_downt = (
            lax.all_gather(ffn_low[n], "frame", axis=0, tiled=True) for n in (0, 1)
        )
        time_full = lax.all_gather(time_embed, "head", axis=1, tiled=True)

    with jax.named_scope("latent_keys"):
        zhat_zero, zrstd_zero = normalize_rows(latents)
        normed_lat = (zhat_zero * gains[1]).astype(bf16)
        query = nn(normed_lat, w_query).astype(bf16)
        q_all = lax.all_gather(query, "head", axis=1, tiled=True)
        w_key_own = lax.dynamic_slice_in_dim(w_key, h * cols, cols, 1)
        w_value_own = lax.dynamic_slice_in_dim(w_value, h * cols, cols, 1)
        lat_key = nn(normed_lat, w_key_own).astype(bf16).reshape(lat_count, heads_dev, HEAD_SIZE)
        lat_value = nn(normed_lat, w_value_own).astype(bf16).reshape(lat_count, heads_dev, HEAD_SIZE)
        qw = absorb(q_all, w_key, scale)

    with jax.named_scope("read"):
        own_lens = lax.dynamic_slice_in_dim(lengths, h * videos_dev, videos_dev, 0)
        state = None
        for j in range(videos_dev):
            state = read_pass(
                j, state, feat, got[j], time_full, gains[0:1], own_lens[j], qw, w_value, h, videos_dev
            )
        xn_all, e_all, px_all, st_all, o_all = state

    with jax.named_scope("combine"):
        heads = depth // HEAD_SIZE
        lse_local = (
            (st_all[:, 126] + jnp.log(st_all[:, 127]))
            .reshape(videos_dev, heads, lat_count)
            .transpose(0, 2, 1)
            .reshape(videos_dev * lat_count, heads)
        )
        pay = jnp.concatenate(
            [o_all.astype(bf16), split_three(lse_local)], 1
        ).reshape(frame_size, share, depth + 3 * heads)
        pay = lax.all_to_all(pay, "frame", 0, 0, tiled=True)
        lse_each = join_three(pay[..., depth:])
        o_each = pay[..., :depth].astype(f32).reshape(frame_size, share, heads, HEAD_SIZE)
        top = jnp.max(lse_each, 0)
        weight = jnp.exp(lse_each - top)
        total = jnp.sum(weight, 0)
        o_tok = jnp.sum(o_each * weight[..., None], 0) / total[..., None]
        lse_tok = top + jnp.log(total)
        o_heads = o_tok.reshape(share, head_size, cols).transpose(1, 0, 2).astype(bf16)
        l_heads = split_three(lse_tok.reshape(share, head_size, heads_dev).transpose(1, 0, 2))
        pay = lax.all_to_all(jnp.concatenate([o_heads, l_heads], 2), "head", 0, 0, tiled=True)
        lse_tok = join_three(pay[..., cols:])
        o_tok = pay[..., :cols].astype(f32).reshape(head_size, share, heads_dev, HEAD_SIZE)
        first_row = lax.rem(f * share, lat_count)
        q_rows = lax.dynamic_slice_in_dim(query, first_row, share, 0).reshape(
            share, heads_dev, HEAD_SIZE
        )
        lat_scores = (
            jnp.einsum("rnd,jnd->rnj", q_rows, lat_key, preferred_element_type=f32) * scale
        )
        lse = jnp.logaddexp(lse_tok, jax.nn.logsumexp(lat_scores, -1)[None])
        lat_prob = jnp.exp(lat_scores[None] - lse[..., None])
        attn = o_tok * jnp.exp(lse_tok - lse)[..., None] + jnp.einsum(
            "srnj,jnd->srnd", lat_prob, lat_value.astype(f32), precision=HIGH_ACCURACY
        )
        rows = head_size * share
        attn_low = attn.reshape(rows, cols).astype(bf16)

    with jax.named_scope("latent_forward"):
        lat_rows = jnp.tile(lax.dynamic_slice_in_dim(latents, first_row, share, 0), (head_size, 1))
        z_one = lat_rows + sum_head(nt(attn_low, w_outt))
        z1hat, z1rstd = normalize_rows(z_one)
        ffn_in = (z1hat * gains[2]).astype(bf16)
        pre = nn(ffn_in, w_up)
        hidden = jax.nn.gelu(pre).astype(bf16)
        z_two = z_one + sum_head(nt(hidden, w_downt))
        z2hat, z2rstd = normalize_rows(z_two)
        final = (z2hat * gains[3]).astype(bf16)
        dec = jnp.concatenate([nn(final, w_query), nn(final, w_dec)], 1).astype(bf16)

    def to_tokens(x):
        x = lax.all_to_all(x.reshape(head_size, share, -1), "head", 0, 0, tiled=True)
        x = x.transpose(1, 0, 2)
        x = jnp.broadcast_to(x[None], (frame_size,) + x.shape)
        x = lax.all_to_all(x, "frame", 0, 0, tiled=True)
        return x.reshape(videos_dev * lat_count, head_size, -1)

    with jax.named_scope("decode"):
        dec_all = to_tokens(dec)
        dq_all = dec_all[..., :cols].reshape(videos_dev * lat_count, depth)
        dv_all = dec_all[..., cols:].reshape(videos_dev * lat_count, depth)
        own_mask = lax.dynamic_slice_in_dim(loss_mask, h * videos_dev, videos_dev, 0).astype(f32)
        counts = own_mask.reshape(videos_dev * tokens_video, 1)
        decoded = [
            decode_pass(
                j, xn_all, feat, got[j], counts, dq_all, dv_all, w_key, h, scale, videos_dev
            )
            for j in range(videos_dev)
        ]
        loss_part = sum(jnp.sum(d[4]) for d in decoded)
        count_part = jnp.sum(own_mask)
        dec_side = sum(d[3] for d in decoded)

    with jax.named_scope("latent_backward"):
        ddec = jnp.concatenate(
            [
                jnp.concatenate([d[n] for d in decoded], 0).reshape(frame_size, share, head_size, cols)
                for n in (0, 1)
            ],
            3,
        ).astype(bf16)
        ddec = lax.all_to_all(
            ddec.reshape(frame_size, share, -1), "frame", 0, 0, tiled=True
        ).astype(f32)
        ddec = jnp.sum(ddec, 0).astype(bf16).reshape(share, head_size, 2 * cols).transpose(1, 0, 2)
        ddec = lax.all_to_all(ddec, "head", 0, 0, tiled=True).reshape(rows, 2 * cols)
        ddq_low, ddv_low = (ddec[:, :cols], ddec[:, cols:])
        dfinal = sum_head(nt(ddq_low, w_query) + nt(ddv_low, w_dec))
        dz_two = norm_reverse(dfinal, z2hat, z2rstd, gains[3])
        dz2_low = dz_two.astype(bf16)
        _, gelu_back = jax.vjp(jax.nn.gelu, pre)
        dpre = gelu_back(nn(dz2_low, w_downt))[0].astype(bf16)
        dffn_in = sum_head(nt(dpre, w_up))
        dz_one = dz_two + norm_reverse(dffn_in, z1hat, z1rstd, gains[2])
        dz1_low = dz_one.astype(bf16)
        dattn = nn(dz1_low, w_outt).astype(bf16)
        dattn_heads = dattn.astype(f32).reshape(head_size, share, heads_dev, HEAD_SIZE)
        delta = jnp.sum(dattn_heads * attn, -1)
        pay = jnp.concatenate(
            [
                dattn,
                split_three(lse.reshape(rows, heads_dev)),
                split_three(delta.reshape(rows, heads_dev)),
            ],
            1,
        )
        pay = to_tokens(pay)
        do_all = pay[..., :cols].reshape(videos_dev * lat_count, depth)

        def by_head(x):
            x = join_three(x).reshape(videos_dev, lat_count, heads)
            return x.transpose(0, 2, 1).reshape(videos_dev * heads * lat_count, 1)

        ld = jnp.concatenate(
            [
                by_head(pay[..., cols : cols + 3 * heads_dev]),
                by_head(pay[..., cols + 3 * heads_dev :]),
            ],
            1,
        )
        ld = jnp.pad(ld, ((0, 0), (0, 126)))

    with jax.named_scope("latent_pairs"):
        lat_value_f = lat_value.astype(f32)
        lat_dprob = jnp.einsum("srnd,jnd->srnj", dattn_heads, lat_value_f, precision=HIGH_ACCURACY)
        lat_dscore = lat_prob * (lat_dprob - delta[..., None]) * scale
        dq_lat = jnp.einsum(
            "srnj,jnd->rnd", lat_dscore, lat_key.astype(f32), precision=HIGH_ACCURACY
        ).reshape(share, cols)
        dk_lat = jnp.einsum(
            "srnj,rnd->jnd", lat_dscore, q_rows.astype(f32), precision=HIGH_ACCURACY
        ).reshape(lat_count, cols)
        dv_lat = jnp.einsum(
            "srnj,srnd->jnd", lat_prob, dattn_heads, precision=HIGH_ACCURACY
        ).reshape(lat_count, cols)
        dk_lat_low = dk_lat.astype(bf16)
        dv_lat_low = dv_lat.astype(bf16)
        dzn_pairs = nt(dk_lat_low, w_key_own) + nt(dv_lat_low, w_value_own)

    with jax.named_scope("value"):
        ow, dwv_t, value_side = value_pass(do_all, w_value, px_all, st_all, ld, videos_dev)

    with jax.named_scope("back"):
        dq_part, dwk_t, back_side = back_pass(
            xn_all, e_all, st_all, ld, ow, qw, q_all, w_key, dq_all,
            [d[2] for d in decoded], scale, videos_dev,
        )

    with jax.named_scope("row_gradients"):
        all_rows = frame_size * rows
        wide = lax.all_gather(
            jnp.concatenate([hidden, dpre, attn_low, ddq_low, ddv_low], 1), "frame", axis=0, tiled=True
        )
        hid = hidden.shape[1]
        narrow = jnp.concatenate(
            [a.reshape(rows, frame_size, rows_dev) for a in (ffn_in, dz2_low, dz1_low, final)], 2
        ).transpose(1, 0, 2)
        narrow = lax.all_to_all(narrow, "frame", 0, 0, tiled=True).reshape(all_rows, 4 * rows_dev)
        ffn_in_own, dz2_own, dz1_own, final_own = (
            narrow[:, n * rows_dev : (n + 1) * rows_dev] for n in range(4)
        )
        grad_up = tn(ffn_in_own, wide[:, hid : 2 * hid])
        grad_downt = tn(dz2_own, wide[:, :hid])
        grad_outt = tn(dz1_own, wide[:, 2 * hid : 2 * hid + cols])
        grad_query = tn(final_own, wide[:, 2 * hid + cols : 2 * hid + 2 * cols])
        grad_dec = tn(final_own, wide[:, 2 * hid + 2 * cols :])

    with jax.named_scope("patch_gradients"):
        side = dec_side + back_side
        pulled = side[:TAIL] + value_side[:TAIL]
        pulled = pulled * gains[0]
        time_part = (
            pulled
            - jnp.mean(pulled, -1, keepdims=True)
            - side[TAIL : 2 * TAIL] / gains[0]
        )
        gain0 = jnp.sum(side[2 * TAIL :] + value_side[TAIL:], 0, keepdims=True) / gains[0]
        pack = jnp.concatenate(
            [dq_part, time_part, gain0, jnp.zeros((7, depth), f32)], 0
        )
        pack = pack.reshape(-1, head_size, cols).transpose(1, 0, 2)
        near, far = scatter_head(pack)
        pack = near + far.astype(f32)
        time_own = pack[lat_count : lat_count + frames_dev]
        dq_pad = lax.dynamic_update_slice_in_dim(
            jnp.zeros((lat_count, cols), f32), dq_lat, first_row, 0
        )
        pack = jnp.concatenate([pack[:lat_count] + dq_pad, pack[lat_count + TAIL :]], 0)
        pack = sum_over(pack, "frame")
        dquery = pack[:lat_count].astype(bf16)
        gain0_own = pack[lat_count]
        dzn_query = sum_head(nt(dquery, w_query))
        lat_direct = lax.dynamic_update_slice_in_dim(
            jnp.zeros((lat_count, depth), f32),
            jnp.sum(dz_one.reshape(head_size, share, depth), 0),
            first_row,
            0,
        )
        row_part = jnp.concatenate(
            [lat_direct, jnp.sum(dffn_in * z1hat, 0)[None], jnp.sum(dfinal * z2hat, 0)[None]], 0
        )
        row_sum, dzn_pairs = lax.psum((row_part * first_head, dzn_pairs), ("frame", "head"))
        dzn = dzn_query + dzn_pairs
        grad_gain1 = jnp.sum(dzn * zhat_zero, 0)
        lat_grad = row_sum[:lat_count] + norm_reverse(dzn, zhat_zero, zrstd_zero, gains[1])
        gain_rest = jnp.stack([grad_gain1, row_sum[lat_count], row_sum[lat_count + 1]])
        gain_grad = jnp.concatenate(
            [gain0_own[None], lax.dynamic_slice_in_dim(gain_rest, h * cols, cols, 1)], 0
        )
        normed_own = lax.dynamic_slice_in_dim(normed_lat, f * rows_dev, rows_dev, 1)
        grad_query = grad_query + tn(normed_own, dquery)

    with jax.named_scope("key_value_gradients"):
        grads = []
        for grad, lat_low in ((dwk_t, dk_lat_low), (dwv_t, dv_lat_low)):
            near, far = scatter_head(grad.reshape(head_size, cols, depth))
            grad = near + far.astype(f32) + tn(lat_low, normed_lat)
            grads.append(grad.astype(bf16))
        both = jnp.concatenate(grads, 0).T
        both = lax.psum_scatter(both, "frame", scatter_dimension=0, tiled=True).astype(f32)
        grad_key, grad_value = (both[:, :cols], both[:, cols:])

    with jax.named_scope("update"):
        sq_grad = jnp.stack([grad_query, grad_key, grad_value, grad_outt, grad_dec])
        ffn_grad = jnp.stack([grad_up, grad_downt])
        squares = (
            jnp.sum(sq_grad * sq_grad) + jnp.sum(ffn_grad * ffn_grad) + jnp.sum(time_own * time_own)
        )
        squares = (
            squares
            + first_frame * first_head * jnp.sum(lat_grad * lat_grad)
            + first_frame * jnp.sum(gain_grad * gain_grad)
        )
        sums = jnp.pad(jnp.stack([loss_part, count_part, squares])[None], ((0, 7), (0, 125)))
        sums = sum_over(sum_over(sums, "head"), "frame")
        loss_sum, masked_count, squares = (sums[0, 0], sums[0, 1], sums[0, 2])
        grad_norm = jnp.sqrt(squares) / masked_count
        factor = jnp.minimum(1.0, clip_max / grad_norm) / masked_count
        out_rate = ((FRAMES * PATCH + LATENTS) / 64.0) ** 0.5
        sq_rates = jnp.array([1.0, 1.0, 1.0, out_rate, 1.0], f32) * 0.02
        ffn_rates = jnp.array([0.02, 0.02], f32)
        sq_out = soap_update(
            sq_weight, sq_grad * factor, sq_first, sq_second, left_bases[:5], right_sq, sq_rates
        )
        ffn_out = soap_update(
            ffn_weight, ffn_grad * factor, ffn_first, ffn_second, left_bases[5:], right_ffn, ffn_rates
        )
        lat_out = adamw_update(latents, lat_grad * factor, lat_first, lat_second, 0.01)
        time_out = adamw_update(time_embed, time_own * factor, time_first, time_second, 0.01)
        gain_own = lax.dynamic_slice_in_dim(gains, h * cols, cols, 1)
        gain_out = adamw_update(gain_own, gain_grad * factor, gain_first, gain_second, 0.0)
    return (loss_sum, masked_count, grad_norm, *sq_out, *ffn_out, *lat_out, *time_out, *gain_out)


def solution(mesh):
    matrix = P(None, "frame", "head")
    frame_rows = P("frame", "head")
    by_head = P(None, "head")
    placed = (
        P(None, "frame", None, "head"),
        P(None, "frame"),
        P(None, "frame", None),
        matrix, matrix, matrix, matrix, matrix, matrix,
        P(None, "frame", None, None),
        P(None, "head", None, None),
        P(None, "head", None, None),
        P(), P(), P(),
        frame_rows, frame_rows, frame_rows,
        P(), by_head, by_head,
    )
    outs = (
        P(), P(), P(),
        matrix, matrix, matrix, matrix, matrix, matrix, matrix, matrix,
        P(), P(), P(),
        frame_rows, frame_rows, frame_rows,
        by_head, by_head, by_head,
    )
    return jax.shard_map(per_device, mesh=mesh, in_specs=placed, out_specs=outs, check_vma=False)
```

time: 3210 us -> 1180 us (0.37)
  waiting for transfers between devices: 1040 us -> 218 us
  matrix products: 833 us -> 73.6 us
  other arithmetic: 549 us -> 97.9 us
  local copies, waits for them, and re-layouts: 566 us -> 175 us
  Pallas kernels: 0 us -> 293 us
  blocking collectives: 177 us -> 245 us
  starting transfers between devices: 0.46 us -> 43.3 us
    dot_general x51 -> x36, matrix products: 833 us -> 71.8 us  [the longest x8 16 us: tn(): lax.dot_general(a, b, (((0,), (0,)), ((), ())), preferred_element_type=f32)]
    all_gather x4 -> x9, waiting for transfers between devices: 763 us -> 64.4 us  [the longest x3 26 us: per_device(): lax.all_gather(sq_low[n], 'frame', axis=0, tiled=True)]
    pallas_call x0 -> x7, Pallas kernels: none -> 293 us  [the longest x2 105 us: decode_pass(): pl.pallas_call(functools.partial(kernel_decode, nf, scale), grid_spec=plt...]
    psum x6 -> x1, waiting for transfers between devices: 231 us -> 0.02 us  [per_device(): lax.psum((row_part * first_head, dzn_pairs), ('frame', 'head'))]
    mul x6 -> x1, other arithmetic: 213 us -> 0.8 us  [per_device(): row_part * first_head]
    all_gather x2, blocking collectives: 62 us -> 208 us  [the longest x1 154 us: per_device(): time_full = lax.all_gather(time_embed, 'head', axis=1, tiled=True)]
    convert_element_type x13 -> x11, local copies, waits for them, and re-layouts: 152 us -> 6.91 us  [the longest x1 2.52 us: per_device(): ddec = jnp.concatenate([jnp.concatenate([d[n] for d in decoded], 0).resha...]
    psum x3 -> x0, blocking collectives: 115 us -> none  [the longest x1 39.9 us: per_device(): lax.psum((loss_part, count_part, squares), ('frame', 'head'))]
  transfers between devices with their start and end apart: 11 -> 47, of which waited for: 10 -> 25; matrix products, arithmetic and copies ran while one was open for 6% -> 16% of each run, Pallas kernels for 0% -> 16%
where the time goes in v1:
time: 1180 us; the launch traced here: 1170 us
  Pallas kernels  293 us (25%)
  blocking collectives  245 us (21%)
  waiting for transfers between devices  218 us (18%)
  local copies, waits for them, and re-layouts  175 us (15%)
  other arithmetic  97.9 us (8%)
  matrix products  73.6 us (6%)
  starting transfers between devices  43.3 us (4%)
  between operations  24.4 us (2%)
    all_gather x1, blocking collectives, per_device(): time_full = lax.all_gather(time_embed, 'head', axis=1, tiled=True)  154 us
    pallas_call x2, Pallas kernels, decode_pass(): pl.pallas_call(functools.partial(kernel_decode, nf, scale), grid_spec=plt...  105 us
    ppermute x30, waiting for transfers between devices, swap(): return lax.ppermute(x, axis, [(i, i ^ bit) for i in range(size)])  103 us
    pallas_call x2, Pallas kernels, read_pass(): pl.pallas_call(functools.partial(kernel_read, nf), grid_spec=pltpu.Prefet...  100 us
    pallas_call x1, Pallas kernels, back_pass(): pl.pallas_call(functools.partial(kernel_back, nf, scale, videos_dev), gri...  66.1 us
    all_gather x1, blocking collectives, per_device(): q_all = lax.all_gather(query, 'head', axis=1, tiled=True)  53.6 us
    unnamed x222, local copies, waits for them, and re-layouts  27.7 us
    all_gather x3, waiting for transfers between devices, per_device(): lax.all_gather(sq_low[n], 'frame', axis=0, tiled=True)  26 us
  transfers between devices with their start and end apart: 47, of which 25 were waited for; matrix products, arithmetic and copies ran while one was open for 16% of the time, Pallas kernels for 16%

profile of v1, /device:TPU:0, one launch (start us, length us, event | category | flops | bytes accessed | tf_op | source)
XLA Modules:
  0.0 1171.1 jit_solution(9849731520358521431)
XLA Ops:
  10.5 19.9 %all-gather.17.cloned.1.call-done = bf16[2,192,1536]{2,1,0:T(8,128)(2,1)} async-done(((bf16[2,192,384]{2,1,0:T(8,128)(2,1)}), bf16[2,192,1536]{2,1,0:T(8,128)(2,1)}) %all-gather.17.cloned.1.call-update) | async-done | bytes 1179664 | tf_op jit(solution)/shard_map/weights/all_gather | solution.py:634
  37.0 10.8 dynamic-slice_bitcast_fusion
  50.4 154.2 %all_gather.33.time_ref = f32[12,1536]{1,0:T(8,128)} all-gather(f32[12,384]{1,0:T(8,128)S(1)} %copy-done.67), channel_id=1, replica_groups=mesh['frame'=8,'head'=4] {'head'}, dimensions={1}, use_global_device_ids=true | all-gather | bytes 92160 | tf_op jit(solution)/shard_map/weights/all_gather | solution.py:644
  210.7 53.6 %all_gather.35.x_ref.q = bf16[64,1536]{1,0:T(8,128)(2,1)} all-gather(bf16[64,384]{1,0:T(8,128)(2,1)S(1)} %fusion.56), channel_id=1, replica_groups=mesh['frame'=8,'head'=4] {'head'}, dimensions={1}, use_global_device_ids=true | all-gather | bytes 245760 | tf_op jit(solution)/shard_map/latent_keys/all_gather | solution.py:650
  264.3 5.8 absorb.1.qw
  271.3 49.8 %read_pass.2 = (bf16[6144,1664]{1,0:T(8,128)(2,1)}, bf16[2048,3072]{1,0:T(8,128)(2,1)}, bf16[2048,1664]{1,0:T(8,128)(2,1)}, f32[2048,128]{1,0:T(8,128)}, f32[128,1536]{1,0:T(8,128)}) custom-call(s32[13]{0:T(128)} %pad_add_fusion.2.place, bf16[24576,384]{1,0:T(8,128)(2,1)} %bitcast.290, bf16[3072,384]{1,0:T(8,128)(2,1)} %collective-permute-done.3.ra, ...), custom_call_target="tpu_custom_call" | custom-call | flops 19327352832 | bytes 37748736 | tf_op jit(solution)/shard_map/read/read_pass/pallas_call | solution.py:251
  321.1 50.2 %read_pass.3 = (bf16[6144,1664]{1,0:T(8,128)(2,1)}, bf16[2048,3072]{1,0:T(8,128)(2,1)}, bf16[2048,1664]{1,0:T(8,128)(2,1)}, f32[2048,128]{1,0:T(8,128)}, f32[128,1536]{1,0:T(8,128)}) custom-call(s32[13]{0:T(128)} %pad_add_fusion.1.place, ...), custom_call_target="tpu_custom_call", output_to_operand_aliasing={{0}: (9, {}), {1}: (10, {}), {2}: (11, {}), {3}: (12, {}), ... | custom-call | flops 19327352832 | bytes 37748736 | tf_op jit(solution)/shard_map/read/read_pass/pallas_call | solution.py:251
  374.7 5.4 all-to-all-start
  385.0 15.8 %all-to-all-done = bf16[8,16,1584]{2,1,0:T(8,128)(2,1)S(1)} async-done(((bf16[8,16,1584]{2,1,0:T(8,128)(2,1)}), bf16[8,16,1584]{2,1,0:T(8,128)(2,1)S(1)}, u32[]{:S(2)}, u32[]{:S(2)}) %all-to-all-start) | async-done | bytes 405536 | tf_op jit(solution)/shard_map/combine/all_to_all | solution.py:677
  419.5 6.8 collective-permute-done.7
  431.0 18.4 %all-gather.31.cloned.1.call-done = bf16[1,1536,1536]{2,1,0:T(8,128)(2,1)} async-done(((bf16[1,192,1536]{2,1,0:T(8,128)(2,1)}), bf16[1,1536,1536]{2,1,0:T(8,128)(2,1)}) %all-gather.31.cloned.1.call-update) | async-done | bytes 4718608 | tf_op jit(solution)/shard_map/weights/all_gather | solution.py:642
  457.9 5.4 collective-permute-done.9
  467.0 26.0 %all-gather.33.cloned.1.call-done = bf16[1,1536,384]{2,1,0:T(8,128)(2,1)} async-done(((bf16[1,192,384]{2,1,0:T(8,128)(2,1)}), bf16[1,1536,384]{2,1,0:T(8,128)(2,1)}) %all-gather.33.cloned.1.call-update) | async-done | bytes 1179664 | tf_op jit(solution)/shard_map/weights/all_gather | solution.py:638
  495.5 6.8 all_to_all.45
  510.2 5.5 reshape.398.msk
  515.8 12.5 %all-to-all-done.3 = bf16[8,16,4,768]{3,2,1,0:T(4,128)(2,1)} async-done(((bf16[8,16,4,768]{3,2,1,0:T(4,128)(2,1)}), bf16[8,16,4,768]{3,2,1,0:T(4,128)(2,1)}, u32[]{:S(2)}, u32[]{:S(2)}) %all-to-all-start.3) | async-done | bytes 786464 | tf_op jit(solution)/shard_map/decode/all_to_all | solution.py:721
  531.3 52.3 %decode_pass.2 = (f32[64,1536]{1,0:T(8,128)}, f32[64,1536]{1,0:T(8,128)}, bf16[1024,1536]{1,0:T(8,128)(2,1)}, f32[40,1536]{1,0:T(8,128)}, f32[8,384]{1,0:T(8,128)}) custom-call(s32[1]{0:T(128)} %bitcast.place, bf16[6144,1664]{1,0:T(8,128)(2,1)} %get-tuple-element.51.xn, bf16[24576,384]{1,0:T(8,128)(2,1)} %bitcast.292, ...), custom_call_target="tpu_custom_call" | custom-call | flops 28991029248 | bytes 18874368 | tf_op jit(solution)/shard_map/decode/decode_pass/pallas_call | solution.py:377
  584.6 52.5 %decode_pass.3 = (f32[64,1536]{1,0:T(8,128)}, f32[64,1536]{1,0:T(8,128)}, bf16[1024,1536]{1,0:T(8,128)(2,1)}, f32[40,1536]{1,0:T(8,128)}, f32[8,384]{1,0:T(8,128)}) custom-call(s32[1]{0:T(128)} %bitcast.place, bf16[6144,1664]{1,0:T(8,128)(2,1)} %get-tuple-element.51.xn, bf16[24576,384]{1,0:T(8,128)(2,1)} %bitcast.293, ...), custom_call_target="tpu_custom_call" | custom-call | flops 28991029248 | bytes 18874368 | tf_op jit(solution)/shard_map/decode/decode_pass/pallas_call | solution.py:377
  650.2 24.0 %all_to_all.46 = bf16[8,16,3072]{2,1,0:T(8,128)(2,1)} all-to-all(bf16[8,16,3072]{2,1,0:T(8,128)(2,1)} %convert_element_type.232), channel_id=1, replica_groups=mesh['frame'=8,'head'=4] {'frame'}, dimensions={0} | all-to-all | bytes 1572864 | tf_op jit(solution)/shard_map/latent_backward/all_to_all | solution.py:748
  678.7 6.9 all_to_all.47
  689.0 6.6 collective-permute-done.11
  754.1 12.5 %all-to-all-done.8 = bf16[8,16,4,408]{3,1,2,0:T(8,128)(2,1)} async-done(((bf16[8,16,4,408]{3,1,2,0:T(8,128)(2,1)}), bf16[8,16,4,408]{3,1,2,0:T(8,128)(2,1)}, u32[]{:S(2)}, u32[]{:S(2)}) %all-to-all-start.8) | async-done | bytes 417824 | tf_op jit(solution)/shard_map/latent_backward/all_to_all | solution.py:721
  777.3 16.7 %value_pass.1 = (bf16[2048,1536]{1,0:T(8,128)(2,1)}, bf16[1536,1536]{1,0:T(8,128)(2,1)}, f32[24,1536]{1,0:T(8,128)}) custom-call(bf16[128,1536]{1,0:T(8,128)(2,1)} %bitcast.315, bf16[1536,1536]{1,0:T(8,128)(2,1)} %bitcast.296, bf16[2048,1664]{1,0:T(8,128)(2,1)} %get-tuple-element.61.px, f32[2048,128]{1,0:T(8,128)} %get-tuple-element.53.st, f32[2048,128]{1,0:T(8,128)} %pad.8.ld), custom_call_target="tpu_custom_call" | custom-call | tf_op jit(solution)/shard_map/value/value_pass/pallas_call | solution.py:462
  794.0 66.1 %back_pass.1 = (f32[64,1536]{1,0:T(8,128)}, bf16[1536,1536]{1,0:T(8,128)(2,1)}, f32[40,1536]{1,0:T(8,128)}) custom-call(bf16[6144,1664]{1,0:T(8,128)(2,1)} %get-tuple-element.51.xn, bf16[2048,3072]{1,0:T(8,128)(2,1)} %get-tuple-element.60.e, f32[2048,128]{1,0:T(8,128)} %get-tuple-element.53.st, f32[2048,128]{1,0:T(8,128)} %pad.8.ld, ...), custom_call_target="tpu_custom_call" | custom-call | flops 38654705664 | bytes 37748736 | tf_op jit(solution)/shard_map/back/back_pass/pallas_call | solution.py:551
  860.1 4.9 constant_dynamic-slice_fusion.4
  869.5 4.9 constant_dynamic-slice_fusion.2
  913.2 44.4 %collective-permute-done.15 = bf16[88,384]{1,0:T(8,128)(2,1)S(1)} collective-permute-done((bf16[88,384]{1,0:T(8,128)(2,1)S(1)}, bf16[88,384]{1,0:T(8,128)(2,1)S(1)}, u32[]{:S(2)}, u32[]{:S(2)}) %collective-permute-start.15) | collective-permute-done | bytes 67616 | tf_op jit(solution)/shard_map/patch_gradients/ppermute | solution.py:86
  972.8 8.2 collective-permute-done.17
  981.1 11.6 collective-permute-done.18
  1096.3 7.8 add_divide_fusion
  1108.3 4.9 fusion.17
  1136.3 5.0 add_divide_fusion.1
  (588 shorter events, 370.6 us)
Async XLA Ops:
  7.2 23.2 %all-gather.17.cloned.1.call-start = ((), (), s32[]{:S(2)}) async-start(), calls=%async_computation.10 | async-start | bytes 1474560 | tf_op jit(solution)/shard_map/weights/all_gather | solution.py:634
  9.6 199.4 %all-gather.21.cloned.1.call-start = ((), (), s32[]{:S(2)}) async-start(), calls=%async_computation.13 | async-start | bytes 1327104 | tf_op jit(solution)/shard_map/weights/all_gather | solution.py:638
  10.4 253.8 %all-gather.23.cloned.1.call-start = ((), (), s32[]{:S(2)}) async-start(), calls=%async_computation.14 | async-start | bytes 5308416 | tf_op jit(solution)/shard_map/weights/all_gather | solution.py:635
  32.7 237.4 %all-gather.25.cloned.1.call-start = ((), (), s32[]{:S(2)}) async-start(), calls=%async_computation.15 | async-start | bytes 5308416 | tf_op jit(solution)/shard_map/weights/all_gather | solution.py:636
  33.3 381.7 %all-gather.27.cloned.1.call-start = ((), (), s32[]{:S(2)}) async-start(), calls=%async_computation.16 | async-start | bytes 1327104 | tf_op jit(solution)/shard_map/weights/all_gather | solution.py:638
  33.9 392.9 %all-gather.29.cloned.1.call-start = ((), (), s32[]{:S(2)}) async-start(), calls=%async_computation.17 | async-start | bytes 5308416 | tf_op jit(solution)/shard_map/weights/all_gather | solution.py:642
  36.8 412.6 %all-gather.31.cloned.1.call-start = ((), (), s32[]{:S(2)}) async-start(), calls=%async_computation.18 | async-start | bytes 5308416 | tf_op jit(solution)/shard_map/weights/all_gather | solution.py:642
  47.7 160.4 %collective-permute-start.3 = (bf16[3072,384]{1,0:T(8,128)(2,1)}, bf16[3072,384]{1,0:T(8,128)(2,1)}, u32[]{:S(2)}, u32[]{:S(2)}) collective-permute-start(bf16[3072,384]{1,0:T(8,128)(2,1)} %get-tuple-element.120), channel_id=1, source_target_pairs={{0,1},{1,0},{2,3},{3,2},{4,5},{5,4},{6,7},{7,6},{8,9},{9,8},{10,11... | collective-permute-start | bytes 7077896 | tf_op jit(solution)/shard_map/exchange/ppermute | solution.py:86
  48.0 222.1 %collective-permute-start.4 = (bf16[3072,384]{1,0:T(8,128)(2,1)}, bf16[3072,384]{1,0:T(8,128)(2,1)}, u32[]{:S(2)}, u32[]{:S(2)}) collective-permute-start(bf16[3072,384]{1,0:T(8,128)(2,1)} %get-tuple-element.119), channel_id=1, source_target_pairs={{0,2},{1,3},{2,0},{3,1},{4,6},{5,7},{6,4},{7,5},{8,10},{9,11},{10,... | collective-permute-start | bytes 7077896 | tf_op jit(solution)/shard_map/exchange/ppermute | solution.py:86
  48.1 221.9 %collective-permute-start.5 = (bf16[3072,384]{1,0:T(8,128)(2,1)}, bf16[3072,384]{1,0:T(8,128)(2,1)}, u32[]{:S(2)}, u32[]{:S(2)}) collective-permute-start(bf16[3072,384]{1,0:T(8,128)(2,1)} %get-tuple-element.118), channel_id=1, source_target_pairs={{0,3},{1,2},{2,1},{3,0},{4,7},{5,6},{6,5},{7,4},{8,11},{9,10},{10,... | collective-permute-start | bytes 7077896 | tf_op jit(solution)/shard_map/exchange/ppermute | solution.py:86
  49.6 271.5 %collective-permute-start = (bf16[3072,384]{1,0:T(8,128)(2,1)}, bf16[3072,384]{1,0:T(8,128)(2,1)}, u32[]{:S(2)}, u32[]{:S(2)}) collective-permute-start(bf16[3072,384]{1,0:T(8,128)(2,1)} %get-tuple-element.123), channel_id=1, source_target_pairs={{0,1},{1,0},{2,3},{3,2},{4,5},{5,4},{6,7},{7,6},{8,9},{9,8},{10,11... | collective-permute-start | bytes 7077896 | tf_op jit(solution)/shard_map/exchange/ppermute | solution.py:86
  50.1 271.0 %collective-permute-start.1 = (bf16[3072,384]{1,0:T(8,128)(2,1)}, bf16[3072,384]{1,0:T(8,128)(2,1)}, u32[]{:S(2)}, u32[]{:S(2)}) collective-permute-start(bf16[3072,384]{1,0:T(8,128)(2,1)} %get-tuple-element.122), channel_id=1, source_target_pairs={{0,2},{1,3},{2,0},{3,1},{4,6},{5,7},{6,4},{7,5},{8,10},{9,11},{10,... | collective-permute-start | bytes 7077896 | tf_op jit(solution)/shard_map/exchange/ppermute | solution.py:86
  208.1 113.0 %collective-permute-start.2 = (bf16[3072,384]{1,0:T(8,128)(2,1)}, bf16[3072,384]{1,0:T(8,128)(2,1)}, u32[]{:S(2)}, u32[]{:S(2)}) collective-permute-start(bf16[3072,384]{1,0:T(8,128)(2,1)} %get-tuple-element.121), channel_id=1, source_target_pairs={{0,3},{1,2},{2,1},{3,0},{4,7},{5,6},{6,5},{7,4},{8,11},{9,10},{10,... | collective-permute-start | bytes 7077896 | tf_op jit(solution)/shard_map/exchange/ppermute | solution.py:86
  374.7 26.1 %all-to-all-start = ((bf16[8,16,1584]{2,1,0:T(8,128)(2,1)}), bf16[8,16,1584]{2,1,0:T(8,128)(2,1)S(1)}, u32[]{:S(2)}, u32[]{:S(2)}) async-start(bf16[8,16,1584]{2,1,0:T(8,128)(2,1)} %bitcast.17), calls=%async_computation | async-start | bytes 851968 | tf_op jit(solution)/shard_map/combine/all_to_all | solution.py:677
  408.8 84.2 %all-gather.33.cloned.1.call-start = ((), (), s32[]{:S(2)}) async-start(), calls=%async_computation.19 | async-start | bytes 1327104 | tf_op jit(solution)/shard_map/weights/all_gather | solution.py:638
  503.5 24.8 %all-to-all-start.3 = ((bf16[8,16,4,768]{3,2,1,0:T(4,128)(2,1)}), bf16[8,16,4,768]{3,2,1,0:T(4,128)(2,1)}, u32[]{:S(2)}, u32[]{:S(2)}) async-start(bf16[8,16,4,768]{3,2,1,0:T(4,128)(2,1)} %broadcast_in_dim.22), calls=%async_computation.3 | async-start | bytes 1572864 | tf_op jit(solution)/shard_map/decode/all_to_all | solution.py:721
  705.4 7.5 collective-permute-start.12
  731.2 12.2 %all-to-all-start.7 = ((bf16[4,16,408]{2,1,0:T(8,128)(2,1)}), bf16[4,16,408]{2,1,0:T(8,128)(2,1)}, u32[]{:S(2)}, u32[]{:S(2)}) async-start(bf16[4,16,408]{2,1,0:T(8,128)(2,1)} %bitcast.44), calls=%async_computation.7 | async-start | bytes 131072 | tf_op jit(solution)/shard_map/latent_backward/all_to_all | solution.py:718
  735.1 275.4 %all-reduce.5.cloned.1.call-start = ((), (), s32[]{:S(2)}) async-start(), calls=%async_computation.20 | async-start | bytes 1671168 | tf_op jit(solution)/shard_map/patch_gradients/psum | solution.py:868
  745.0 21.5 %all-to-all-start.8 = ((bf16[8,16,4,408]{3,1,2,0:T(8,128)(2,1)}), bf16[8,16,4,408]{3,1,2,0:T(8,128)(2,1)}, u32[]{:S(2)}, u32[]{:S(2)}) async-start(bf16[8,16,4,408]{3,1,2,0:T(8,128)(2,1)} %broadcast_in_dim.23), calls=%async_computation.8 | async-start | bytes 1048576 | tf_op jit(solution)/shard_map/latent_backward/all_to_all | solution.py:721
  749.2 276.5 %all-gather.19.cloned.1.call-start = ((), (), s32[]{:S(2)}) async-start(), calls=%async_computation.11 | async-start | bytes 4866048 | tf_op jit(solution)/shard_map/row_gradients/all_gather | solution.py:817
  750.1 298.2 %reduce-scatter.2.cloned.1.call-start = ((), (), s32[]{:S(2)}) async-start(), calls=%async_computation.12 | async-start | bytes 2654208 | tf_op jit(solution)/shard_map/key_value_gradients/reduce_scatter | solution.py:886
  869.4 28.6 %collective-permute-start.19 = (bf16[2,384,1536]{1,2,0:T(8,128)(2,1)}, bf16[2,384,1536]{1,2,0:T(8,128)(2,1)}, u32[]{:S(2)}, u32[]{:S(2)}) collective-permute-start(bf16[2,384,1536]{1,2,0:T(8,128)(2,1)} %bitcast.313), channel_id=1, source_target_pairs={{0,1},{1,0},{2,3},{3,2},{4,5},{5,4},{6,7},{7,6},{8,9},{9,8},{10,11... | collective-permute-start | bytes 7077896 | tf_op jit(solution)/shard_map/key_value_gradients/ppermute | solution.py:86
  878.7 25.4 %collective-permute-start.21 = (bf16[2,384,1536]{1,2,0:T(8,128)(2,1)}, bf16[2,384,1536]{1,2,0:T(8,128)(2,1)}, u32[]{:S(2)}, u32[]{:S(2)}) collective-permute-start(bf16[2,384,1536]{1,2,0:T(8,128)(2,1)} %bitcast.312), channel_id=1, source_target_pairs={{0,1},{1,0},{2,3},{3,2},{4,5},{5,4},{6,7},{7,6},{8,9},{9,8},{10,11... | collective-permute-start | bytes 7077896 | tf_op jit(solution)/shard_map/key_value_gradients/ppermute | solution.py:86
  889.4 21.6 %collective-permute-start.14 = (f32[2,88,384]{2,1,0:T(8,128)}, f32[2,88,384]{2,1,0:T(8,128)}, u32[]{:S(2)}, u32[]{:S(2)}) collective-permute-start(f32[2,88,384]{2,1,0:T(8,128)} %bitcast.288), channel_id=1, source_target_pairs={{0,1},{1,0},{2,3},{3,2},{4,5},{5,4},{6,7},{7,6},{8,9},{9,8},{10,11... | collective-permute-start | bytes 811016 | tf_op jit(solution)/shard_map/patch_gradients/ppermute | solution.py:86
  902.0 56.5 %collective-permute-start.20 = (bf16[384,1536]{0,1:T(8,128)(2,1)}, bf16[384,1536]{0,1:T(8,128)(2,1)}, u32[]{:S(2)}, u32[]{:S(2)}) collective-permute-start(bf16[384,1536]{0,1:T(8,128)(2,1)} %fusion.30), channel_id=1, source_target_pairs={{0,2},{1,3},{2,0},{3,1},{4,6},{5,7},{6,4},{7,5},{8,10},{9,11},{10,... | collective-permute-start | bytes 3538952 | tf_op jit(solution)/shard_map/key_value_gradients/ppermute | solution.py:86
  909.0 52.8 %collective-permute-start.22 = (bf16[384,1536]{0,1:T(8,128)(2,1)}, bf16[384,1536]{0,1:T(8,128)(2,1)}, u32[]{:S(2)}, u32[]{:S(2)}) collective-permute-start(bf16[384,1536]{0,1:T(8,128)(2,1)} %fusion.31), channel_id=1, source_target_pairs={{0,2},{1,3},{2,0},{3,1},{4,6},{5,7},{6,4},{7,5},{8,10},{9,11},{10,... | collective-permute-start | bytes 3538952 | tf_op jit(solution)/shard_map/key_value_gradients/ppermute | solution.py:86
  912.8 44.8 %collective-permute-start.15 = (bf16[88,384]{1,0:T(8,128)(2,1)S(1)}, bf16[88,384]{1,0:T(8,128)(2,1)S(1)}, u32[]{:S(2)}, u32[]{:S(2)}) collective-permute-start(bf16[88,384]{1,0:T(8,128)(2,1)S(1)} %fusion.122), channel_id=1, source_target_pairs={{0,2},{1,3},{2,0},{3,1},{4,6},{5,7},{6,4},{7,5},{8,10},{9,11},{10,... | collective-permute-start | bytes 202760 | tf_op jit(solution)/shard_map/patch_gradients/ppermute | solution.py:86
  972.4 8.6 collective-permute-start.17
  981.1 11.6 collective-permute-start.18
  993.4 11.5 collective-permute-start.23
  1001.0 24.6 %all-to-all-start.6 = ((bf16[8,64,768]{2,1,0:T(8,128)(2,1)}), bf16[8,64,768]{2,1,0:T(8,128)(2,1)S(1)}, u32[]{:S(2)}, u32[]{:S(2)}) async-start(bf16[8,64,768]{2,1,0:T(8,128)(2,1)} %maximum_bitcast_fusion.1), calls=%async_computation.6 | async-start | bytes 1572864 | tf_op jit(solution)/shard_map/row_gradients/all_to_all | solution.py:824
  (120 other events, 2314.8 us)
Sparse Core Ops, SparseCore 0:
  10.2 20.1 all-gather.16
  33.1 41.0 all-gather.20
  77.0 78.6 all-gather.22
  158.3 78.0 all-gather.24
  238.9 39.2 all-gather.26
  280.8 78.6 all-gather.28
  362.3 87.1 all-gather.30
  453.5 39.3 all-gather.32
  743.4 131.4 all-reduce.4
  877.6 74.7 all-gather.18
  966.8 76.8 reduce-scatter.1

commit v2 on v1

v2 whole, which is shorter than its diff:
```python
import functools

import jax
import jax.numpy as jnp
from jax import lax
from jax.experimental import pallas as pl
from jax.experimental.pallas import tpu as pltpu
from jax.sharding import PartitionSpec as P

HEAD_SIZE = 96
LATENTS = 64
PATCH = 256
FRAMES = 96
STEP = 5
GROUP = 4
EXTRA = 128
TAIL = 16
VMEM_BYTES = 62 * 1024 * 1024

HIGH_ACCURACY = lax.Precision.HIGHEST
clip_max = 0.05
beta_one = 0.5
beta_two = 0.6
adam_eps = 1e-08
BRIEF = pl.CostEstimate(flops=1, bytes_accessed=1, transcendentals=0)
f32 = jnp.float32
bf16 = jnp.bfloat16


def nn(a, b):
    return lax.dot_general(a, b, (((1,), (0,)), ((), ())), preferred_element_type=f32)


def nt(a, b):
    return lax.dot_general(a, b, (((1,), (1,)), ((), ())), preferred_element_type=f32)


def tn(a, b):
    return lax.dot_general(a, b, (((0,), (0,)), ((), ())), preferred_element_type=f32)


def normalize_rows(v):
    cent = v - jnp.mean(v, -1, keepdims=True)
    rstd = lax.rsqrt(jnp.mean(cent * cent, -1, keepdims=True) + 1e-05)
    return (cent * rstd, rstd)


def norm_reverse(dy, xhat, rstd, gain):
    scaled = dy * gain
    first = jnp.mean(scaled, -1, keepdims=True)
    second = jnp.mean(scaled * xhat, -1, keepdims=True)
    return rstd * (scaled - first - xhat * second)


def adam_moments(grad, one, two):
    one = beta_one * one + (1.0 - beta_one) * grad
    two = beta_two * two + (1.0 - beta_two) * grad * grad
    step = one / (1.0 - beta_one**STEP) / (jnp.sqrt(two / (1.0 - beta_two**STEP)) + adam_eps)
    return (one, two, step)


def adamw_update(weight, grad, one, two, decay):
    one, two, step = adam_moments(grad, one, two)
    return (weight - 0.3 * (step + decay * weight), one, two)


def swap(x, axis, bit):
    size = lax.axis_size(axis)
    return lax.ppermute(x, axis, [(i, i ^ bit) for i in range(size)])


def sum_over(x, axis):
    bit = 1
    while bit < lax.axis_size(axis):
        x = x + swap(x, axis, bit)
        bit *= 2
    return x


def sum_rounded(x, axis):
    bit = 1
    while bit < lax.axis_size(axis):
        x = lax.reduce_precision(x, 8, 7)
        x = x + swap(x.astype(bf16), axis, bit).astype(f32)
        bit *= 2
    return x


def sum_head(x):
    x = x + swap(x, "head", 1)
    x = lax.reduce_precision(x, 8, 7)
    return x + swap(x.astype(bf16), "head", 2).astype(f32)


def gather_head(x, axis):
    me = lax.axis_index("head")
    bit = 1
    while bit < lax.axis_size("head"):
        away = swap(x, "head", bit)
        mine_first = (me & bit) == 0
        x = jnp.concatenate(
            [jnp.where(mine_first, x, away), jnp.where(mine_first, away, x)], axis
        )
        bit *= 2
    return x


def zero_of(x):
    return (x[(0,) * x.ndim].astype(f32) * 0.0).astype(jnp.int32)


def after(x, *deps):
    return lax.optimization_barrier((x, *deps))[0]


def split_three(x):
    high = lax.reduce_precision(x, 8, 7)
    rest = x - high
    mid = lax.reduce_precision(rest, 8, 7)
    return jnp.concatenate([high, mid, rest - mid], -1).astype(bf16)


def join_three(x):
    n = x.shape[-1] // 3
    x = x.astype(f32)
    return x[..., :n] + x[..., n : 2 * n] + x[..., 2 * n :]


def head_of_lane(rows, cols):
    return lax.broadcasted_iota(jnp.int32, (rows, cols), 1) // HEAD_SIZE


def spread(x):
    owner = head_of_lane(*x.shape)
    x = x.astype(f32)
    return jnp.concatenate([jnp.where(owner == j, x, 0.0) for j in range(GROUP)], 0).astype(bf16)


def collect(r):
    rows = r.shape[0] // GROUP
    owner = head_of_lane(rows, r.shape[1])
    out = jnp.where(owner == 0, r[:rows], 0.0)
    for j in range(1, GROUP):
        out = out + jnp.where(owner == j, r[j * rows : (j + 1) * rows], 0.0)
    return out


def whole(shape):
    return pl.BlockSpec(shape, lambda *_: (0,) * len(shape), pipeline_mode=pl.Buffered(1))


def kernel_absorb(scale, x_ref, w_ref, out_ref):
    out_ref[...] = (nt(spread(x_ref[...]), w_ref[...]) * scale).astype(bf16)


def absorb(x, w, scale):
    depth, width = w.shape
    cols = GROUP * HEAD_SIZE
    groups = width // cols
    rows = GROUP * LATENTS
    return pl.pallas_call(
        functools.partial(kernel_absorb, scale),
        grid=(groups,),
        in_specs=[
            pl.BlockSpec((LATENTS, cols), lambda g: (0, g)),
            pl.BlockSpec((depth, cols), lambda g: (0, g)),
        ],
        out_specs=pl.BlockSpec((rows, depth), lambda g: (g, 0)),
        out_shape=jax.ShapeDtypeStruct((groups * rows, depth), bf16),
        compiler_params=pltpu.CompilerParams(vmem_limit_bytes=VMEM_BYTES),
        cost_estimate=BRIEF,
        name="absorb",
    )(x, w)


def kernel_pick(place, a, b, c, far_o, near_o):
    del place
    far_o[0] = a[...]
    far_o[1] = b[...]
    near_o[...] = c[...]


def pick(feat, place, j, c, videos_dev):
    count, tokens_video, cols = feat.shape
    frames_dev = tokens_video // PATCH
    cuts, nf = chunks_of(frames_dev)
    step = nf * PATCH
    blocks = cuts[c] // nf
    start = (j * frames_dev + sum(cuts[:c])) // nf
    tokens = cuts[c] * PATCH
    feat2 = feat.reshape(count * tokens_video, cols)

    def spot(k):
        return lambda i, p: ((p[0] ^ k) * (videos_dev * frames_dev // nf) + start + i, 0)

    return pl.pallas_call(
        kernel_pick,
        grid_spec=pltpu.PrefetchScalarGridSpec(
            num_scalar_prefetch=1,
            grid=(blocks,),
            in_specs=[pl.BlockSpec((step, cols), spot(k)) for k in (2, 3, 1)],
            out_specs=[
                pl.BlockSpec((2, step, cols), lambda i, p: (0, i, 0)),
                pl.BlockSpec((step, cols), lambda i, p: (i, 0)),
            ],
        ),
        out_shape=[
            jax.ShapeDtypeStruct((2, tokens, cols), bf16),
            jax.ShapeDtypeStruct((tokens, cols), bf16),
        ],
        compiler_params=pltpu.CompilerParams(vmem_limit_bytes=VMEM_BYTES),
        cost_estimate=BRIEF,
        name="pick",
    )(place[None], feat2, feat2, feat2)


def kernel_gate(*refs):
    del refs


def gate(x, *deps):
    anyspec = pl.BlockSpec(memory_space=pl.ANY)
    return pl.pallas_call(
        kernel_gate,
        in_specs=[anyspec] * (1 + len(deps)),
        out_specs=anyspec,
        out_shape=jax.ShapeDtypeStruct(x.shape, x.dtype),
        input_output_aliases={0: 0},
        cost_estimate=BRIEF,
        name="gate",
    )(x, *deps)


def frames_a_block(frames):
    return 2 if frames % 2 == 0 else 1


def chunks_of(frames):
    if frames % 6 == 0:
        return (frames // 3 * 2, frames // 3), frames // 3
    return (frames,), 1


def kernel_read(
    nf, first, place, own, ra, rb, rc, time_ref, g0, qw, wv, xn_in, ft_in, e_in, px_in, st_in, o_in, dep,
    xn_o, ft_o, e_o, px_o, st_o, o_o, token_o, xs, acc, run,
):
    del xn_in, ft_in, e_in, px_in, st_in, o_in, dep
    i = pl.program_id(0)
    tokens, depth = xs.shape
    cols = own.shape[1]
    heads_rows = GROUP * LATENTS
    groups = qw.shape[0] // heads_rows

    @pl.when(i == 0)
    def _():
        acc[...] = jnp.zeros_like(acc)
        run[0] = jnp.full(run.shape[1:], -1e30, f32)
        run[1] = jnp.zeros(run.shape[1:], f32)
        st_o[...] = jnp.zeros_like(st_o)

    for k, part in enumerate((own, ra, rb, rc)):
        off = pl.multiple_of((place[0] ^ k) * cols, 128)
        for f in range(nf):
            rows = slice(f * PATCH, (f + 1) * PATCH)
            raw = part[rows, :]
            ft_o[rows, pl.ds(off, cols)] = raw
            row = first + i * nf + f
            moved = raw.astype(f32) + time_ref[pl.ds(row, 1), pl.ds(off, cols)]
            xs[rows, pl.ds(off, cols)] = moved.astype(bf16)
    x = xs[...].astype(f32)
    cent = x - jnp.sum(x, -1, keepdims=True) * (1.0 / depth)
    rstd = lax.rsqrt(jnp.sum(cent * cent, -1, keepdims=True) * (1.0 / depth) + 1e-05)
    xn_o[:, :depth] = (cent * rstd * g0[...]).astype(bf16)
    lane = lax.broadcasted_iota(jnp.int32, (tokens, EXTRA), 1)
    frame = lax.broadcasted_iota(jnp.int32, (tokens, EXTRA), 0) // PATCH + first + i * nf
    xn_o[:, depth:] = jnp.where(lane == frame, rstd, 0.0).astype(bf16)
    key = lax.broadcasted_iota(jnp.int32, (1, tokens), 1)
    limit = place[1 + first + i * nf]
    for f in range(1, nf):
        limit = jnp.where(key >= f * PATCH, f * PATCH + place[1 + first + i * nf + f], limit)
    valid = key < limit
    block = lax.broadcasted_iota(jnp.int32, (heads_rows, 128), 1)
    last = i == pl.num_programs(0) - 1
    for g in range(groups):
        rows = slice(g * heads_rows, (g + 1) * heads_rows)
        scores = jnp.where(valid, nt(qw[rows, :], xn_o[:, :depth]), -1e30)
        old = run[0, rows, :]
        new = jnp.maximum(old, jnp.max(scores, -1, keepdims=True))
        expo = jnp.exp(scores - new[:, :1])
        shrink = jnp.exp(old - new)
        total = run[1, rows, :] * shrink + jnp.sum(expo, -1, keepdims=True)
        run[0, rows, :] = new
        run[1, rows, :] = total
        low = expo.astype(bf16)
        e_o[rows, :] = low
        stats = jnp.where(block == i, new, st_o[rows, :])
        stats = jnp.where(last & (block == 126), new, stats)
        st_o[rows, :] = jnp.where(last & (block == 127), total, stats)
        acc[rows, :] = acc[rows, :] * shrink[:, :1] + nn(low, xn_o[...])

    @pl.when(last)
    def _():
        for g in range(groups):
            rows = slice(g * heads_rows, (g + 1) * heads_rows)
            wide = slice(g * cols, (g + 1) * cols)
            held = acc[rows, :].astype(bf16)
            px_o[rows, :] = held
            mixed = nn(held[:, :depth], wv[:, wide]) * (1.0 / run[1, rows, :1])
            o_o[:, wide] = collect(mixed)
        token_o[...] = run[1, 0:8, :]


def read_pass(j, c, prev, feat, got, time_full, gain, lens, qw, wv, dep, h, videos_dev):
    count, tokens_video, cols = feat.shape
    depth = wv.shape[0]
    frames_dev = tokens_video // PATCH
    cuts, nf = chunks_of(frames_dev)
    chunks = len(cuts)
    frames = cuts[c]
    before = sum(cuts[:c])
    tokens = nf * PATCH
    blocks = frames // nf
    start = (j * frames_dev + before) // nf
    rows = qw.shape[0]
    part = j * chunks + c
    parts = videos_dev * chunks
    place = jnp.concatenate([h[None], lens]).astype(jnp.int32)
    feat2 = feat.reshape(count * tokens_video, cols)
    shapes = (
        jax.ShapeDtypeStruct((videos_dev * tokens_video, depth + EXTRA), bf16),
        jax.ShapeDtypeStruct((videos_dev * tokens_video, depth), bf16),
        jax.ShapeDtypeStruct((videos_dev * rows, tokens_video), bf16),
        jax.ShapeDtypeStruct((parts * rows, depth + EXTRA), bf16),
        jax.ShapeDtypeStruct((parts * rows, 128), f32),
        jax.ShapeDtypeStruct((parts * LATENTS, depth), f32),
    )
    aliases = {}
    if prev is None:
        prev = [jnp.zeros((16, 128), s.dtype) for s in shapes]
    else:
        aliases = {9 + n: n for n in range(6)}
    anyspec = pl.BlockSpec(memory_space=pl.ANY)
    one = pl.Buffered(1)
    return pl.pallas_call(
        functools.partial(kernel_read, nf, before),
        grid_spec=pltpu.PrefetchScalarGridSpec(
            num_scalar_prefetch=1,
            grid=(blocks,),
            in_specs=[
                pl.BlockSpec(
                    (tokens, cols),
                    lambda i, p: (p[0] * (videos_dev * frames_dev // nf) + start + i, 0),
                ),
                pl.BlockSpec((tokens, cols), lambda i, p: (i, 0)),
                pl.BlockSpec((tokens, cols), lambda i, p: (i, 0)),
                pl.BlockSpec((tokens, cols), lambda i, p: (i, 0)),
                whole(time_full.shape),
                whole(gain.shape),
                whole(qw.shape),
                whole(wv.shape),
            ]
            + [anyspec] * 7,
            out_specs=[
                pl.BlockSpec((tokens, depth + EXTRA), lambda i, p: (start + i, 0)),
                pl.BlockSpec((tokens, depth), lambda i, p: (start + i, 0)),
                pl.BlockSpec((rows, tokens), lambda i, p: (j, before // nf + i)),
                pl.BlockSpec((rows, depth + EXTRA), lambda i, p: (part, 0), pipeline_mode=one),
                pl.BlockSpec((rows, 128), lambda i, p: (part, 0), pipeline_mode=one),
                pl.BlockSpec((LATENTS, depth), lambda i, p: (part, 0), pipeline_mode=one),
                whole((8, 128)),
            ],
            scratch_shapes=[
                pltpu.VMEM((tokens, depth), bf16),
                pltpu.VMEM((rows, depth + EXTRA), f32),
                pltpu.VMEM((2, rows, 128), f32),
            ],
        ),
        out_shape=(*shapes, jax.ShapeDtypeStruct((8, 128), f32)),
        input_output_aliases=aliases,
        compiler_params=pltpu.CompilerParams(vmem_limit_bytes=VMEM_BYTES),
        cost_estimate=pl.CostEstimate(
            flops=rows * frames * PATCH * depth // 2,
            bytes_accessed=frames * PATCH * depth,
            transcendentals=rows * frames * PATCH,
        ),
        name="read_pass",
    )(place, feat2, *got, time_full, gain, qw, wv, *prev, dep)


def kernel_decode(
    nf, scale, xn, feat, msk, dq, dv, wk,
    ddq_o, ddv_o, dx_o, side_o, loss_o, dqw, dvd, sc, zs, acc, dacc, loss,
):
    i = pl.program_id(0)
    tokens = xn.shape[0]
    depth = wk.shape[0]
    heads_rows = GROUP * LATENTS
    total_rows = dqw.shape[0]
    groups = total_rows // heads_rows
    cols = depth // groups

    @pl.when(i == 0)
    def _():
        acc[...] = jnp.zeros_like(acc)
        dacc[...] = jnp.zeros_like(dacc)
        loss[...] = jnp.zeros_like(loss)
        for g in range(groups):
            rows = slice(g * heads_rows, (g + 1) * heads_rows)
            wide = slice(g * cols, (g + 1) * cols)
            dqw[rows, :] = (nt(spread(dq[:, wide]), wk[:, wide]) * scale).astype(bf16)
            dvd[g] = spread(dv[:, wide])

    sc[...] = nt(dqw[...], xn[:, :depth])
    counts = msk[...]
    second = jnp.zeros((1, tokens), f32)
    for g in range(groups):
        rows = slice(g * heads_rows, (g + 1) * heads_rows)
        wide = slice(g * cols, (g + 1) * cols)
        s = sc[rows, :].reshape(GROUP, LATENTS, tokens)
        a = jnp.exp(s - jnp.max(s, 1, keepdims=True))
        a = a * (1.0 / jnp.sum(a, 1, keepdims=True))
        low = a.reshape(heads_rows, tokens).astype(bf16)
        error = tn(low, dvd[g]) - feat[:, wide].astype(f32)
        kept = counts * error
        loss[...] += jnp.sum((kept * error).reshape(tokens // 8, 8, cols), 0)
        dp = (2.0 * kept).astype(bf16)
        dacc[g] += nn(low, dp)
        da = nt(dvd[g], dp).reshape(GROUP, LATENTS, tokens)
        z = a * (da - jnp.sum(a * da, 1, keepdims=True))
        second = second + jnp.sum((z * s).reshape(heads_rows, tokens), 0, keepdims=True)
        zs[rows, :] = z.reshape(heads_rows, tokens).astype(bf16)
    zs[total_rows:, :] = tail_rows(nf, i, second, xn, depth)
    acc[...] += nn(zs[...], xn[...])

    @pl.when(i == pl.num_programs(0) - 1)
    def _():
        gain = jnp.zeros((8, depth), f32)
        for g in range(groups):
            rows = slice(g * heads_rows, (g + 1) * heads_rows)
            wide = slice(g * cols, (g + 1) * cols)
            held = acc[rows, :depth]
            low = held.astype(bf16)
            dx_o[rows, :] = low
            ddq_o[:, wide] = collect(nn(low, wk[:, wide])) * scale
            ddv_o[:, wide] = collect(dacc[g])
            gain = gain + jnp.sum(
                (held * dqw[rows, :].astype(f32)).reshape(heads_rows // 8, 8, depth), 0
            )
        side_o[0:TAIL, :] = tn(acc[:total_rows, depth:].astype(bf16), dqw[...])[:TAIL]
        side_o[TAIL : 2 * TAIL, :] = acc[total_rows:, :depth]
        side_o[2 * TAIL :, :] = gain
        loss_o[...] = loss[...]


def tail_rows(nf, i, second, xn, depth):
    tokens = xn.shape[0]
    rstd = nt(jnp.ones((TAIL, EXTRA), bf16), xn[:, depth:])
    row = lax.broadcasted_iota(jnp.int32, (TAIL, tokens), 0)
    frame = lax.broadcasted_iota(jnp.int32, (TAIL, tokens), 1) // PATCH + i * nf
    return jnp.where(row == frame, rstd * second * (1.0 / depth), 0.0).astype(bf16)


def decode_pass(j, xn_all, ft_all, counts, dq_all, dv_all, wk, scale, videos_dev):
    depth = wk.shape[0]
    tokens_video = xn_all.shape[0] // videos_dev
    cols = GROUP * HEAD_SIZE
    frames_dev = tokens_video // PATCH
    nf = frames_a_block(frames_dev)
    tokens = nf * PATCH
    blocks = frames_dev // nf
    groups = depth // cols
    heads_rows = GROUP * LATENTS
    rows = groups * heads_rows
    one = pl.Buffered(1)
    return pl.pallas_call(
        functools.partial(kernel_decode, nf, scale),
        grid=(blocks,),
        in_specs=[
            pl.BlockSpec((tokens, depth + EXTRA), lambda i: (j * blocks + i, 0)),
            pl.BlockSpec((tokens, depth), lambda i: (j * blocks + i, 0)),
            pl.BlockSpec((tokens, 1), lambda i: (j * blocks + i, 0)),
            pl.BlockSpec((LATENTS, depth), lambda i: (j, 0), pipeline_mode=one),
            pl.BlockSpec((LATENTS, depth), lambda i: (j, 0), pipeline_mode=one),
            whole(wk.shape),
        ],
        out_specs=[
            whole((LATENTS, depth)),
            whole((LATENTS, depth)),
            whole((rows, depth)),
            whole((2 * TAIL + 8, depth)),
            whole((8, cols)),
        ],
        scratch_shapes=[
            pltpu.VMEM((rows, depth), bf16),
            pltpu.VMEM((groups, heads_rows, cols), bf16),
            pltpu.VMEM((rows, tokens), f32),
            pltpu.VMEM((rows + TAIL, tokens), bf16),
            pltpu.VMEM((rows + TAIL, depth + EXTRA), f32),
            pltpu.VMEM((groups, heads_rows, cols), f32),
            pltpu.VMEM((8, cols), f32),
        ],
        out_shape=(
            jax.ShapeDtypeStruct((LATENTS, depth), f32),
            jax.ShapeDtypeStruct((LATENTS, depth), f32),
            jax.ShapeDtypeStruct((rows, depth), bf16),
            jax.ShapeDtypeStruct((2 * TAIL + 8, depth), f32),
            jax.ShapeDtypeStruct((8, cols), f32),
        ),
        compiler_params=pltpu.CompilerParams(vmem_limit_bytes=VMEM_BYTES),
        cost_estimate=pl.CostEstimate(
            flops=6 * rows * tokens_video * depth,
            bytes_accessed=tokens_video * depth * 4,
            transcendentals=rows * tokens_video,
        ),
        name="decode_pass",
    )(xn_all, ft_all, counts, dq_all, dv_all, wk)


def head_column(ld, first):
    lane = lax.broadcasted_iota(jnp.int32, ld.shape, 1)
    return jnp.concatenate(
        [jnp.sum(jnp.where(lane == first + j, ld, 0.0), -1, keepdims=True) for j in range(GROUP)], 0
    )


def kernel_value(chunks, place, do, wv, ld, *rest):
    pxs = rest[:chunks]
    sts = rest[chunks : 2 * chunks]
    ow_o, near_o, away_o, side_o, acc = rest[2 * chunks :]
    k = pl.program_id(0)
    v = pl.program_id(1)
    depth = wv.shape[0]

    @pl.when((k == 0) & (v == 0))
    def _():
        side_o[...] = jnp.zeros_like(side_o)

    diag = spread(do[...])
    ow = nt(diag, wv[...]).astype(bf16)
    ow_o[...] = ow
    norm = 0.0
    lse = head_column(ld[...], (place[0] ^ k) * GROUP)
    for px, st in zip(pxs, sts):
        norm = norm + px[...].astype(f32) * jnp.exp(st[:, 126:127] - lse)
    low = norm.astype(bf16)
    part = tn(diag, low[:, :depth])

    @pl.when(v == 0)
    def _():
        acc[...] = part

    @pl.when(v > 0)
    def _():
        acc[...] += part

    @pl.when(k & 1 == 0)
    def _():
        near_o[0] = acc[...].astype(bf16)

    @pl.when(k & 1 == 1)
    def _():
        away_o[0] = acc[...].astype(bf16)

    side_o[0:TAIL, :] += tn(low[:, depth:], ow)[:TAIL]
    rows = ow.shape[0]
    side_o[TAIL:, :] += jnp.sum((ow.astype(f32) * norm[:, :depth]).reshape(rows // 8, 8, depth), 0)


def value_pass(do_all, wv, px_all, st_all, ld, h, videos_dev):
    depth = wv.shape[0]
    cols = GROUP * HEAD_SIZE
    groups = depth // cols
    rows = GROUP * LATENTS
    chunks = px_all.shape[0] // (videos_dev * groups * rows)

    def spot(c):
        return lambda k, v, p: ((v * chunks + c) * groups + (p[0] ^ k), 0)

    return pl.pallas_call(
        functools.partial(kernel_value, chunks),
        grid_spec=pltpu.PrefetchScalarGridSpec(
            num_scalar_prefetch=1,
            grid=(groups, videos_dev),
            in_specs=[
                pl.BlockSpec((LATENTS, cols), lambda k, v, p: (v, p[0] ^ k)),
                pl.BlockSpec((depth, cols), lambda k, v, p: (0, p[0] ^ k)),
                pl.BlockSpec((LATENTS, 128), lambda k, v, p: (v, 0)),
            ]
            + [pl.BlockSpec((rows, depth + EXTRA), spot(c)) for c in range(chunks)]
            + [pl.BlockSpec((rows, 128), spot(c)) for c in range(chunks)],
            out_specs=[
                pl.BlockSpec((rows, depth), lambda k, v, p: (v * groups + (p[0] ^ k), 0)),
                pl.BlockSpec((1, cols, depth), lambda k, v, p: (k >> 1, 0, 0)),
                pl.BlockSpec((1, cols, depth), lambda k, v, p: (k >> 1, 0, 0)),
                pl.BlockSpec((TAIL + 8, depth), lambda k, v, p: (0, 0)),
            ],
            scratch_shapes=[pltpu.VMEM((cols, depth), f32)],
        ),
        out_shape=(
            jax.ShapeDtypeStruct((videos_dev * groups * rows, depth), bf16),
            jax.ShapeDtypeStruct((groups // 2, cols, depth), bf16),
            jax.ShapeDtypeStruct((groups // 2, cols, depth), bf16),
            jax.ShapeDtypeStruct((TAIL + 8, depth), f32),
        ),
        compiler_params=pltpu.CompilerParams(vmem_limit_bytes=VMEM_BYTES),
        cost_estimate=BRIEF,
        name="value_pass",
    )(jnp.full((1,), h, jnp.int32), do_all, wv, ld, *[px_all] * chunks, *[st_all] * chunks)


def kernel_back(
    nf, per_chunk, per_read, scale, videos_dev, final, place, xn, e, st, ld, ow, qw, q, wk, *rest
):
    dqs = rest[:videos_dev]
    dxs = rest[videos_dev : 2 * videos_dev]
    rest = rest[2 * videos_dev :]
    if final:
        g0, side_a, side_b, dq_o, near_o, away_o, pack_o, zs, acc, pack = rest
    else:
        dq_o, near_o, away_o, side_o, zs, acc = rest
    v = pl.program_id(0)
    i = pl.program_id(1)
    tokens = xn.shape[0]
    depth = wk.shape[0]
    heads_rows = GROUP * LATENTS
    total_rows = qw.shape[0]
    groups = total_rows // heads_rows
    cols = GROUP * HEAD_SIZE

    @pl.when((v == 0) & (i == 0))
    def _():
        acc[...] = jnp.zeros_like(acc)

    second = jnp.zeros((1, tokens), f32)
    block = lax.broadcasted_iota(jnp.int32, (heads_rows, 128), 1)
    heads_total = depth // HEAD_SIZE
    base = (place[0] >> 1 if final else (place[0] >> 1) ^ 1) * groups
    for g in range(groups):
        rows = slice(g * heads_rows, (g + 1) * heads_rows)
        spot = lax.rem(i, per_chunk) // per_read
        peak = jnp.sum(jnp.where(block == spot, st[rows, :], 0.0), -1, keepdims=True)
        lse = head_column(ld[...], (base + g) * GROUP)
        delta = head_column(ld[...], (heads_total // GROUP + base + g) * GROUP)
        dp = nt(ow[rows, :], xn[:, :depth])
        expo = e[rows, :].astype(f32)
        prob = expo * jnp.exp(peak - lse)
        z = prob * (dp - delta)
        score = jnp.log(jnp.maximum(expo, 1e-37)) + peak
        second = second + jnp.sum(z * score + prob * dp, 0, keepdims=True)
        zs[rows, :] = z.astype(bf16)
    zs[total_rows:, :] = tail_rows(nf, i, second, xn, depth)
    acc[...] += nn(zs[...], xn[...])

    @pl.when((v == videos_dev - 1) & (i == pl.num_programs(1) - 1))
    def _():
        gain = jnp.zeros((8, depth), f32)
        for k in range(groups):
            g = (place[0] & 1) ^ k
            rows = pl.ds(pl.multiple_of(g * heads_rows, heads_rows), heads_rows)
            wide = pl.ds(pl.multiple_of(g * cols, 128), cols)
            low = acc[rows, :depth].astype(bf16)
            dq_o[k] = collect(nn(low, wk[:, wide])) * scale
            grad = tn(spread(q[:, wide]), low)
            for one, dx in zip(dqs, dxs):
                grad = grad + tn(spread(one[:, wide]), dx[rows, :])
            target = away_o if k & 1 else near_o
            target[...] = (grad * scale).astype(bf16)
        for g in range(groups):
            rows = slice(g * heads_rows, (g + 1) * heads_rows)
            gain = gain + jnp.sum(
                (acc[rows, :depth] * qw[rows, :].astype(f32)).reshape(heads_rows // 8, 8, depth), 0
            )
        pulled = tn(acc[:total_rows, depth:].astype(bf16), qw[...])[:TAIL]
        moved = acc[total_rows:, :depth]
        if final:
            pulled = (pulled + side_a[0:TAIL, :] + side_b[0:TAIL, :]) * g0[...]
            moved = moved + side_a[TAIL : 2 * TAIL, :] + side_b[TAIL : 2 * TAIL, :]
            moved = moved * (1.0 / g0[...])
            gain = gain + side_a[2 * TAIL :, :] + side_b[2 * TAIL :, :]
            mean = jnp.sum(pulled, -1, keepdims=True) * (1.0 / depth)
            pack[0:TAIL, :] = pulled - mean - moved
            pack[TAIL:, :] = gain * (1.0 / g0[...])
            for k in range(pack_o.shape[0]):
                wide = pl.ds(pl.multiple_of((place[0] ^ k) * cols, 128), cols)
                pack_o[(k & 1) * 2 + (k >> 1)] = pack[:, wide]
        else:
            side_o[0:TAIL, :] = pulled
            side_o[TAIL : 2 * TAIL, :] = moved
            side_o[2 * TAIL :, :] = gain


def back_pass(
    far, xn_all, e_all, st_all, ld, ow, qw, q_all, wk, dq_all, dxs, sides, gain, scale, h, videos_dev
):
    depth = wk.shape[0]
    tokens_video = e_all.shape[1]
    frames_dev = tokens_video // PATCH
    cuts, read_nf = chunks_of(frames_dev)
    chunks = len(cuts)
    nf = frames_a_block(read_nf)
    tokens = nf * PATCH
    blocks = frames_dev // nf
    per_chunk = cuts[0] // nf
    rows = qw.shape[0] // 2
    cols = GROUP * HEAD_SIZE
    groups = depth // cols
    packed = TAIL + 8
    final = not far
    one = pl.Buffered(1)

    def y(p):
        return (p[0] >> 1) ^ 1 if far else p[0] >> 1

    outs = [
        jax.ShapeDtypeStruct((2, LATENTS, cols), f32),
        jax.ShapeDtypeStruct((cols, depth), bf16),
        jax.ShapeDtypeStruct((cols, depth), bf16),
    ]
    scratch = [
        pltpu.VMEM((rows + TAIL, tokens), bf16),
        pltpu.VMEM((rows + TAIL, depth + EXTRA), f32),
    ]
    extra = []
    if final:
        extra = [gain, *sides]
        outs.append(jax.ShapeDtypeStruct((groups, packed, cols), f32))
        scratch.append(pltpu.VMEM((packed, depth), f32))
    else:
        outs.append(jax.ShapeDtypeStruct((2 * TAIL + 8, depth), f32))
    return pl.pallas_call(
        functools.partial(
            kernel_back, nf, per_chunk, read_nf // nf, scale, videos_dev, final
        ),
        grid_spec=pltpu.PrefetchScalarGridSpec(
            num_scalar_prefetch=1,
            grid=(videos_dev, blocks),
            in_specs=[
                pl.BlockSpec((tokens, depth + EXTRA), lambda v, i, p: (v * blocks + i, 0)),
                pl.BlockSpec((rows, tokens), lambda v, i, p: (v * 2 + y(p), i)),
                pl.BlockSpec(
                    (rows, 128), lambda v, i, p: ((v * chunks + i // per_chunk) * 2 + y(p), 0)
                ),
                pl.BlockSpec((LATENTS, 128), lambda v, i, p: (v, 0)),
                pl.BlockSpec((rows, depth), lambda v, i, p: (v * 2 + y(p), 0)),
                pl.BlockSpec((rows, depth), lambda v, i, p: (y(p), 0), pipeline_mode=one),
                pl.BlockSpec((LATENTS, 2 * cols), lambda v, i, p: (0, y(p)), pipeline_mode=one),
                pl.BlockSpec((depth, 2 * cols), lambda v, i, p: (0, y(p)), pipeline_mode=one),
            ]
            + [
                pl.BlockSpec((LATENTS, 2 * cols), lambda v, i, p, n=n: (n, y(p)), pipeline_mode=one)
                for n in range(videos_dev)
            ]
            + [
                pl.BlockSpec((rows, depth), lambda v, i, p: (y(p), 0), pipeline_mode=one)
                for _ in dxs
            ]
            + [whole(a.shape) for a in extra],
            out_specs=[whole(a.shape) for a in outs],
            scratch_shapes=scratch,
        ),
        out_shape=outs,
        compiler_params=pltpu.CompilerParams(vmem_limit_bytes=VMEM_BYTES),
        cost_estimate=pl.CostEstimate(
            flops=4 * videos_dev * rows * tokens_video * depth,
            bytes_accessed=videos_dev * tokens_video * depth * 4,
            transcendentals=videos_dev * rows * tokens_video,
        ),
        name="back_far" if far else "back_near",
    )(
        jnp.full((1,), h, jnp.int32), xn_all, e_all, st_all, ld, ow, qw, q_all, wk,
        *[dq_all] * videos_dev, *dxs, *extra,
    )


def halves(x):
    high = x.astype(bf16)
    return high, (x - high.astype(f32)).astype(bf16)


def precise(a, b, dims):
    dims = ((dims[0], dims[1]), ((), ()))
    ah, al = halves(a)
    bh, bl = halves(b)
    out = lax.dot_general(ah, bh, dims, preferred_element_type=f32)
    out = out + lax.dot_general(ah, bl, dims, preferred_element_type=f32)
    return out + lax.dot_general(al, bh, dims, preferred_element_type=f32)


def turn_body(g, left, right, out, total):
    @pl.when(pl.program_id(0) == 0)
    def _():
        total[...] = jnp.zeros_like(total)

    rows, cols = g.shape
    square = g * g
    part = square[:, :128]
    for c in range(1, cols // 128):
        part = part + square[:, c * 128 : (c + 1) * 128]
    total[...] += jnp.sum(part.reshape(rows // 8, 8, 128), 0)
    turned = precise(left[0], g, ((0,), (0,)))
    for c in range(cols // 128):
        wide = slice(c * 128, (c + 1) * 128)
        out[:, wide] = precise(turned[:, wide], right[0, c], ((1,), (0,)))


def kernel_turn(grad, left, right, out, total):
    turn_body(grad[...].astype(f32), left, right, out, total)


def kernel_turn_product(a, b, left, right, out, total):
    frames, _, rows, own = a.shape
    turn_body(tn(a[...].reshape(frames * rows, own), b[...]), left, right, out, total)


def kernel_turn_sum(a, b, c, d, left, right, out, total):
    frames, _, rows, own = a.shape
    grad = tn(a[...].reshape(frames * rows, own), b[...]) + tn(c[...], d[...])
    turn_body(grad, left, right, out, total)


def turn(slab, slot, operands, rows, cols, left, right):
    step = 3 * 128
    if len(operands) == 1:
        body = kernel_turn
        specs = [pl.BlockSpec((rows, step), lambda i: (0, i))]
        arrays = operands
    else:
        a, which, b, first = operands[:4]
        body = kernel_turn_product
        specs = [
            pl.BlockSpec((a.shape[0], 1) + a.shape[2:], lambda i: (0, which, 0, 0)),
            pl.BlockSpec((b.shape[0], step), lambda i: (0, first // step + i)),
        ]
        arrays = [a, b]
        if len(operands) > 4:
            body = kernel_turn_sum
            c, d = operands[4:]
            specs += [
                pl.BlockSpec(c.shape, lambda i: (0, 0)),
                pl.BlockSpec((d.shape[0], step), lambda i: (0, i)),
            ]
            arrays += [c, d]
    return pl.pallas_call(
        body,
        grid=(cols // step,),
        in_specs=specs
        + [
            pl.BlockSpec((1, rows, rows), lambda i: (slab, 0, 0)),
            pl.BlockSpec((1, 3, 128, 128), lambda i: (slot, i, 0, 0)),
        ],
        out_specs=[
            pl.BlockSpec((rows, step), lambda i: (0, i)),
            pl.BlockSpec((8, 128), lambda i: (0, 0)),
        ],
        out_shape=(
            jax.ShapeDtypeStruct((rows, cols), f32),
            jax.ShapeDtypeStruct((8, 128), f32),
        ),
        compiler_params=pltpu.CompilerParams(vmem_limit_bytes=VMEM_BYTES),
        cost_estimate=BRIEF,
        name="turn",
    )(*arrays, left, right)


def kernel_update(rates, factor, weight, one, two, left, right, *rest):
    turned = rest[: len(rates)]
    new_o, one_o, two_o, low_o = rest[len(rates) :]
    slab = pl.program_id(0)
    g = turned[0][...]
    rate = jnp.float32(rates[0])
    for n in range(1, len(rates)):
        g = jnp.where(slab == n, turned[n][...], g)
        rate = jnp.where(slab == n, jnp.float32(rates[n]), rate)
    first, second, step = adam_moments(g * factor[0], one[0], two[0])
    one_o[0] = first
    two_o[0] = second
    cols = step.shape[1]
    back = jnp.concatenate(
        [
            precise(step[:, c * 128 : (c + 1) * 128], right[0, c], ((1,), (1,)))
            for c in range(cols // 128)
        ],
        1,
    )
    back = precise(left[0], back, ((1,), (0,)))
    held = weight[0]
    new = held - rate * (back + 0.01 * held)
    new_o[0] = new
    low_o[0] = new.astype(bf16)


def update(factor, weight, one, two, first_slab, left, right, turned, rates):
    slabs, rows, cols = weight.shape
    step = 6 * 128 if cols % (6 * 128) == 0 else 3 * 128
    tile = pl.BlockSpec((1, rows, step), lambda s, i: (s, 0, i))
    own = [
        pl.BlockSpec((rows, step), lambda s, i, n=n: (0, jnp.where(s == n, i, 0)))
        for n in range(slabs)
    ]
    return pl.pallas_call(
        functools.partial(kernel_update, rates),
        grid=(slabs, cols // step),
        in_specs=[
            pl.BlockSpec(memory_space=pltpu.SMEM),
            tile,
            tile,
            tile,
            pl.BlockSpec((1, rows, rows), lambda s, i: (first_slab + s, 0, 0)),
            pl.BlockSpec((1, step // 128, 128, 128), lambda s, i: (s, i, 0, 0)),
        ]
        + own,
        out_specs=[tile] * 4,
        out_shape=[jax.ShapeDtypeStruct(weight.shape, f32)] * 3
        + [jax.ShapeDtypeStruct(weight.shape, bf16)],
        compiler_params=pltpu.CompilerParams(vmem_limit_bytes=VMEM_BYTES),
        cost_estimate=BRIEF,
        name="update",
    )(factor, weight, one, two, left, right, *turned)


def sum_near(near, away):
    near = near.astype(f32) + swap(away, "head", 1).astype(f32)
    return near[0] + swap(near[1].astype(bf16), "head", 2).astype(f32)


def to_frames(x):
    f = lax.axis_index("frame")
    out = []
    for d in range(x.shape[0]):
        piece = lax.dynamic_index_in_dim(x, f ^ d, 0, False)
        out.append(swap(piece, "frame", d) if d else piece)
    return jnp.stack(out)


def scatter_deep(x):
    mine = lax.axis_index("frame") >> 1
    total = lax.dynamic_index_in_dim(x, mine, 0, False)
    low = x.astype(bf16)
    for d in range(1, x.shape[0]):
        send = lax.dynamic_index_in_dim(low, mine ^ d, 0, False)
        total = total + swap(send, "frame", 2 * d).astype(f32)
    return total


def per_device(
    features, lengths, loss_mask, sq_weight, sq_first, sq_second, ffn_weight, ffn_first,
    ffn_second, left_bases, right_sq, right_ffn, latents, lat_first, lat_second, time_embed,
    time_first, time_second, gains, gain_first, gain_second,
):
    videos, frames_dev, patches, cols = features.shape
    lat_count, depth = latents.shape
    heads_dev = cols // HEAD_SIZE
    head_size = lax.axis_size("head")
    frame_size = lax.axis_size("frame")
    videos_dev = videos // head_size
    rows_dev = sq_weight.shape[1]
    scale = HEAD_SIZE ** (-0.5)
    f = lax.axis_index("frame")
    h = lax.axis_index("head")
    first_frame = (f == 0).astype(f32)
    first_head = (h == 0).astype(f32)
    share = videos_dev * lat_count // frame_size
    tokens_video = frames_dev * patches

    chunks = len(chunks_of(frames_dev)[0])
    feat = features.reshape(videos, tokens_video, cols)

    with jax.named_scope("weights"):
        sq_low = sq_weight.astype(bf16)
        ffn_low = ffn_weight.astype(bf16)
        zhat_zero, zrstd_zero = normalize_rows(latents)
        normed_lat = (zhat_zero * gains[1]).astype(bf16)
        normed_own = lax.dynamic_slice_in_dim(normed_lat, f * rows_dev, rows_dev, 1)
        kv_own = jnp.concatenate([sq_low[1], sq_low[2]], 1)
        kv_far = swap(kv_own, "head", 2)
        low_side = (h & 2) == 0
        kv_rows = jnp.concatenate(
            [jnp.where(low_side, kv_own, kv_far), jnp.where(low_side, kv_far, kv_own)], 1
        )
        away, near = zip(
            *[pick(feat, h, j, c, videos_dev) for j in range(videos_dev) for c in range(chunks)]
        )
        slabs, blocks_dev, bl, _ = left_bases.shape
        left = (
            left_bases[:, :, :, None, :] * jnp.eye(blocks_dev, dtype=f32)[None, :, None, :, None]
        ).reshape(slabs, rows_dev, rows_dev)
        opening = gate(away[0], kv_far)
        query = nn(normed_own, sq_low[0])
        bit = 1
        while bit < frame_size:
            query = query + swap(query, "frame", bit)
            if bit == 1:
                held = sum((zero_of(n) for n in near[1:]), zero_of(opening))
                query = query + held.astype(f32)
            bit *= 2
        query = query.astype(bf16)
        even_core = (h & 1) == 0
        q_all = gather_head(query, 1)
        time_full = gather_head(time_embed, 1)

    with jax.named_scope("exchange"):
        crossed = [swap(opening, "head", 2)]
        waiting = [opening] + [gate(n, crossed[0], q_all, time_full) for n in away[1:2]]

    with jax.named_scope("weights"):
        kv_half = lax.all_gather(kv_rows, "frame", axis=0, tiled=True)
        kv_half = kv_half + (zero_of(waiting[-1]) + zero_of(left)).astype(bf16)
        kv_away = swap(kv_half, "head", 1)
        even = jnp.where(even_core, kv_half, kv_away)
        odd = jnp.where(even_core, kv_away, kv_half)
        w_key, w_value = (
            jnp.concatenate(
                [
                    side[:, at : at + cols]
                    for at in (n * cols, (n + 2) * cols)
                    for side in (even, odd)
                ],
                1,
            )
            for n in (0, 1)
        )
        rest = lax.all_gather(
            after(
                jnp.concatenate([sq_low[0], sq_low[3], sq_low[4], ffn_low[0], ffn_low[1]], 1), kv_half
            ),
            "frame",
            axis=0,
            tiled=True,
        )
        w_query, w_outt, w_dec = (rest[:, n * cols : (n + 1) * cols] for n in range(3))
        hid = ffn_low.shape[2]
        w_up = rest[:, 3 * cols : 3 * cols + hid]
        w_downt = rest[:, 3 * cols + hid :]
        w_key_own = jnp.where(low_side, kv_half[:, :cols], kv_half[:, 2 * cols : 3 * cols])
        w_value_own = jnp.where(low_side, kv_half[:, cols : 2 * cols], kv_half[:, 3 * cols :])

    with jax.named_scope("latent_keys"):
        lat_key = nn(normed_lat, w_key_own).astype(bf16).reshape(lat_count, heads_dev, HEAD_SIZE)
        lat_value = nn(normed_lat, w_value_own).astype(bf16).reshape(lat_count, heads_dev, HEAD_SIZE)
        qw = absorb(q_all, w_key, scale)

    with jax.named_scope("read"):
        own_lens = lax.dynamic_slice_in_dim(lengths, h * videos_dev, videos_dev, 0)
        state = None
        parts = videos_dev * chunks
        token = qw
        for n in range(parts):
            j, c = divmod(n, chunks)
            passed = crossed[n][1] if n < 2 else gate(crossed[n][1], token)
            got = [swap(near[n], "head", 1), crossed[n].reshape(-1, cols), swap(passed, "head", 1)]
            if n + 1 < parts:
                crossed.append(swap(waiting[n + 1], "head", 2))
            if n + 2 < parts and n % 2 == 0:
                waiting.append(gate(away[n + 2], crossed[n + 1], token))
            *state, token = read_pass(
                j, c, state, feat, got, time_full, gains[0:1], own_lens[j], qw, w_value,
                waiting[-1], h, videos_dev,
            )
            if n + 2 < parts and n % 2 == 1:
                waiting.append(gate(away[n + 2], crossed[n + 1], token))
        xn_all, ft_all, e_all, px_all, st_all, o_all = state

    with jax.named_scope("combine"):
        heads = depth // HEAD_SIZE
        lse_parts = (
            (st_all[:, 126] + jnp.log(st_all[:, 127]))
            .reshape(videos_dev, chunks, heads, lat_count)
            .transpose(1, 0, 3, 2)
            .reshape(chunks, videos_dev * lat_count, heads)
        )
        o_parts = o_all.reshape(videos_dev, chunks, lat_count, heads, HEAD_SIZE)
        o_parts = o_parts.transpose(1, 0, 2, 3, 4).reshape(chunks, -1, heads, HEAD_SIZE)
        lse_local = jax.nn.logsumexp(lse_parts, 0)
        o_local = jnp.sum(o_parts * jnp.exp(lse_parts - lse_local)[..., None], 0)
        pay = jnp.concatenate(
            [o_local.reshape(-1, depth).astype(bf16), split_three(lse_local)], 1
        ).reshape(frame_size, share, depth + 3 * heads)
        pay = to_frames(pay)
        lse_each = join_three(pay[..., depth:])
        o_each = pay[..., :depth].astype(f32).reshape(frame_size, share, heads, HEAD_SIZE)
        top = jnp.max(lse_each, 0)
        weight = jnp.exp(lse_each - top)
        total = jnp.sum(weight, 0)
        o_tok = jnp.sum(o_each * weight[..., None], 0) / total[..., None]
        lse_tok = top + jnp.log(total)
        o_heads = o_tok.reshape(share, head_size, cols).transpose(1, 0, 2).astype(bf16)
        l_heads = split_three(lse_tok.reshape(share, head_size, heads_dev).transpose(1, 0, 2))
        pay = lax.all_to_all(jnp.concatenate([o_heads, l_heads], 2), "head", 0, 0, tiled=True)
        lse_tok = join_three(pay[..., cols:])
        o_tok = pay[..., :cols].astype(f32).reshape(head_size, share, heads_dev, HEAD_SIZE)
        first_row = lax.rem(f * share, lat_count)
        q_rows = lax.dynamic_slice_in_dim(query, first_row, share, 0).reshape(
            share, heads_dev, HEAD_SIZE
        )
        lat_scores = (
            jnp.einsum("rnd,jnd->rnj", q_rows, lat_key, preferred_element_type=f32) * scale
        )
        lse = jnp.logaddexp(lse_tok, jax.nn.logsumexp(lat_scores, -1)[None])
        lat_prob = jnp.exp(lat_scores[None] - lse[..., None])
        attn = o_tok * jnp.exp(lse_tok - lse)[..., None] + jnp.einsum(
            "srnj,jnd->srnd", lat_prob, lat_value.astype(f32), precision=HIGH_ACCURACY
        )
        rows = head_size * share
        attn_low = attn.reshape(rows, cols).astype(bf16)

    with jax.named_scope("latent_forward"):
        lat_rows = jnp.tile(lax.dynamic_slice_in_dim(latents, first_row, share, 0), (head_size, 1))
        z_one = lat_rows + sum_head(nt(attn_low, w_outt))
        z1hat, z1rstd = normalize_rows(z_one)
        ffn_in = (z1hat * gains[2]).astype(bf16)
        pre = nn(ffn_in, w_up)
        hidden = jax.nn.gelu(pre).astype(bf16)
        z_two = z_one + sum_head(nt(hidden, w_downt))
        z2hat, z2rstd = normalize_rows(z_two)
        final = (z2hat * gains[3]).astype(bf16)
        dec = jnp.concatenate([nn(final, w_query), nn(final, w_dec)], 1).astype(bf16)

    def to_tokens(x):
        x = lax.all_to_all(x.reshape(head_size, share, -1), "head", 0, 0, tiled=True)
        x = x.transpose(1, 0, 2)
        x = jnp.broadcast_to(x[None], (frame_size,) + x.shape)
        x = lax.all_to_all(x, "frame", 0, 0, tiled=True)
        return x.reshape(videos_dev * lat_count, head_size, -1)

    with jax.named_scope("decode"):
        dec_all = to_tokens(dec)
        dq_all = dec_all[..., :cols].reshape(videos_dev * lat_count, depth)
        dv_all = dec_all[..., cols:].reshape(videos_dev * lat_count, depth)
        own_mask = lax.dynamic_slice_in_dim(loss_mask, h * videos_dev, videos_dev, 0).astype(f32)
        counts = own_mask.reshape(videos_dev * tokens_video, 1)
        decoded = [
            decode_pass(j, xn_all, ft_all, counts, dq_all, dv_all, w_key, scale, videos_dev)
            for j in range(videos_dev)
        ]
        loss_part = sum(jnp.sum(d[4]) for d in decoded)
        count_part = jnp.sum(own_mask)
        dec_side = sum(d[3] for d in decoded)

    with jax.named_scope("latent_backward"):
        ddec = jnp.concatenate(
            [
                jnp.concatenate([d[n] for d in decoded], 0).reshape(frame_size, share, head_size, cols)
                for n in (0, 1)
            ],
            3,
        ).astype(bf16)
        ddec = to_frames(ddec.reshape(frame_size, share, -1)).astype(f32)
        ddec = jnp.sum(ddec, 0).astype(bf16).reshape(share, head_size, 2 * cols).transpose(1, 0, 2)
        ddec = lax.all_to_all(ddec, "head", 0, 0, tiled=True).reshape(rows, 2 * cols)
        ddq_low, ddv_low = (ddec[:, :cols], ddec[:, cols:])
        dfinal = sum_head(nt(ddq_low, w_query) + nt(ddv_low, w_dec))
        dz_two = norm_reverse(dfinal, z2hat, z2rstd, gains[3])
        dz2_low = dz_two.astype(bf16)
        _, gelu_back = jax.vjp(jax.nn.gelu, pre)
        dpre = gelu_back(nn(dz2_low, w_downt))[0].astype(bf16)
        dffn_in = sum_head(nt(dpre, w_up))
        dz_one = dz_two + norm_reverse(dffn_in, z1hat, z1rstd, gains[2])
        dz1_low = dz_one.astype(bf16)
        dattn = nn(dz1_low, w_outt).astype(bf16)
        dattn_heads = dattn.astype(f32).reshape(head_size, share, heads_dev, HEAD_SIZE)
        delta = jnp.sum(dattn_heads * attn, -1)
        pay = jnp.concatenate(
            [
                dattn,
                split_three(lse.reshape(rows, heads_dev)),
                split_three(delta.reshape(rows, heads_dev)),
            ],
            1,
        )
        pay = to_tokens(pay)
        do_all = pay[..., :cols].reshape(videos_dev * lat_count, depth)

        both = join_three(pay[..., cols:].reshape(-1, head_size, 2, 3 * heads_dev))
        both = both.transpose(0, 2, 1, 3).reshape(videos_dev * lat_count, 2 * heads)
        ld = jnp.pad(both, ((0, 0), (0, 128 - 2 * heads)))

    with jax.named_scope("latent_pairs"):
        lat_value_f = lat_value.astype(f32)
        lat_dprob = jnp.einsum("srnd,jnd->srnj", dattn_heads, lat_value_f, precision=HIGH_ACCURACY)
        lat_dscore = lat_prob * (lat_dprob - delta[..., None]) * scale
        dq_lat = jnp.einsum(
            "srnj,jnd->rnd", lat_dscore, lat_key.astype(f32), precision=HIGH_ACCURACY
        ).reshape(share, cols)
        dk_lat = jnp.einsum(
            "srnj,rnd->jnd", lat_dscore, q_rows.astype(f32), precision=HIGH_ACCURACY
        ).reshape(lat_count, cols)
        dv_lat = jnp.einsum(
            "srnj,srnd->jnd", lat_prob, dattn_heads, precision=HIGH_ACCURACY
        ).reshape(lat_count, cols)
        dk_lat_low = dk_lat.astype(bf16)
        dv_lat_low = dv_lat.astype(bf16)
        pairs = jnp.concatenate([dk_lat, dv_lat], 0)
        lat_part = jnp.concatenate(
            [
                jnp.sum(dz_one.reshape(head_size, share, depth), 0),
                jnp.sum(dffn_in * z1hat, 0)[None],
                jnp.sum(dfinal * z2hat, 0)[None],
                jnp.zeros((6, depth), f32),
            ],
            0,
        )
        lat_parts = lax.all_gather(lat_part, "frame")
        lat_direct = jnp.sum(
            lat_parts[:, :share].reshape(videos_dev, lat_count, depth), 0
        )
        gain_rows = jnp.sum(lat_parts[:, share : share + 2], 0)

    with jax.named_scope("row_gradients"):
        wide_a = lax.all_gather(
            jnp.concatenate([hidden, attn_low], 1), "frame", axis=0, tiled=True
        )
        wide_b = lax.all_gather(
            jnp.concatenate([dpre, ddq_low, ddv_low], 1), "frame", axis=0, tiled=True
        )

        own_cols = jnp.stack(
            [a.reshape(rows, frame_size, rows_dev) for a in (ffn_in, final, dz2_low, dz1_low)]
        ).transpose(2, 0, 1, 3)
        own_cols = lax.all_to_all(own_cols, "frame", 0, 0, tiled=True)

    with jax.named_scope("value"):
        ow, dwv_own, dwv_other, value_side = value_pass(do_all, w_value, px_all, st_all, ld, h, videos_dev)
        side = dec_side + jnp.concatenate(
            [value_side[:TAIL], jnp.zeros((TAIL, depth), f32), value_side[TAIL:]], 0
        )

    half = head_size // 2
    back = functools.partial(
        back_pass, e_all=e_all, ld=ld, ow=ow, qw=qw, q_all=q_all, wk=w_key, dq_all=dq_all,
        dxs=[d[2] for d in decoded], scale=scale, h=h, videos_dev=videos_dev,
    )

    with jax.named_scope("value_gradient"):
        dwv = dwv_own.astype(f32) + swap(dwv_other, "head", 1).astype(f32)
        dwv_pay = dwv[1].astype(bf16)
        dwv_far = swap(dwv_pay, "head", 2)

    with jax.named_scope("back"):
        xn_all = gate(xn_all, dwv_pay)
        far_dq, far_near, far_away, far_side = back(
            True, xn_all, st_all=st_all, sides=None, gain=None
        )

    with jax.named_scope("value_gradient"):
        dwv = dwv[0] + dwv_far.astype(f32) + tn(dv_lat_low, normed_lat)
        dwv = dwv.T.reshape(frame_size // 2, 2, rows_dev, cols)
        dwv_away = lax.dynamic_index_in_dim(dwv, 1 - (f & 1), 1, False).astype(bf16)
        dwv_near = lax.dynamic_index_in_dim(dwv, f & 1, 1, False)
        dwv_x = swap(dwv_away, "frame", 1)

    with jax.named_scope("key_gradient"):
        far_sum = far_near.astype(f32) + swap(far_away, "head", 1).astype(f32)
        dq_sum = far_dq[0] + swap(far_dq[1], "head", 1)
        dwk_pay = far_sum.astype(bf16)
        dwk_far = swap(dwk_pay, "head", 2)
        dq_far = swap(dq_sum, "head", 2)

    with jax.named_scope("back"):
        xn_all = gate(xn_all, dwk_pay, dq_sum, dwv_away)
        own_dq, own_near, own_away, pack = back(
            False, xn_all, st_all=st_all, sides=[side, far_side],
            gain=gains[0:1],
        )

    with jax.named_scope("value_gradient"):
        grad_value = scatter_deep(dwv_near + dwv_x.astype(f32))

    with jax.named_scope("key_gradient"):
        key_sum = own_near.astype(f32) + swap(own_away, "head", 1).astype(f32)
        key_sum = key_sum + dwk_far.astype(f32) + tn(dk_lat_low, normed_lat)
        key_sum = key_sum.T.reshape(frame_size // 2, 2, rows_dev, cols)
        key_away = lax.dynamic_index_in_dim(key_sum, 1 - (f & 1), 1, False).astype(bf16)
        key_near = lax.dynamic_index_in_dim(key_sum, f & 1, 1, False)
        key_half = key_near + swap(key_away, "frame", 1).astype(f32)

    with jax.named_scope("patch_gradients"):
        dq_pad = lax.dynamic_update_slice_in_dim(
            jnp.zeros((lat_count, cols), f32), dq_lat, first_row, 0
        )
        dquery = own_dq[0] + swap(own_dq[1], "head", 1) + dq_far + dq_pad
        dquery = jnp.concatenate([dquery + zero_of(key_away).astype(f32), pairs], 0)
        dquery = sum_rounded(dquery, "frame").astype(bf16)
        dquery, dk_sum, dv_sum = (
            dquery[n * lat_count : (n + 1) * lat_count] for n in range(3)
        )

    with jax.named_scope("key_gradient"):
        grad_key = scatter_deep(key_half)

    with jax.named_scope("patch_gradients"):
        pack = sum_near(pack[:half], pack[half:])
        time_own = pack[:frames_dev]
        gain0_own = sum_over(jnp.sum(pack[TAIL:], 0)[None], "frame")[0]
        dzn = sum_head(nt(dquery, w_query) + nt(dk_sum, w_key_own) + nt(dv_sum, w_value_own))
        grad_gain1 = jnp.sum(dzn * zhat_zero, 0)
        lat_grad = lat_direct + norm_reverse(dzn, zhat_zero, zrstd_zero, gains[1])
        gain_rest = jnp.concatenate([grad_gain1[None], gain_rows], 0)
        gain_grad = jnp.concatenate(
            [gain0_own[None], lax.dynamic_slice_in_dim(gain_rest, h * cols, cols, 1)], 0
        )

    with jax.named_scope("update"):
        own_cols = gate(own_cols, key_away)
        sq = functools.partial(turn, rows=rows_dev, cols=cols, left=left, right=right_sq)
        ffn = functools.partial(turn, rows=rows_dev, cols=hid, left=left, right=right_ffn)
        turned, totals = zip(
            sq(0, 0, (own_cols, 1, wide_b, hid, normed_own, dquery)),
            sq(1, 1, (grad_key,)),
            sq(2, 2, (grad_value,)),
            sq(3, 3, (own_cols, 3, wide_a, hid)),
            sq(4, 4, (own_cols, 1, wide_b, hid + cols)),
            ffn(5, 0, (own_cols, 0, wide_b, 0)),
            ffn(6, 1, (own_cols, 2, wide_a, 0)),
        )
        squares = (
            jnp.sum(sum(totals))
            + jnp.sum(time_own * time_own)
            + first_frame * first_head * jnp.sum(lat_grad * lat_grad)
            + first_frame * jnp.sum(gain_grad * gain_grad)
        )
        sums = jnp.pad(jnp.stack([loss_part, count_part, squares])[None], ((0, 7), (0, 125)))
        sums = sum_over(sum_over(sums, "head"), "frame")
        loss_sum, masked_count, squares = (sums[0, 0], sums[0, 1], sums[0, 2])
        grad_norm = jnp.sqrt(squares) / masked_count
        factor = jnp.minimum(1.0, clip_max / grad_norm) / masked_count
        out_rate = ((FRAMES * PATCH + LATENTS) / 64.0) ** 0.5
        ffn_out = update(
            factor[None], ffn_weight, ffn_first, ffn_second, 5, left, right_ffn, turned[5:],
            (0.02, 0.02),
        )
        sq_out = update(
            factor[None], sq_weight, sq_first, sq_second, 0, left, right_sq, turned[:5],
            (0.02, 0.02, 0.02, 0.02 * out_rate, 0.02),
        )
        lat_out = adamw_update(latents, lat_grad * factor, lat_first, lat_second, 0.01)
        time_out = adamw_update(time_embed, time_own * factor, time_first, time_second, 0.01)
        gain_own = lax.dynamic_slice_in_dim(gains, h * cols, cols, 1)
        gain_out = adamw_update(gain_own, gain_grad * factor, gain_first, gain_second, 0.0)
    return (loss_sum, masked_count, grad_norm, *sq_out, *ffn_out, *lat_out, *time_out, *gain_out)


def solution(mesh):
    matrix = P(None, "frame", "head")
    frame_rows = P("frame", "head")
    by_head = P(None, "head")
    placed = (
        P(None, "frame", None, "head"),
        P(None, "frame"),
        P(None, "frame", None),
        matrix, matrix, matrix, matrix, matrix, matrix,
        P(None, "frame", None, None),
        P(None, "head", None, None),
        P(None, "head", None, None),
        P(), P(), P(),
        frame_rows, frame_rows, frame_rows,
        P(), by_head, by_head,
    )
    outs = (
        P(), P(), P(),
        matrix, matrix, matrix, matrix, matrix, matrix, matrix, matrix,
        P(), P(), P(),
        frame_rows, frame_rows, frame_rows,
        by_head, by_head, by_head,
    )
    return jax.shard_map(per_device, mesh=mesh, in_specs=placed, out_specs=outs, check_vma=False)
```

time: 1180 us -> 925 us (0.78)
  blocking collectives: 245 us -> 43.2 us
  local copies, waits for them, and re-layouts: 175 us -> 76.5 us
  Pallas kernels: 293 us -> 372 us
  starting transfers between devices: 43.3 us -> 86.1 us
  matrix products: 73.6 us -> 42.3 us
  other arithmetic: 97.9 us -> 70.2 us
  waiting for transfers between devices: 218 us -> 197 us
    all_gather x2 -> x0, blocking collectives: 208 us -> none  [the longest x1 154 us: per_device(): time_full = lax.all_gather(time_embed, 'head', axis=1, tiled=True)]
    pallas_call x6 -> x31, Pallas kernels: 288 us -> 366 us  [the longest x4 112 us: read_pass(): pl.pallas_call(functools.partial(kernel_read, nf, before), grid_spec=pltp...]
    ppermute x30 -> x74, waiting for transfers between devices: 103 us -> 179 us  [swap(): return lax.ppermute(x, axis, [(i, i ^ bit) for i in range(size)])]
    all_gather x9 -> x5, waiting for transfers between devices: 64.4 us -> 0.08 us  [the longest x1 0.02 us: per_device(): lat_parts = lax.all_gather(lat_part, 'frame')]
    ppermute x30 -> x74, starting transfers between devices: 17.6 us -> 74.9 us  [swap(): return lax.ppermute(x, axis, [(i, i ^ bit) for i in range(size)])]
    reshape x20 -> x12, local copies, waits for them, and re-layouts: 33 us -> 6.53 us  [the longest x8 4.17 us: per_device(): jnp.stack([a.reshape(rows, frame_size, rows_dev) for a in (ffn_in, final,...]
    dot_general x8 -> x0, matrix products: 22.1 us -> none  [the longest x4 13.1 us: rotate(): jnp.einsum('maij,majcl,mckl->maick', left, blocks, right, precision=HIGH_...]
    all_to_all x3 -> x1, waiting for transfers between devices: 20.6 us -> 0.01 us  [per_device(): own_cols = lax.all_to_all(own_cols, 'frame', 0, 0, tiled=True)]
  transfers between devices with their start and end apart: 47 -> 82, of which waited for: 25 -> 37; matrix products, arithmetic and copies ran while one was open for 16% -> 14% of each run, Pallas kernels for 16% -> 28%
where the time goes in v2:
time: 925 us; the launch traced here: 916 us
  Pallas kernels  372 us (40%)
  waiting for transfers between devices  197 us (21%)
  starting transfers between devices  86.1 us (9%)
  local copies, waits for them, and re-layouts  76.5 us (8%)
  other arithmetic  70.2 us (8%)
  blocking collectives  43.2 us (5%)
  matrix products  42.3 us (5%)
  between operations  28.8 us (3%)
    ppermute x74, waiting for transfers between devices, swap(): return lax.ppermute(x, axis, [(i, i ^ bit) for i in range(size)])  179 us
    pallas_call x4, Pallas kernels, read_pass(): pl.pallas_call(functools.partial(kernel_read, nf, before), grid_spec=pltp...  112 us
    pallas_call x2, Pallas kernels, decode_pass(): pl.pallas_call(functools.partial(kernel_decode, nf, scale), grid=(blocks,...  101 us
    pallas_call x2, Pallas kernels, back_pass(): pl.pallas_call(functools.partial(kernel_back, nf, per_chunk, read_nf // n...  76.6 us
    ppermute x74, starting transfers between devices, swap(): return lax.ppermute(x, axis, [(i, i ^ bit) for i in range(size)])  74.9 us
    pallas_call x7, Pallas kernels, turn(): pl.pallas_call(body, grid=(cols // step,), in_specs=specs + [pl.BlockSpec...  25.2 us
    all_to_all x1, blocking collectives, to_tokens(): x = lax.all_to_all(x, 'frame', 0, 0, tiled=True)  23.2 us
    dot_general x8, matrix products, nt(): lax.dot_general(a, b, (((1,), (1,)), ((), ())), preferred_element_type=f32)  19.3 us
  transfers between devices with their start and end apart: 82, of which 37 were waited for; matrix products, arithmetic and copies ran while one was open for 14% of the time, Pallas kernels for 28%

profile of v2, /device:TPU:0, one launch (start us, length us, event | category | flops | bytes accessed | tf_op | source)
XLA Modules:
  0.0 916.1 jit_solution(8409731517500774426)
XLA Ops:
  11.8 7.0 collective-permute-done.1.refs_1_
  63.8 12.7 %collective-permute-done.4 = f32[64,384]{1,0:T(8,128)S(1)} collective-permute-done((f32[64,384]{1,0:T(8,128)S(1)}, f32[64,384]{1,0:T(8,128)S(1)}, u32[]{:S(2)}, u32[]{:S(2)}) %collective-permute-start.4) | collective-permute-done | bytes 98336 | tf_op jit(solution)/shard_map/weights/ppermute | solution.py:69
  77.3 12.7 %collective-permute-done.5 = f32[64,384]{1,0:T(8,128)S(1)} collective-permute-done((f32[64,384]{1,0:T(8,128)S(1)}, f32[64,384]{1,0:T(8,128)S(1)}, u32[]{:S(2)}, u32[]{:S(2)}) %collective-permute-start.5) | collective-permute-done | bytes 98336 | tf_op jit(solution)/shard_map/weights/ppermute | solution.py:69
  90.1 20.1 %collective-permute-done.9 = f32[12,768]{1,0:T(8,128)S(1)} collective-permute-done((f32[12,768]{1,0:T(8,128)S(1)}, f32[12,768]{1,0:T(8,128)S(1)}, u32[]{:S(2)}, u32[]{:S(2)}) %collective-permute-start.9) | collective-permute-done | bytes 36896 | tf_op jit(solution)/shard_map/weights/ppermute | solution.py:69
  124.1 6.6 collective-permute-done.11
  146.8 12.8 %collective-permute-done.10.refs_1_ = bf16[2,1024,384]{2,1,0:T(8,128)(2,1)} collective-permute-done((bf16[2,1024,384]{2,1,0:T(8,128)(2,1)}, bf16[2,1024,384]{2,1,0:T(8,128)(2,1)}, u32[]{:S(2)}, u32[]{:S(2)}) %collective-permute-start.10) | collective-permute-done | bytes 1572896 | tf_op jit(solution)/shard_map/read/ppermute | solution.py:69
  171.4 36.6 %read_pass.4 = (bf16[6144,1664]{1,0:T(8,128)(2,1)}, bf16[6144,1536]{1,0:T(8,128)(2,1)}, bf16[2048,3072]{1,0:T(8,128)(2,1)}, bf16[4096,1664]{1,0:T(8,128)(2,1)}, ...) custom-call(s32[13]{0:T(128)} %pad_add_fusion.2.place, bf16[24576,384]{1,0:T(8,128)(2,1)} %bitcast.301, ...), custom_call_target="tpu_custom_call" | custom-call | flops 1610612736 | bytes 3145728 | tf_op jit(solution)/shard_map/read/read_pass/pallas_call | solution.py:345
  208.0 19.6 %read_pass.5 = (bf16[6144,1664]{1,0:T(8,128)(2,1)}, bf16[6144,1536]{1,0:T(8,128)(2,1)}, bf16[2048,3072]{1,0:T(8,128)(2,1)}, bf16[4096,1664]{1,0:T(8,128)(2,1)}, ...) custom-call(s32[13]{0:T(128)} %pad_add_fusion.2.place, ...), custom_call_target="tpu_custom_call", output_to_operand_aliasing={{0}: (9, {}), {1}: (10, {}), {2}: (11, {}), {3}: (12, {}), ... | custom-call | flops 805306368 | bytes 1572864 | tf_op jit(solution)/shard_map/read/read_pass/pallas_call | solution.py:345
  236.1 36.3 %read_pass.6 = (bf16[6144,1664]{1,0:T(8,128)(2,1)}, bf16[6144,1536]{1,0:T(8,128)(2,1)}, bf16[2048,3072]{1,0:T(8,128)(2,1)}, bf16[4096,1664]{1,0:T(8,128)(2,1)}, ...) custom-call(s32[13]{0:T(128)} %pad_add_fusion.1.place, ...), custom_call_target="tpu_custom_call", output_to_operand_aliasing={{0}: (9, {}), {1}: (10, {}), {2}: (11, {}), {3}: (12, {}), ... | custom-call | flops 1610612736 | bytes 3145728 | tf_op jit(solution)/shard_map/read/read_pass/pallas_call | solution.py:345
  278.5 19.6 %read_pass.7 = (bf16[6144,1664]{1,0:T(8,128)(2,1)}, bf16[6144,1536]{1,0:T(8,128)(2,1)}, bf16[2048,3072]{1,0:T(8,128)(2,1)}, bf16[4096,1664]{1,0:T(8,128)(2,1)}, ...) custom-call(s32[13]{0:T(128)} %pad_add_fusion.1.place, ...), custom_call_target="tpu_custom_call", output_to_operand_aliasing={{0}: (9, {}), {1}: (10, {}), {2}: (11, {}), {3}: (12, {}), ... | custom-call | flops 805306368 | bytes 1572864 | tf_op jit(solution)/shard_map/read/read_pass/pallas_call | solution.py:345
  342.1 5.9 collective-permute-done.29
  358.9 6.7 collective-permute-done.31
  369.9 6.7 all_to_all.35
  387.7 13.7 %all-to-all-done.2 = bf16[8,16,4,768]{3,2,1,0:T(4,128)(2,1)S(1)} async-done(((bf16[8,16,4,768]{3,2,1,0:T(4,128)(2,1)}), bf16[8,16,4,768]{3,2,1,0:T(4,128)(2,1)S(1)}, u32[]{:S(2)}, u32[]{:S(2)}) %all-to-all-start.2) | async-done | bytes 786464 | tf_op jit(solution)/shard_map/decode/all_to_all | solution.py:1123
  403.2 50.4 %decode_pass.2 = (f32[64,1536]{1,0:T(8,128)}, f32[64,1536]{1,0:T(8,128)}, bf16[1024,1536]{1,0:T(8,128)(2,1)}, f32[40,1536]{1,0:T(8,128)}, f32[8,384]{1,0:T(8,128)}) custom-call(bf16[6144,1664]{1,0:T(8,128)(2,1)} %get-tuple-element.127.xn.refs_0_, bf16[6144,1536]{1,0:T(8,128)(2,1)} %get-tuple-element.128.feat, f32[6144,1]{1,0:T(8,128)} %reshape.432.msk, ...), custom_call_target="tpu_custom_call" | custom-call | flops 28991029248 | bytes 18874368 | tf_op jit(solution)/shard_map/decode/decode_pass/pallas_call | solution.py:476
  453.6 50.8 %decode_pass.3 = (f32[64,1536]{1,0:T(8,128)}, f32[64,1536]{1,0:T(8,128)}, bf16[1024,1536]{1,0:T(8,128)(2,1)}, f32[40,1536]{1,0:T(8,128)}, f32[8,384]{1,0:T(8,128)}) custom-call(bf16[6144,1664]{1,0:T(8,128)(2,1)} %get-tuple-element.127.xn.refs_0_, bf16[6144,1536]{1,0:T(8,128)(2,1)} %get-tuple-element.128.feat, f32[6144,1]{1,0:T(8,128)} %reshape.432.msk, ...), custom_call_target="tpu_custom_call" | custom-call | flops 28991029248 | bytes 18874368 | tf_op jit(solution)/shard_map/decode/decode_pass/pallas_call | solution.py:476
  518.2 6.7 collective-permute-done.35
  527.4 6.8 all_to_all.36
  540.0 6.6 collective-permute-done.40
  558.1 6.5 collective-permute-done.42
  569.7 6.5 all_to_all.37
  576.2 23.2 %all_to_all.38 = bf16[8,16,4,408]{3,1,2,0:T(8,128)(2,1)S(1)} all-to-all(bf16[8,16,4,408]{3,1,2,0:T(8,128)(2,1)S(1)} %broadcast_in_dim.33), channel_id=1, replica_groups=mesh['frame'=8,'head'=4] {'frame'}, dimensions={0} | all-to-all | bytes 835584 | tf_op jit(solution)/shard_map/latent_backward/all_to_all | solution.py:1123
  601.2 18.6 %value_pass.1 = (bf16[2048,1536]{1,0:T(8,128)(2,1)}, bf16[2,384,1536]{2,1,0:T(8,128)(2,1)}, bf16[2,384,1536]{2,1,0:T(8,128)(2,1)}, f32[24,1536]{1,0:T(8,128)}) custom-call(s32[1]{0:T(128)} %bitcast.place, bf16[128,1536]{1,0:T(8,128)(2,1)} %bitcast.314, bf16[1536,1536]{1,0:T(8,128)(2,1)} %pad_maximum_fusion.1.wv, f32[128,128]{1,0:T(8,128)} %pad.8.ld, ...), custom_call_target="tpu_custom_call" | custom-call | flops 1 | bytes 1 | tf_op jit(solution)/shard_map/value/value_pass/pallas_call | solution.py:580
  636.4 38.2 %back_far.1 = (f32[2,64,384]{2,1,0:T(8,128)}, bf16[384,1536]{1,0:T(8,128)(2,1)}, bf16[384,1536]{1,0:T(8,128)(2,1)}, f32[40,1536]{1,0:T(8,128)}) custom-call(s32[1]{0:T(128)} %bitcast.place, bf16[6144,1664]{1,0:T(8,128)(2,1)} %gate.15.xn.refs_0_, bf16[2048,3072]{1,0:T(8,128)(2,1)} %get-tuple-element.141.e, f32[4096,128]{1,0:T(8,128)} %get-tuple-element.130.rest_2_.rest_3_.st, ...), custom_call_target="tpu_custom_call" | custom-call | flops 19327352832 | bytes 37748736 | tf_op jit(solution)/shard_map/back/back_far/pallas_call | solution.py:731
  689.9 38.4 %back_near.1 = (f32[2,64,384]{2,1,0:T(8,128)}, bf16[384,1536]{1,0:T(8,128)(2,1)}, bf16[384,1536]{1,0:T(8,128)(2,1)}, f32[4,24,384]{2,1,0:T(8,128)}) custom-call(s32[1]{0:T(128)} %bitcast.place, bf16[6144,1664]{1,0:T(8,128)(2,1)} %gate.16.xn, bf16[2048,3072]{1,0:T(8,128)(2,1)} %get-tuple-element.141.e, f32[4096,128]{1,0:T(8,128)} %get-tuple-element.130.rest_2_.rest_3_.st, ...), custom_call_target="tpu_custom_call" | custom-call | flops 19327352832 | bytes 37748736 | tf_op jit(solution)/shard_map/back/back_near/pallas_call | solution.py:731
  742.1 20.0 %collective-permute-done.66 = f32[1,384]{1,0:T(1,128)S(1)} collective-permute-done((f32[1,384]{1,0:T(1,128)S(1)}, f32[1,384]{1,0:T(1,128)S(1)}, u32[]{:S(2)}, u32[]{:S(2)}) %collective-permute-start.66) | collective-permute-done | bytes 1568 | tf_op jit(solution)/shard_map/patch_gradients/ppermute | solution.py:69
  793.1 10.1 %collective-permute-done.60 = bf16[192,384]{1,0:T(8,128)(2,1)S(1)} collective-permute-done((bf16[192,384]{1,0:T(8,128)(2,1)S(1)}, bf16[192,384]{1,0:T(8,128)(2,1)S(1)}, u32[]{:S(2)}, u32[]{:S(2)}) %collective-permute-start.60) | collective-permute-done | bytes 147488 | tf_op jit(solution)/shard_map/value_gradient/ppermute | solution.py:69
  832.4 6.7 collective-permute-done.56
  839.8 6.0 turn.12
  845.8 6.0 turn.13
  890.2 9.7 %update.3 = (f32[2,192,1536]{2,1,0:T(8,128)}, f32[2,192,1536]{2,1,0:T(8,128)}, f32[2,192,1536]{2,1,0:T(8,128)}, bf16[2,192,1536]{2,1,0:T(8,128)(2,1)}) custom-call(f32[1]{0:T(128)} %bitcast.116.factor, f32[2,192,1536]{2,1,0:T(8,128)} %weight.3, f32[2,192,1536]{2,1,0:T(8,128)} %one.3, f32[2,192,1536]{2,1,0:T(8,128)} %two.3, f32[7,192,192]{2,1,0:T(8,128)} %copy-done.2, ...), custom_call_target="tpu_custom_call" | custom-call | flops 1 | bytes 1 | tf_op jit(solution)/shard_map/update/update/pallas_call | solution.py:901
  899.9 8.1 update.2
  (670 shorter events, 351.0 us)
Async XLA Ops:
  7.2 110.4 %all-gather.7.cloned.1.call-start = ((), (), s32[]{:S(2)}) async-start(), calls=%async_computation.7 | async-start | bytes 5308416 | tf_op jit(solution)/shard_map/weights/all_gather | solution.py:1007
  19.8 317.6 %all-gather.9.cloned.1.call-start = ((), (), s32[]{:S(2)}) async-start(), calls=%async_computation.8 | async-start | bytes 14598144 | tf_op jit(solution)/shard_map/weights/all_gather | solution.py:1023
  23.8 37.4 %collective-permute-start.3 = (f32[64,384]{1,0:T(8,128)}, f32[64,384]{1,0:T(8,128)}, u32[]{:S(2)}, u32[]{:S(2)}) collective-permute-start(f32[64,384]{1,0:T(8,128)} %fusion.53), channel_id=1, source_target_pairs={{0,4},{4,0},{8,12},{12,8},{16,20},{20,16},{24,28},{28,24},{1,5},{5... | collective-permute-start | bytes 294920 | tf_op jit(solution)/shard_map/weights/ppermute | solution.py:69
  25.5 38.3 %collective-permute-start.8 = (f32[12,384]{1,0:T(8,128)S(1)}, f32[12,384]{1,0:T(8,128)S(1)}, u32[]{:S(2)}, u32[]{:S(2)}) collective-permute-start(f32[12,384]{1,0:T(8,128)S(1)} %copy-done.75), channel_id=1, source_target_pairs={{0,1},{1,0},{2,3},{3,2},{4,5},{5,4},{6,7},{7,6},{8,9},{9,8},{10,11... | collective-permute-start | bytes 55304 | tf_op jit(solution)/shard_map/weights/ppermute | solution.py:69
  38.5 77.2 %collective-permute-start.2 = (bf16[2,2048,384]{2,1,0:T(8,128)(2,1)}, bf16[2,2048,384]{2,1,0:T(8,128)(2,1)}, u32[]{:S(2)}, u32[]{:S(2)}) collective-permute-start(bf16[2,2048,384]{2,1,0:T(8,128)(2,1)} %gate.9), channel_id=1, source_target_pairs={{0,2},{1,3},{2,0},{3,1},{4,6},{5,7},{6,4},{7,5},{8,10},{9,11},{10,... | collective-permute-start | bytes 9437192 | tf_op jit(solution)/shard_map/exchange/ppermute | solution.py:69
  76.6 33.6 %collective-permute-start.9 = (f32[12,768]{1,0:T(8,128)S(1)}, f32[12,768]{1,0:T(8,128)S(1)}, u32[]{:S(2)}, u32[]{:S(2)}) collective-permute-start(f32[12,768]{1,0:T(8,128)S(1)} %pad_maximum_fusion.14), channel_id=1, source_target_pairs={{0,2},{1,3},{2,0},{3,1},{4,6},{5,7},{6,4},{7,5},{8,10},{9,11},{10,... | collective-permute-start | bytes 110600 | tf_op jit(solution)/shard_map/weights/ppermute | solution.py:69
  90.1 20.2 %collective-permute-start.6 = (bf16[64,384]{1,0:T(8,128)(2,1)S(1)}, bf16[64,384]{1,0:T(8,128)(2,1)S(1)}, u32[]{:S(2)}, u32[]{:S(2)}) collective-permute-start(bf16[64,384]{1,0:T(8,128)(2,1)S(1)} %add_convert_fusion.2), channel_id=1, source_target_pairs={{0,1},{1,0},{2,3},{3,2},{4,5},{5,4},{6,7},{7,6},{8,9},{9,8},{10,11... | collective-permute-start | bytes 147464 | tf_op jit(solution)/shard_map/weights/ppermute | solution.py:69
  122.5 37.1 %collective-permute-start.10 = (bf16[2,1024,384]{2,1,0:T(8,128)(2,1)}, bf16[2,1024,384]{2,1,0:T(8,128)(2,1)}, u32[]{:S(2)}, u32[]{:S(2)}) collective-permute-start(bf16[2,1024,384]{2,1,0:T(8,128)(2,1)} %gate.10), channel_id=1, source_target_pairs={{0,2},{1,3},{2,0},{3,1},{4,6},{5,7},{6,4},{7,5},{8,10},{9,11},{10,... | collective-permute-start | bytes 4718600 | tf_op jit(solution)/shard_map/read/ppermute | solution.py:69
  159.6 70.0 %collective-permute-start.12 = (bf16[2,2048,384]{2,1,0:T(8,128)(2,1)}, bf16[2,2048,384]{2,1,0:T(8,128)(2,1)}, u32[]{:S(2)}, u32[]{:S(2)}) collective-permute-start(bf16[2,2048,384]{2,1,0:T(8,128)(2,1)} %gate.11.dep), channel_id=1, source_target_pairs={{0,2},{1,3},{2,0},{3,1},{4,6},{5,7},{6,4},{7,5},{8,10},{9,11},{10,... | collective-permute-start | bytes 9437192 | tf_op jit(solution)/shard_map/read/ppermute | solution.py:69
  164.4 43.6 %collective-permute-start.13 = (bf16[1024,384]{1,0:T(8,128)(2,1)}, bf16[1024,384]{1,0:T(8,128)(2,1)}, u32[]{:S(2)}, u32[]{:S(2)}) collective-permute-start(bf16[1024,384]{1,0:T(8,128)(2,1)} %get-tuple-element.104), channel_id=1, source_target_pairs={{0,1},{1,0},{2,3},{3,2},{4,5},{5,4},{6,7},{7,6},{8,9},{9,8},{10,11... | collective-permute-start | bytes 2359304 | tf_op jit(solution)/shard_map/read/ppermute | solution.py:69
  167.3 40.7 %collective-permute-start.14 = (bf16[1024,384]{1,0:T(8,128)(2,1)}, bf16[1024,384]{1,0:T(8,128)(2,1)}, u32[]{:S(2)}, u32[]{:S(2)}) collective-permute-start(bf16[1024,384]{1,0:T(8,128)(2,1)} %slice_bitcast_fusion.4), channel_id=1, source_target_pairs={{0,1},{1,0},{2,3},{3,2},{4,5},{5,4},{6,7},{7,6},{8,9},{9,8},{10,11... | collective-permute-start | bytes 2359304 | tf_op jit(solution)/shard_map/read/ppermute | solution.py:69
  170.0 65.4 %collective-permute-start.18 = (bf16[2048,384]{1,0:T(8,128)(2,1)}, bf16[2048,384]{1,0:T(8,128)(2,1)}, u32[]{:S(2)}, u32[]{:S(2)}) collective-permute-start(bf16[2048,384]{1,0:T(8,128)(2,1)} %get-tuple-element.105), channel_id=1, source_target_pairs={{0,1},{1,0},{2,3},{3,2},{4,5},{5,4},{6,7},{7,6},{8,9},{9,8},{10,11... | collective-permute-start | bytes 4718600 | tf_op jit(solution)/shard_map/read/ppermute | solution.py:69
  232.3 40.0 %collective-permute-start.17 = (bf16[2,1024,384]{2,1,0:T(8,128)(2,1)}, bf16[2,1024,384]{2,1,0:T(8,128)(2,1)S(1)}, u32[]{:S(2)}, u32[]{:S(2)}) collective-permute-start(bf16[2,1024,384]{2,1,0:T(8,128)(2,1)} %gate.12.dep), channel_id=1, source_target_pairs={{0,2},{1,3},{2,0},{3,1},{4,6},{5,7},{6,4},{7,5},{8,10},{9,11},{10,... | collective-permute-start | bytes 4718600 | tf_op jit(solution)/shard_map/read/ppermute | solution.py:69
  233.8 44.7 %collective-permute-start = (bf16[1024,384]{1,0:T(8,128)(2,1)}, bf16[1024,384]{1,0:T(8,128)(2,1)}, u32[]{:S(2)}, u32[]{:S(2)}) collective-permute-start(bf16[1024,384]{1,0:T(8,128)(2,1)} %get-tuple-element.99), channel_id=1, source_target_pairs={{0,1},{1,0},{2,3},{3,2},{4,5},{5,4},{6,7},{7,6},{8,9},{9,8},{10,11... | collective-permute-start | bytes 2359304 | tf_op jit(solution)/shard_map/read/ppermute | solution.py:69
  377.7 23.7 %all-to-all-start.2 = ((bf16[8,16,4,768]{3,2,1,0:T(4,128)(2,1)}), bf16[8,16,4,768]{3,2,1,0:T(4,128)(2,1)S(1)}, u32[]{:S(2)}, u32[]{:S(2)}) async-start(bf16[8,16,4,768]{3,2,1,0:T(4,128)(2,1)} %broadcast_in_dim.32), calls=%async_computation.2 | async-start | bytes 1572864 | tf_op jit(solution)/shard_map/decode/all_to_all | solution.py:1123
  381.3 353.4 %all-gather.15.cloned.1.call-start = ((), (), s32[]{:S(2)}) async-start(), calls=%async_computation.11 | async-start | bytes 1327104 | tf_op jit(solution)/shard_map/latent_pairs/all_gather | solution.py:1203
  510.5 14.4 %collective-permute-start.35 = (bf16[16,3072]{1,0:T(8,128)(2,1)S(1)}, bf16[16,3072]{1,0:T(8,128)(2,1)S(1)}, u32[]{:S(2)}, u32[]{:S(2)}) collective-permute-start(bf16[16,3072]{1,0:T(8,128)(2,1)S(1)} %get-tuple-element.232), channel_id=1, source_target_pairs={{0,16},{4,20},{8,24},{12,28},{16,0},{20,4},{24,8},{28,12},{1,17},{... | collective-permute-start | bytes 294920 | tf_op jit(solution)/shard_map/latent_backward/ppermute | solution.py:69
  510.5 16.7 %collective-permute-start.36 = (bf16[16,3072]{1,0:T(8,128)(2,1)S(1)}, bf16[16,3072]{1,0:T(8,128)(2,1)S(1)}, u32[]{:S(2)}, u32[]{:S(2)}) collective-permute-start(bf16[16,3072]{1,0:T(8,128)(2,1)S(1)} %get-tuple-element.231), channel_id=1, source_target_pairs={{0,20},{4,16},{8,28},{12,24},{16,4},{20,0},{24,12},{28,8},{1,21},{... | collective-permute-start | bytes 294920 | tf_op jit(solution)/shard_map/latent_backward/ppermute | solution.py:69
  565.9 241.9 %all-gather.13.cloned.1.call-start = ((), (), s32[]{:S(2)}) async-start(), calls=%async_computation.10 | async-start | bytes 2211840 | tf_op jit(solution)/shard_map/row_gradients/all_gather | solution.py:1210
  566.7 243.8 %all-gather.11.cloned.1.call-start = ((), (), s32[]{:S(2)}) async-start(), calls=%async_computation.9 | async-start | bytes 2654208 | tf_op jit(solution)/shard_map/row_gradients/all_gather | solution.py:1213
  635.4 43.1 %collective-permute-start.46 = (bf16[384,1536]{1,0:T(8,128)(2,1)S(1)}, bf16[384,1536]{1,0:T(8,128)(2,1)}, u32[]{:S(2)}, u32[]{:S(2)}) collective-permute-start(bf16[384,1536]{1,0:T(8,128)(2,1)S(1)} %fusion.12.refs_1_), channel_id=1, source_target_pairs={{0,2},{1,3},{2,0},{3,1},{4,6},{5,7},{6,4},{7,5},{8,10},{9,11},{10,... | collective-permute-start | bytes 3538952 | tf_op jit(solution)/shard_map/value_gradient/ppermute | solution.py:69
  730.7 76.2 %all-to-all-start.4 = ((bf16[8,4,64,192]{3,2,1,0:T(8,128)(2,1)}), bf16[8,4,64,192]{3,2,1,0:T(8,128)(2,1)S(1)}, u32[]{:S(2)}, u32[]{:S(2)}) async-start(bf16[8,4,64,192]{3,2,1,0:T(8,128)(2,1)} %maximum_bitcast_fusion), calls=%async_computation.4 | async-start | bytes 2097152 | tf_op jit(solution)/shard_map/row_gradients/all_to_all | solution.py:1220
  737.9 24.2 %collective-permute-start.50 = (f32[64,384]{1,0:T(8,128)S(1)}, f32[64,384]{1,0:T(8,128)S(1)}, u32[]{:S(2)}, u32[]{:S(2)}) collective-permute-start(f32[64,384]{1,0:T(8,128)S(1)} %copy-done.48), channel_id=1, source_target_pairs={{0,2},{1,3},{2,0},{3,1},{4,6},{5,7},{6,4},{7,5},{8,10},{9,11},{10,... | collective-permute-start | bytes 294920 | tf_op jit(solution)/shard_map/key_gradient/ppermute | solution.py:69
  739.0 29.0 %collective-permute-start.48 = (bf16[384,1536]{1,0:T(8,128)(2,1)S(1)}, bf16[384,1536]{1,0:T(8,128)(2,1)S(1)}, u32[]{:S(2)}, u32[]{:S(2)}) collective-permute-start(bf16[384,1536]{1,0:T(8,128)(2,1)S(1)} %copy-done.16), channel_id=1, source_target_pairs={{0,2},{1,3},{2,0},{3,1},{4,6},{5,7},{6,4},{7,5},{8,10},{9,11},{10,... | collective-permute-start | bytes 3538952 | tf_op jit(solution)/shard_map/key_gradient/ppermute | solution.py:69
  740.0 44.7 %collective-permute-start.58 = (bf16[4,192,384]{2,1,0:T(8,128)(2,1)}, bf16[4,192,384]{2,1,0:T(8,128)(2,1)}, u32[]{:S(2)}, u32[]{:S(2)}) collective-permute-start(bf16[4,192,384]{2,1,0:T(8,128)(2,1)} %fusion.23.refs_3_), channel_id=1, source_target_pairs={{0,4},{4,0},{8,12},{12,8},{16,20},{20,16},{24,28},{28,24},{1,5},{5... | collective-permute-start | bytes 1769480 | tf_op jit(solution)/shard_map/value_gradient/ppermute | solution.py:69
  741.9 21.5 %collective-permute-start.47 = (bf16[384,1536]{1,0:T(8,128)(2,1)}, bf16[384,1536]{1,0:T(8,128)(2,1)S(1)}, u32[]{:S(2)}, u32[]{:S(2)}) collective-permute-start(bf16[384,1536]{1,0:T(8,128)(2,1)} %get-tuple-element.153), channel_id=1, source_target_pairs={{0,1},{1,0},{2,3},{3,2},{4,5},{5,4},{6,7},{7,6},{8,9},{9,8},{10,11... | collective-permute-start | bytes 3538952 | tf_op jit(solution)/shard_map/key_gradient/ppermute | solution.py:69
  742.0 20.1 %collective-permute-start.66 = (f32[1,384]{1,0:T(1,128)S(1)}, f32[1,384]{1,0:T(1,128)S(1)}, u32[]{:S(2)}, u32[]{:S(2)}) collective-permute-start(f32[1,384]{1,0:T(1,128)S(1)} %broadcast_in_dim.38), channel_id=1, source_target_pairs={{0,4},{4,0},{8,12},{12,8},{16,20},{20,16},{24,28},{28,24},{1,5},{5... | collective-permute-start | bytes 4616 | tf_op jit(solution)/shard_map/patch_gradients/ppermute | solution.py:69
  762.1 16.4 %collective-permute-start.67 = (f32[1,384]{1,0:T(1,128)S(1)}, f32[1,384]{1,0:T(1,128)S(1)}, u32[]{:S(2)}, u32[]{:S(2)}) collective-permute-start(f32[1,384]{1,0:T(1,128)S(1)} %reshape_add_fusion), channel_id=1, source_target_pairs={{0,8},{4,12},{8,0},{12,4},{16,24},{20,28},{24,16},{28,20},{1,9},{5... | collective-permute-start | bytes 4616 | tf_op jit(solution)/shard_map/patch_gradients/ppermute | solution.py:69
  786.6 16.6 %collective-permute-start.60 = (bf16[192,384]{1,0:T(8,128)(2,1)S(1)}, bf16[192,384]{1,0:T(8,128)(2,1)S(1)}, u32[]{:S(2)}, u32[]{:S(2)}) collective-permute-start(bf16[192,384]{1,0:T(8,128)(2,1)S(1)} %get-tuple-element.244), channel_id=1, source_target_pairs={{0,16},{4,20},{8,24},{12,28},{16,0},{20,4},{24,8},{28,12},{1,17},{... | collective-permute-start | bytes 442376 | tf_op jit(solution)/shard_map/value_gradient/ppermute | solution.py:69
  791.3 22.0 %collective-permute-start.53 = (bf16[192,384]{1,0:T(8,128)(2,1)}, bf16[192,384]{1,0:T(8,128)(2,1)}, u32[]{:S(2)}, u32[]{:S(2)}) collective-permute-start(bf16[192,384]{1,0:T(8,128)(2,1)} %fusion.42), channel_id=1, source_target_pairs={{0,16},{4,20},{8,24},{12,28},{16,0},{20,4},{24,8},{28,12},{1,17},{... | collective-permute-start | bytes 442376 | tf_op jit(solution)/shard_map/patch_gradients/ppermute | solution.py:69
  806.4 14.9 %collective-permute-start.54 = (bf16[4,192,384]{2,1,0:T(8,128)(2,1)S(1)}, bf16[4,192,384]{2,1,0:T(8,128)(2,1)}, u32[]{:S(2)}, u32[]{:S(2)}) collective-permute-start(bf16[4,192,384]{2,1,0:T(8,128)(2,1)S(1)} %fusion.24.refs_1_), channel_id=1, source_target_pairs={{0,4},{4,0},{8,12},{12,8},{16,20},{20,16},{24,28},{28,24},{1,5},{5... | collective-permute-start | bytes 1769480 | tf_op jit(solution)/shard_map/key_gradient/ppermute | solution.py:69
  829.3 30.7 %collective-permute-start.65 = (bf16[64,1536]{1,0:T(8,128)(2,1)}, bf16[64,1536]{1,0:T(8,128)(2,1)}, u32[]{:S(2)}, u32[]{:S(2)}) collective-permute-start(bf16[64,1536]{1,0:T(8,128)(2,1)} %fusion.48), channel_id=1, source_target_pairs={{0,2},{1,3},{2,0},{3,1},{4,6},{5,7},{6,4},{7,5},{8,10},{9,11},{10,... | collective-permute-start | bytes 589832 | tf_op jit(solution)/shard_map/patch_gradients/ppermute | solution.py:69
  (146 other events, 1751.8 us)
Sparse Core Ops, SparseCore 0:
  20.0 83.3 all-gather.6
  122.5 181.5 all-gather.8
  566.0 43.1 all-gather.14
  611.2 46.2 all-gather.12
  660.2 51.1 all-gather.10

commit v3 on v2

--- a/solution.py
+++ b/solution.py
@@ -242,10 +242,10 @@
 
 
 def kernel_read(
-    nf, first, place, own, ra, rb, rc, time_ref, g0, qw, wv, xn_in, ft_in, e_in, px_in, st_in, o_in, dep,
+    nf, first, carry, final, place, own, ra, rb, rc, time_ref, g0, qw, wv, xn_in, ft_in, e_in, px_in, st_in, o_in, dep,
     xn_o, ft_o, e_o, px_o, st_o, o_o, token_o, xs, acc, run,
 ):
-    del xn_in, ft_in, e_in, px_in, st_in, o_in, dep
+    del xn_in, ft_in, e_in, o_in, dep
     i = pl.program_id(0)
     tokens, depth = xs.shape
     cols = own.shape[1]
@@ -254,10 +254,16 @@
 
     @pl.when(i == 0)
     def _():
-        acc[...] = jnp.zeros_like(acc)
-        run[0] = jnp.full(run.shape[1:], -1e30, f32)
-        run[1] = jnp.zeros(run.shape[1:], f32)
-        st_o[...] = jnp.zeros_like(st_o)
+        if carry:
+            acc[...] = px_in[...].astype(f32)
+            run[0] = jnp.broadcast_to(st_in[:, 126:127], run.shape[1:])
+            run[1] = jnp.broadcast_to(st_in[:, 127:128], run.shape[1:])
+            st_o[...] = st_in[...]
+        else:
+            acc[...] = jnp.zeros_like(acc)
+            run[0] = jnp.full(run.shape[1:], -1e30, f32)
+            run[1] = jnp.zeros(run.shape[1:], f32)
+            st_o[...] = jnp.zeros_like(st_o)
 
     for k, part in enumerate((own, ra, rb, rc)):
         off = pl.multiple_of((place[0] ^ k) * cols, 128)
@@ -294,7 +300,7 @@
         run[1, rows, :] = total
         low = expo.astype(bf16)
         e_o[rows, :] = low
-        stats = jnp.where(block == i, new, st_o[rows, :])
+        stats = jnp.where(block == first // nf + i, new, st_o[rows, :])
         stats = jnp.where(last & (block == 126), new, stats)
         st_o[rows, :] = jnp.where(last & (block == 127), total, stats)
         acc[rows, :] = acc[rows, :] * shrink[:, :1] + nn(low, xn_o[...])
@@ -306,8 +312,11 @@
             wide = slice(g * cols, (g + 1) * cols)
             held = acc[rows, :].astype(bf16)
             px_o[rows, :] = held
-            mixed = nn(held[:, :depth], wv[:, wide]) * (1.0 / run[1, rows, :1])
-            o_o[:, wide] = collect(mixed)
+            if final:
+                mixed = nn(held[:, :depth], wv[:, wide]) * (1.0 / run[1, rows, :1])
+                o_o[:, wide] = collect(mixed)
+        if not final:
+            o_o[...] = jnp.zeros_like(o_o)
         token_o[...] = run[1, 0:8, :]
 
 
@@ -323,17 +332,15 @@
     blocks = frames // nf
     start = (j * frames_dev + before) // nf
     rows = qw.shape[0]
-    part = j * chunks + c
-    parts = videos_dev * chunks
     place = jnp.concatenate([h[None], lens]).astype(jnp.int32)
     feat2 = feat.reshape(count * tokens_video, cols)
     shapes = (
         jax.ShapeDtypeStruct((videos_dev * tokens_video, depth + EXTRA), bf16),
         jax.ShapeDtypeStruct((videos_dev * tokens_video, depth), bf16),
         jax.ShapeDtypeStruct((videos_dev * rows, tokens_video), bf16),
-        jax.ShapeDtypeStruct((parts * rows, depth + EXTRA), bf16),
-        jax.ShapeDtypeStruct((parts * rows, 128), f32),
-        jax.ShapeDtypeStruct((parts * LATENTS, depth), f32),
+        jax.ShapeDtypeStruct((videos_dev * rows, depth + EXTRA), bf16),
+        jax.ShapeDtypeStruct((videos_dev * rows, 128), f32),
+        jax.ShapeDtypeStruct((videos_dev * LATENTS, depth), f32),
     )
     aliases = {}
     if prev is None:
@@ -343,7 +350,7 @@
     anyspec = pl.BlockSpec(memory_space=pl.ANY)
     one = pl.Buffered(1)
     return pl.pallas_call(
-        functools.partial(kernel_read, nf, before),
+        functools.partial(kernel_read, nf, before, c > 0, c == chunks - 1),
         grid_spec=pltpu.PrefetchScalarGridSpec(
             num_scalar_prefetch=1,
             grid=(blocks,),
@@ -360,14 +367,23 @@
                 whole(qw.shape),
                 whole(wv.shape),
             ]
-            + [anyspec] * 7,
+            + [anyspec] * 3
+            + (
+                [
+                    pl.BlockSpec((rows, depth + EXTRA), lambda i, p: (j, 0), pipeline_mode=one),
+                    pl.BlockSpec((rows, 128), lambda i, p: (j, 0), pipeline_mode=one),
+                ]
+                if c
+                else [anyspec] * 2
+            )
+            + [anyspec] * 2,
             out_specs=[
                 pl.BlockSpec((tokens, depth + EXTRA), lambda i, p: (start + i, 0)),
                 pl.BlockSpec((tokens, depth), lambda i, p: (start + i, 0)),
                 pl.BlockSpec((rows, tokens), lambda i, p: (j, before // nf + i)),
-                pl.BlockSpec((rows, depth + EXTRA), lambda i, p: (part, 0), pipeline_mode=one),
-                pl.BlockSpec((rows, 128), lambda i, p: (part, 0), pipeline_mode=one),
-                pl.BlockSpec((LATENTS, depth), lambda i, p: (part, 0), pipeline_mode=one),
+                pl.BlockSpec((rows, depth + EXTRA), lambda i, p: (j, 0), pipeline_mode=one),
+                pl.BlockSpec((rows, 128), lambda i, p: (j, 0), pipeline_mode=one),
+                pl.BlockSpec((LATENTS, depth), lambda i, p: (j, 0), pipeline_mode=one),
                 whole((8, 128)),
             ],
             scratch_shapes=[
@@ -392,7 +408,7 @@
     nf, scale, xn, feat, msk, dq, dv, wk,
     ddq_o, ddv_o, dx_o, side_o, loss_o, dqw, dvd, sc, zs, acc, dacc, loss,
 ):
-    i = pl.program_id(0)
+    i = pl.program_id(1)
     tokens = xn.shape[0]
     depth = wk.shape[0]
     heads_rows = GROUP * LATENTS
@@ -433,7 +449,7 @@
     zs[total_rows:, :] = tail_rows(nf, i, second, xn, depth)
     acc[...] += nn(zs[...], xn[...])
 
-    @pl.when(i == pl.num_programs(0) - 1)
+    @pl.when(i == pl.num_programs(1) - 1)
     def _():
         gain = jnp.zeros((8, depth), f32)
         for g in range(groups):
@@ -447,10 +463,10 @@
             gain = gain + jnp.sum(
                 (held * dqw[rows, :].astype(f32)).reshape(heads_rows // 8, 8, depth), 0
             )
-        side_o[0:TAIL, :] = tn(acc[:total_rows, depth:].astype(bf16), dqw[...])[:TAIL]
-        side_o[TAIL : 2 * TAIL, :] = acc[total_rows:, :depth]
-        side_o[2 * TAIL :, :] = gain
-        loss_o[...] = loss[...]
+        side_o[0, 0:TAIL, :] = tn(acc[:total_rows, depth:].astype(bf16), dqw[...])[:TAIL]
+        side_o[0, TAIL : 2 * TAIL, :] = acc[total_rows:, :depth]
+        side_o[0, 2 * TAIL :, :] = gain
+        loss_o[0] = loss[...]
 
 
 def tail_rows(nf, i, second, xn, depth):
@@ -461,7 +477,7 @@
     return jnp.where(row == frame, rstd * second * (1.0 / depth), 0.0).astype(bf16)
 
 
-def decode_pass(j, xn_all, ft_all, counts, dq_all, dv_all, wk, scale, videos_dev):
+def decode_pass(xn_all, ft_all, counts, dq_all, dv_all, wk, scale, videos_dev):
     depth = wk.shape[0]
     tokens_video = xn_all.shape[0] // videos_dev
     cols = GROUP * HEAD_SIZE
@@ -475,21 +491,21 @@
     one = pl.Buffered(1)
     return pl.pallas_call(
         functools.partial(kernel_decode, nf, scale),
-        grid=(blocks,),
+        grid=(videos_dev, blocks),
         in_specs=[
-            pl.BlockSpec((tokens, depth + EXTRA), lambda i: (j * blocks + i, 0)),
-            pl.BlockSpec((tokens, depth), lambda i: (j * blocks + i, 0)),
-            pl.BlockSpec((tokens, 1), lambda i: (j * blocks + i, 0)),
-            pl.BlockSpec((LATENTS, depth), lambda i: (j, 0), pipeline_mode=one),
-            pl.BlockSpec((LATENTS, depth), lambda i: (j, 0), pipeline_mode=one),
+            pl.BlockSpec((tokens, depth + EXTRA), lambda j, i: (j * blocks + i, 0)),
+            pl.BlockSpec((tokens, depth), lambda j, i: (j * blocks + i, 0)),
+            pl.BlockSpec((tokens, 1), lambda j, i: (j * blocks + i, 0)),
+            pl.BlockSpec((LATENTS, depth), lambda j, i: (j, 0), pipeline_mode=one),
+            pl.BlockSpec((LATENTS, depth), lambda j, i: (j, 0), pipeline_mode=one),
             whole(wk.shape),
         ],
         out_specs=[
-            whole((LATENTS, depth)),
-            whole((LATENTS, depth)),
-            whole((rows, depth)),
-            whole((2 * TAIL + 8, depth)),
-            whole((8, cols)),
+            pl.BlockSpec((LATENTS, depth), lambda j, i: (j, 0), pipeline_mode=one),
+            pl.BlockSpec((LATENTS, depth), lambda j, i: (j, 0), pipeline_mode=one),
+            pl.BlockSpec((rows, depth), lambda j, i: (j, 0), pipeline_mode=one),
+            pl.BlockSpec((1, 2 * TAIL + 8, depth), lambda j, i: (j, 0, 0), pipeline_mode=one),
+            pl.BlockSpec((1, 8, cols), lambda j, i: (j, 0, 0), pipeline_mode=one),
         ],
         scratch_shapes=[
             pltpu.VMEM((rows, depth), bf16),
@@ -501,11 +517,11 @@
             pltpu.VMEM((8, cols), f32),
         ],
         out_shape=(
-            jax.ShapeDtypeStruct((LATENTS, depth), f32),
-            jax.ShapeDtypeStruct((LATENTS, depth), f32),
-            jax.ShapeDtypeStruct((rows, depth), bf16),
-            jax.ShapeDtypeStruct((2 * TAIL + 8, depth), f32),
-            jax.ShapeDtypeStruct((8, cols), f32),
+            jax.ShapeDtypeStruct((videos_dev * LATENTS, depth), f32),
+            jax.ShapeDtypeStruct((videos_dev * LATENTS, depth), f32),
+            jax.ShapeDtypeStruct((videos_dev * rows, depth), bf16),
+            jax.ShapeDtypeStruct((videos_dev, 2 * TAIL + 8, depth), f32),
+            jax.ShapeDtypeStruct((videos_dev, 8, cols), f32),
         ),
         compiler_params=pltpu.CompilerParams(vmem_limit_bytes=VMEM_BYTES),
         cost_estimate=pl.CostEstimate(
@@ -610,7 +626,7 @@
 
 
 def kernel_back(
-    nf, per_chunk, per_read, scale, videos_dev, final, place, xn, e, st, ld, ow, qw, q, wk, *rest
+    nf, per_read, scale, videos_dev, final, place, xn, e, st, ld, ow, qw, q, wk, *rest
 ):
     dqs = rest[:videos_dev]
     dxs = rest[videos_dev : 2 * videos_dev]
@@ -638,7 +654,7 @@
     base = (place[0] >> 1 if final else (place[0] >> 1) ^ 1) * groups
     for g in range(groups):
         rows = slice(g * heads_rows, (g + 1) * heads_rows)
-        spot = lax.rem(i, per_chunk) // per_read
+        spot = i // per_read
         peak = jnp.sum(jnp.where(block == spot, st[rows, :], 0.0), -1, keepdims=True)
         lse = head_column(ld[...], (base + g) * GROUP)
         delta = head_column(ld[...], (heads_total // GROUP + base + g) * GROUP)
@@ -691,17 +707,15 @@
 
 
 def back_pass(
-    far, xn_all, e_all, st_all, ld, ow, qw, q_all, wk, dq_all, dxs, sides, gain, scale, h, videos_dev
+    far, xn_all, e_all, st_all, ld, ow, qw, q_all, wk, dq_all, dx_all, sides, gain, scale, h, videos_dev
 ):
     depth = wk.shape[0]
     tokens_video = e_all.shape[1]
     frames_dev = tokens_video // PATCH
-    cuts, read_nf = chunks_of(frames_dev)
-    chunks = len(cuts)
+    _, read_nf = chunks_of(frames_dev)
     nf = frames_a_block(read_nf)
     tokens = nf * PATCH
     blocks = frames_dev // nf
-    per_chunk = cuts[0] // nf
     rows = qw.shape[0] // 2
     cols = GROUP * HEAD_SIZE
     groups = depth // cols
@@ -730,7 +744,7 @@
         outs.append(jax.ShapeDtypeStruct((2 * TAIL + 8, depth), f32))
     return pl.pallas_call(
         functools.partial(
-            kernel_back, nf, per_chunk, read_nf // nf, scale, videos_dev, final
+            kernel_back, nf, read_nf // nf, scale, videos_dev, final
         ),
         grid_spec=pltpu.PrefetchScalarGridSpec(
             num_scalar_prefetch=1,
@@ -738,9 +752,7 @@
             in_specs=[
                 pl.BlockSpec((tokens, depth + EXTRA), lambda v, i, p: (v * blocks + i, 0)),
                 pl.BlockSpec((rows, tokens), lambda v, i, p: (v * 2 + y(p), i)),
-                pl.BlockSpec(
-                    (rows, 128), lambda v, i, p: ((v * chunks + i // per_chunk) * 2 + y(p), 0)
-                ),
+                pl.BlockSpec((rows, 128), lambda v, i, p: (v * 2 + y(p), 0)),
                 pl.BlockSpec((LATENTS, 128), lambda v, i, p: (v, 0)),
                 pl.BlockSpec((rows, depth), lambda v, i, p: (v * 2 + y(p), 0)),
                 pl.BlockSpec((rows, depth), lambda v, i, p: (y(p), 0), pipeline_mode=one),
@@ -752,8 +764,8 @@
                 for n in range(videos_dev)
             ]
             + [
-                pl.BlockSpec((rows, depth), lambda v, i, p: (y(p), 0), pipeline_mode=one)
-                for _ in dxs
+                pl.BlockSpec((rows, depth), lambda v, i, p, n=n: (n * 2 + y(p), 0), pipeline_mode=one)
+                for n in range(videos_dev)
             ]
             + [whole(a.shape) for a in extra],
             out_specs=[whole(a.shape) for a in outs],
@@ -769,7 +781,7 @@
         name="back_far" if far else "back_near",
     )(
         jnp.full((1,), h, jnp.int32), xn_all, e_all, st_all, ld, ow, qw, q_all, wk,
-        *[dq_all] * videos_dev, *dxs, *extra,
+        *[dq_all] * videos_dev, *[dx_all] * videos_dev, *extra,
     )
 
 
@@ -1063,18 +1075,14 @@
 
     with jax.named_scope("combine"):
         heads = depth // HEAD_SIZE
-        lse_parts = (
+        lse_local = (
             (st_all[:, 126] + jnp.log(st_all[:, 127]))
-            .reshape(videos_dev, chunks, heads, lat_count)
-            .transpose(1, 0, 3, 2)
-            .reshape(chunks, videos_dev * lat_count, heads)
-        )
-        o_parts = o_all.reshape(videos_dev, chunks, lat_count, heads, HEAD_SIZE)
-        o_parts = o_parts.transpose(1, 0, 2, 3, 4).reshape(chunks, -1, heads, HEAD_SIZE)
-        lse_local = jax.nn.logsumexp(lse_parts, 0)
-        o_local = jnp.sum(o_parts * jnp.exp(lse_parts - lse_local)[..., None], 0)
+            .reshape(videos_dev, heads, lat_count)
+            .transpose(0, 2, 1)
+            .reshape(videos_dev * lat_count, heads)
+        )
         pay = jnp.concatenate(
-            [o_local.reshape(-1, depth).astype(bf16), split_three(lse_local)], 1
+            [o_all.astype(bf16), split_three(lse_local)], 1
         ).reshape(frame_size, share, depth + 3 * heads)
         pay = to_frames(pay)
         lse_each = join_three(pay[..., depth:])
@@ -1129,18 +1137,15 @@
         dv_all = dec_all[..., cols:].reshape(videos_dev * lat_count, depth)
         own_mask = lax.dynamic_slice_in_dim(loss_mask, h * videos_dev, videos_dev, 0).astype(f32)
         counts = own_mask.reshape(videos_dev * tokens_video, 1)
-        decoded = [
-            decode_pass(j, xn_all, ft_all, counts, dq_all, dv_all, w_key, scale, videos_dev)
-            for j in range(videos_dev)
-        ]
-        loss_part = sum(jnp.sum(d[4]) for d in decoded)
+        decoded = decode_pass(xn_all, ft_all, counts, dq_all, dv_all, w_key, scale, videos_dev)
+        loss_part = jnp.sum(decoded[4])
         count_part = jnp.sum(own_mask)
-        dec_side = sum(d[3] for d in decoded)
+        dec_side = jnp.sum(decoded[3], 0)
 
     with jax.named_scope("latent_backward"):
         ddec = jnp.concatenate(
             [
-                jnp.concatenate([d[n] for d in decoded], 0).reshape(frame_size, share, head_size, cols)
+                decoded[n].reshape(frame_size, share, head_size, cols)
                 for n in (0, 1)
             ],
             3,
@@ -1228,7 +1233,7 @@
     half = head_size // 2
     back = functools.partial(
         back_pass, e_all=e_all, ld=ld, ow=ow, qw=qw, q_all=q_all, wk=w_key, dq_all=dq_all,
-        dxs=[d[2] for d in decoded], scale=scale, h=h, videos_dev=videos_dev,
+        dx_all=decoded[2], scale=scale, h=h, videos_dev=videos_dev,
     )
 
     with jax.named_scope("value_gradient"):
@@ -1272,7 +1277,14 @@
         key_sum = key_sum.T.reshape(frame_size // 2, 2, rows_dev, cols)
         key_away = lax.dynamic_index_in_dim(key_sum, 1 - (f & 1), 1, False).astype(bf16)
         key_near = lax.dynamic_index_in_dim(key_sum, f & 1, 1, False)
+        key_away = gate(key_away, grad_value)
+        own_cols = gate(own_cols, key_away)
+        sq = functools.partial(turn, rows=rows_dev, cols=cols, left=left, right=right_sq)
+        ffn = functools.partial(turn, rows=rows_dev, cols=hid, left=left, right=right_ffn)
+        turned_up = ffn(5, 0, (own_cols, 0, wide_b, 0))
+        turned_down = ffn(6, 1, (own_cols, 2, wide_a, 0))
         key_half = key_near + swap(key_away, "frame", 1).astype(f32)
+        key_half = gate(key_half, turned_up[1], turned_down[1])
 
     with jax.named_scope("patch_gradients"):
         dq_pad = lax.dynamic_update_slice_in_dim(
@@ -1280,7 +1292,7 @@
         )
         dquery = own_dq[0] + swap(own_dq[1], "head", 1) + dq_far + dq_pad
         dquery = jnp.concatenate([dquery + zero_of(key_away).astype(f32), pairs], 0)
-        dquery = sum_rounded(dquery, "frame").astype(bf16)
+        dquery = gate(sum_rounded(dquery, "frame").astype(bf16), key_half)
         dquery, dk_sum, dv_sum = (
             dquery[n * lat_count : (n + 1) * lat_count] for n in range(3)
         )
@@ -1301,17 +1313,14 @@
         )
 
     with jax.named_scope("update"):
-        own_cols = gate(own_cols, key_away)
-        sq = functools.partial(turn, rows=rows_dev, cols=cols, left=left, right=right_sq)
-        ffn = functools.partial(turn, rows=rows_dev, cols=hid, left=left, right=right_ffn)
         turned, totals = zip(
             sq(0, 0, (own_cols, 1, wide_b, hid, normed_own, dquery)),
             sq(1, 1, (grad_key,)),
             sq(2, 2, (grad_value,)),
             sq(3, 3, (own_cols, 3, wide_a, hid)),
             sq(4, 4, (own_cols, 1, wide_b, hid + cols)),
-            ffn(5, 0, (own_cols, 0, wide_b, 0)),
-            ffn(6, 1, (own_cols, 2, wide_a, 0)),
+            turned_up,
+            turned_down,
         )
         squares = (
             jnp.sum(sum(totals))

time: 925 us -> 901 us (0.974)
  waiting for transfers between devices: 197 us -> 180 us
    ppermute x74, waiting for transfers between devices: 179 us -> 162 us  [swap(): return lax.ppermute(x, axis, [(i, i ^ bit) for i in range(size)])]
    pallas_call x8 -> x7, Pallas kernels: 290 us -> 287 us  [the longest x4 112 us: read_pass(): pl.pallas_call(functools.partial(kernel_read, nf, before, c > 0, c == chu...]
  transfers between devices with their start and end apart: 82 -> 82, of which waited for: 37 -> 35; matrix products, arithmetic and copies ran while one was open for 14% -> 15% of each run, Pallas kernels for 28% -> 28%
where the time goes in v3:
time: 901 us; the launch traced here: 891 us
  Pallas kernels  368 us (41%)
  waiting for transfers between devices  180 us (20%)
  starting transfers between devices  84.7 us (9%)
  other arithmetic  75 us (8%)
  local copies, waits for them, and re-layouts  70.8 us (8%)
  blocking collectives  43.2 us (5%)
  matrix products  42.4 us (5%)
  between operations  27.1 us (3%)
    ppermute x74, waiting for transfers between devices, swap(): return lax.ppermute(x, axis, [(i, i ^ bit) for i in range(size)])  162 us
    pallas_call x4, Pallas kernels, read_pass(): pl.pallas_call(functools.partial(kernel_read, nf, before, c > 0, c == chu...  112 us
    pallas_call x1, Pallas kernels, decode_pass(): pl.pallas_call(functools.partial(kernel_decode, nf, scale), grid=(videos_...  98.7 us
    pallas_call x2, Pallas kernels, back_pass(): pl.pallas_call(functools.partial(kernel_back, nf, read_nf // nf, scale, v...  76.2 us
    ppermute x74, starting transfers between devices, swap(): return lax.ppermute(x, axis, [(i, i ^ bit) for i in range(size)])  73.7 us
    pallas_call x7, Pallas kernels, turn(): pl.pallas_call(body, grid=(cols // step,), in_specs=specs + [pl.BlockSpec...  25.3 us
    all_to_all x1, blocking collectives, to_tokens(): x = lax.all_to_all(x, 'frame', 0, 0, tiled=True)  23.2 us
    dot_general x8, matrix products, nt(): lax.dot_general(a, b, (((1,), (1,)), ((), ())), preferred_element_type=f32)  19.3 us
  transfers between devices with their start and end apart: 82, of which 35 were waited for; matrix products, arithmetic and copies ran while one was open for 15% of the time, Pallas kernels for 28%

profile of v3, /device:TPU:0, one launch (start us, length us, event | category | flops | bytes accessed | tf_op | source)
XLA Modules:
  0.0 890.7 jit_solution(14117710966044730056)
XLA Ops:
  11.8 7.0 collective-permute-done.1.refs_1_
  63.7 12.7 %collective-permute-done.4 = f32[64,384]{1,0:T(8,128)S(1)} collective-permute-done((f32[64,384]{1,0:T(8,128)S(1)}, f32[64,384]{1,0:T(8,128)S(1)}, u32[]{:S(2)}, u32[]{:S(2)}) %collective-permute-start.4) | collective-permute-done | bytes 98336 | tf_op jit(solution)/shard_map/weights/ppermute | solution.py:69
  77.3 12.7 %collective-permute-done.5 = f32[64,384]{1,0:T(8,128)S(1)} collective-permute-done((f32[64,384]{1,0:T(8,128)S(1)}, f32[64,384]{1,0:T(8,128)S(1)}, u32[]{:S(2)}, u32[]{:S(2)}) %collective-permute-start.5) | collective-permute-done | bytes 98336 | tf_op jit(solution)/shard_map/weights/ppermute | solution.py:69
  90.1 20.1 %collective-permute-done.9 = f32[12,768]{1,0:T(8,128)S(1)} collective-permute-done((f32[12,768]{1,0:T(8,128)S(1)}, f32[12,768]{1,0:T(8,128)S(1)}, u32[]{:S(2)}, u32[]{:S(2)}) %collective-permute-start.9) | collective-permute-done | bytes 36896 | tf_op jit(solution)/shard_map/weights/ppermute | solution.py:69
  124.1 6.6 collective-permute-done.11
  130.7 5.4 broadcast_select_fusion.1
  141.1 5.8 absorb.1.refs_2_.qw
  146.8 12.8 %collective-permute-done.10.refs_1_ = bf16[2,1024,384]{2,1,0:T(8,128)(2,1)} collective-permute-done((bf16[2,1024,384]{2,1,0:T(8,128)(2,1)}, bf16[2,1024,384]{2,1,0:T(8,128)(2,1)}, u32[]{:S(2)}, u32[]{:S(2)}) %collective-permute-start.10) | collective-permute-done | bytes 1572896 | tf_op jit(solution)/shard_map/read/ppermute | solution.py:69
  171.4 35.1 %read_pass.4 = (bf16[6144,1664]{1,0:T(8,128)(2,1)}, bf16[6144,1536]{1,0:T(8,128)(2,1)}, bf16[2048,3072]{1,0:T(8,128)(2,1)}, bf16[2048,1664]{1,0:T(8,128)(2,1)}, ...) custom-call(s32[13]{0:T(128)} %pad_add_fusion.2.place, bf16[24576,384]{1,0:T(8,128)(2,1)} %bitcast.289, ...), custom_call_target="tpu_custom_call" | custom-call | flops 1610612736 | bytes 3145728 | tf_op jit(solution)/shard_map/read/read_pass/pallas_call | solution.py:352
  206.5 21.4 %read_pass.5 = (bf16[6144,1664]{1,0:T(8,128)(2,1)}, bf16[6144,1536]{1,0:T(8,128)(2,1)}, bf16[2048,3072]{1,0:T(8,128)(2,1)}, bf16[2048,1664]{1,0:T(8,128)(2,1)}, ...) custom-call(s32[13]{0:T(128)} %pad_add_fusion.2.place, ...), custom_call_target="tpu_custom_call", output_to_operand_aliasing={{0}: (9, {}), {1}: (10, {}), {2}: (11, {}), {3}: (12, {}), ... | custom-call | flops 805306368 | bytes 1572864 | tf_op jit(solution)/shard_map/read/read_pass/pallas_call | solution.py:352
  236.1 34.9 %read_pass.6 = (bf16[6144,1664]{1,0:T(8,128)(2,1)}, bf16[6144,1536]{1,0:T(8,128)(2,1)}, bf16[2048,3072]{1,0:T(8,128)(2,1)}, bf16[2048,1664]{1,0:T(8,128)(2,1)}, ...) custom-call(s32[13]{0:T(128)} %pad_add_fusion.1.place, ...), custom_call_target="tpu_custom_call", output_to_operand_aliasing={{0}: (9, {}), {1}: (10, {}), {2}: (11, {}), {3}: (12, {}), ... | custom-call | flops 1610612736 | bytes 3145728 | tf_op jit(solution)/shard_map/read/read_pass/pallas_call | solution.py:352
  276.5 20.7 %read_pass.7 = (bf16[6144,1664]{1,0:T(8,128)(2,1)}, bf16[6144,1536]{1,0:T(8,128)(2,1)}, bf16[2048,3072]{1,0:T(8,128)(2,1)}, bf16[2048,1664]{1,0:T(8,128)(2,1)}, ...) custom-call(s32[13]{0:T(128)} %pad_add_fusion.1.place, ...), custom_call_target="tpu_custom_call", output_to_operand_aliasing={{0}: (9, {}), {1}: (10, {}), {2}: (11, {}), {3}: (12, {}), ... | custom-call | flops 805306368 | bytes 1572864 | tf_op jit(solution)/shard_map/read/read_pass/pallas_call | solution.py:352
  333.6 5.9 collective-permute-done.29
  350.3 6.7 collective-permute-done.31
  360.8 6.7 all_to_all.35
  378.4 13.9 %all-to-all-done.2 = bf16[8,16,4,768]{3,2,1,0:T(4,128)(2,1)S(1)} async-done(((bf16[8,16,4,768]{3,2,1,0:T(4,128)(2,1)}), bf16[8,16,4,768]{3,2,1,0:T(4,128)(2,1)S(1)}, u32[]{:S(2)}, u32[]{:S(2)}) %all-to-all-start.2) | async-done | bytes 786464 | tf_op jit(solution)/shard_map/decode/all_to_all | solution.py:1131
  394.2 98.7 %decode_pass.1 = (f32[128,1536]{1,0:T(8,128)}, f32[128,1536]{1,0:T(8,128)}, bf16[2048,1536]{1,0:T(8,128)(2,1)}, f32[2,40,1536]{2,1,0:T(8,128)}, f32[2,8,384]{2,1,0:T(8,128)}) custom-call(bf16[6144,1664]{1,0:T(8,128)(2,1)} %get-tuple-element.122.xn.refs_0_, bf16[6144,1536]{1,0:T(8,128)(2,1)} %get-tuple-element.123.feat, f32[6144,1]{1,0:T(8,128)} %reshape.381.msk, ...), custom_call_target="tpu_custom_call" | custom-call | flops 28991029248 | bytes 18874368 | tf_op jit(solution)/shard_map/decode/decode_pass/pallas_call | solution.py:492
  507.6 6.7 collective-permute-done.35
  516.8 6.9 all_to_all.36
  529.5 6.6 collective-permute-done.40
  546.2 6.5 collective-permute-done.42
  557.8 6.5 all_to_all.37
  564.4 23.2 %all_to_all.38 = bf16[8,16,4,408]{3,1,2,0:T(8,128)(2,1)S(1)} all-to-all(bf16[8,16,4,408]{3,1,2,0:T(8,128)(2,1)S(1)} %broadcast_in_dim.27), channel_id=1, replica_groups=mesh['frame'=8,'head'=4] {'frame'}, dimensions={0} | all-to-all | bytes 835584 | tf_op jit(solution)/shard_map/latent_backward/all_to_all | solution.py:1131
  589.4 17.0 %value_pass.1 = (bf16[2048,1536]{1,0:T(8,128)(2,1)}, bf16[2,384,1536]{2,1,0:T(8,128)(2,1)}, bf16[2,384,1536]{2,1,0:T(8,128)(2,1)}, f32[24,1536]{1,0:T(8,128)}) custom-call(s32[1]{0:T(128)} %bitcast.place, bf16[128,1536]{1,0:T(8,128)(2,1)} %bitcast.303, bf16[1536,1536]{1,0:T(8,128)(2,1)} %pad_maximum_fusion.1.wv, f32[128,128]{1,0:T(8,128)} %pad.8.ld, ...), custom_call_target="tpu_custom_call" | custom-call | flops 1 | bytes 1 | tf_op jit(solution)/shard_map/value/value_pass/pallas_call | solution.py:596
  626.6 37.8 %back_far.1 = (f32[2,64,384]{2,1,0:T(8,128)}, bf16[384,1536]{1,0:T(8,128)(2,1)}, bf16[384,1536]{1,0:T(8,128)(2,1)}, f32[40,1536]{1,0:T(8,128)}) custom-call(s32[1]{0:T(128)} %bitcast.place, bf16[6144,1664]{1,0:T(8,128)(2,1)} %gate.18.xn.refs_0_, bf16[2048,3072]{1,0:T(8,128)(2,1)} %get-tuple-element.133.e, f32[2048,128]{1,0:T(8,128)} %get-tuple-element.125.rest_1_.st, ...), custom_call_target="tpu_custom_call" | custom-call | flops 19327352832 | bytes 37748736 | tf_op jit(solution)/shard_map/back/back_far/pallas_call | solution.py:745
  685.5 38.4 %back_near.1 = (f32[2,64,384]{2,1,0:T(8,128)}, bf16[384,1536]{1,0:T(8,128)(2,1)}, bf16[384,1536]{1,0:T(8,128)(2,1)}, f32[4,24,384]{2,1,0:T(8,128)}) custom-call(s32[1]{0:T(128)} %bitcast.place, bf16[6144,1664]{1,0:T(8,128)(2,1)} %gate.19.xn, bf16[2048,3072]{1,0:T(8,128)(2,1)} %get-tuple-element.133.e, f32[2048,128]{1,0:T(8,128)} %get-tuple-element.125.rest_1_.st, ...), custom_call_target="tpu_custom_call" | custom-call | flops 19327352832 | bytes 37748736 | tf_op jit(solution)/shard_map/back/back_near/pallas_call | solution.py:745
  738.2 7.7 collective-permute-done.51
  773.0 6.0 turn.7
  779.0 6.2 turn.8
  811.7 6.2 collective-permute-done.60
  865.0 9.7 %update.3 = (f32[2,192,1536]{2,1,0:T(8,128)}, f32[2,192,1536]{2,1,0:T(8,128)}, f32[2,192,1536]{2,1,0:T(8,128)}, bf16[2,192,1536]{2,1,0:T(8,128)(2,1)}) custom-call(f32[1]{0:T(128)} %bitcast.117.factor, f32[2,192,1536]{2,1,0:T(8,128)} %weight.3, f32[2,192,1536]{2,1,0:T(8,128)} %one.3, f32[2,192,1536]{2,1,0:T(8,128)} %two.3, f32[7,192,192]{2,1,0:T(8,128)} %copy-done.2, ...), custom_call_target="tpu_custom_call" | custom-call | flops 1 | bytes 1 | tf_op jit(solution)/shard_map/update/update/pallas_call | solution.py:913
  874.7 8.1 update.2
  (615 shorter events, 343.3 us)
Async XLA Ops:
  7.2 110.4 %all-gather.7.cloned.1.call-start = ((), (), s32[]{:S(2)}) async-start(), calls=%async_computation.7 | async-start | bytes 5308416 | tf_op jit(solution)/shard_map/weights/all_gather | solution.py:1019
  19.8 309.0 %all-gather.9.cloned.1.call-start = ((), (), s32[]{:S(2)}) async-start(), calls=%async_computation.8 | async-start | bytes 14598144 | tf_op jit(solution)/shard_map/weights/all_gather | solution.py:1035
  23.8 37.3 %collective-permute-start.3 = (f32[64,384]{1,0:T(8,128)}, f32[64,384]{1,0:T(8,128)}, u32[]{:S(2)}, u32[]{:S(2)}) collective-permute-start(f32[64,384]{1,0:T(8,128)} %fusion.52), channel_id=1, source_target_pairs={{0,4},{4,0},{8,12},{12,8},{16,20},{20,16},{24,28},{28,24},{1,5},{5... | collective-permute-start | bytes 294920 | tf_op jit(solution)/shard_map/weights/ppermute | solution.py:69
  25.5 38.2 %collective-permute-start.8 = (f32[12,384]{1,0:T(8,128)S(1)}, f32[12,384]{1,0:T(8,128)S(1)}, u32[]{:S(2)}, u32[]{:S(2)}) collective-permute-start(f32[12,384]{1,0:T(8,128)S(1)} %copy-done.58), channel_id=1, source_target_pairs={{0,1},{1,0},{2,3},{3,2},{4,5},{5,4},{6,7},{7,6},{8,9},{9,8},{10,11... | collective-permute-start | bytes 55304 | tf_op jit(solution)/shard_map/weights/ppermute | solution.py:69
  38.5 77.2 %collective-permute-start.2 = (bf16[2,2048,384]{2,1,0:T(8,128)(2,1)}, bf16[2,2048,384]{2,1,0:T(8,128)(2,1)}, u32[]{:S(2)}, u32[]{:S(2)}) collective-permute-start(bf16[2,2048,384]{2,1,0:T(8,128)(2,1)} %gate.12), channel_id=1, source_target_pairs={{0,2},{1,3},{2,0},{3,1},{4,6},{5,7},{6,4},{7,5},{8,10},{9,11},{10,... | collective-permute-start | bytes 9437192 | tf_op jit(solution)/shard_map/exchange/ppermute | solution.py:69
  62.0 14.4 %collective-permute-start.4 = (f32[64,384]{1,0:T(8,128)S(1)}, f32[64,384]{1,0:T(8,128)S(1)}, u32[]{:S(2)}, u32[]{:S(2)}) collective-permute-start(f32[64,384]{1,0:T(8,128)S(1)} %add_add_fusion.1), channel_id=1, source_target_pairs={{0,8},{4,12},{8,0},{12,4},{16,24},{20,28},{24,16},{28,20},{1,9},{5... | collective-permute-start | bytes 294920 | tf_op jit(solution)/shard_map/weights/ppermute | solution.py:69
  76.5 33.7 %collective-permute-start.9 = (f32[12,768]{1,0:T(8,128)S(1)}, f32[12,768]{1,0:T(8,128)S(1)}, u32[]{:S(2)}, u32[]{:S(2)}) collective-permute-start(f32[12,768]{1,0:T(8,128)S(1)} %pad_maximum_fusion.12), channel_id=1, source_target_pairs={{0,2},{1,3},{2,0},{3,1},{4,6},{5,7},{6,4},{7,5},{8,10},{9,11},{10,... | collective-permute-start | bytes 110600 | tf_op jit(solution)/shard_map/weights/ppermute | solution.py:69
  90.0 20.2 %collective-permute-start.6 = (bf16[64,384]{1,0:T(8,128)(2,1)S(1)}, bf16[64,384]{1,0:T(8,128)(2,1)S(1)}, u32[]{:S(2)}, u32[]{:S(2)}) collective-permute-start(bf16[64,384]{1,0:T(8,128)(2,1)S(1)} %add_convert_fusion.2), channel_id=1, source_target_pairs={{0,1},{1,0},{2,3},{3,2},{4,5},{5,4},{6,7},{7,6},{8,9},{9,8},{10,11... | collective-permute-start | bytes 147464 | tf_op jit(solution)/shard_map/weights/ppermute | solution.py:69
  122.5 37.1 %collective-permute-start.10 = (bf16[2,1024,384]{2,1,0:T(8,128)(2,1)}, bf16[2,1024,384]{2,1,0:T(8,128)(2,1)}, u32[]{:S(2)}, u32[]{:S(2)}) collective-permute-start(bf16[2,1024,384]{2,1,0:T(8,128)(2,1)} %gate.13), channel_id=1, source_target_pairs={{0,2},{1,3},{2,0},{3,1},{4,6},{5,7},{6,4},{7,5},{8,10},{9,11},{10,... | collective-permute-start | bytes 4718600 | tf_op jit(solution)/shard_map/read/ppermute | solution.py:69
  159.6 70.0 %collective-permute-start.12 = (bf16[2,2048,384]{2,1,0:T(8,128)(2,1)}, bf16[2,2048,384]{2,1,0:T(8,128)(2,1)}, u32[]{:S(2)}, u32[]{:S(2)}) collective-permute-start(bf16[2,2048,384]{2,1,0:T(8,128)(2,1)} %gate.14.dep), channel_id=1, source_target_pairs={{0,2},{1,3},{2,0},{3,1},{4,6},{5,7},{6,4},{7,5},{8,10},{9,11},{10,... | collective-permute-start | bytes 9437192 | tf_op jit(solution)/shard_map/read/ppermute | solution.py:69
  164.4 42.1 %collective-permute-start.13 = (bf16[1024,384]{1,0:T(8,128)(2,1)}, bf16[1024,384]{1,0:T(8,128)(2,1)}, u32[]{:S(2)}, u32[]{:S(2)}) collective-permute-start(bf16[1024,384]{1,0:T(8,128)(2,1)} %get-tuple-element.99), channel_id=1, source_target_pairs={{0,1},{1,0},{2,3},{3,2},{4,5},{5,4},{6,7},{7,6},{8,9},{9,8},{10,11... | collective-permute-start | bytes 2359304 | tf_op jit(solution)/shard_map/read/ppermute | solution.py:69
  167.3 39.2 %collective-permute-start.14 = (bf16[1024,384]{1,0:T(8,128)(2,1)}, bf16[1024,384]{1,0:T(8,128)(2,1)}, u32[]{:S(2)}, u32[]{:S(2)}) collective-permute-start(bf16[1024,384]{1,0:T(8,128)(2,1)} %slice_bitcast_fusion.4), channel_id=1, source_target_pairs={{0,1},{1,0},{2,3},{3,2},{4,5},{5,4},{6,7},{7,6},{8,9},{9,8},{10,11... | collective-permute-start | bytes 2359304 | tf_op jit(solution)/shard_map/read/ppermute | solution.py:69
  170.1 65.4 %collective-permute-start.18 = (bf16[2048,384]{1,0:T(8,128)(2,1)}, bf16[2048,384]{1,0:T(8,128)(2,1)}, u32[]{:S(2)}, u32[]{:S(2)}) collective-permute-start(bf16[2048,384]{1,0:T(8,128)(2,1)} %get-tuple-element.100), channel_id=1, source_target_pairs={{0,1},{1,0},{2,3},{3,2},{4,5},{5,4},{6,7},{7,6},{8,9},{9,8},{10,11... | collective-permute-start | bytes 4718600 | tf_op jit(solution)/shard_map/read/ppermute | solution.py:69
  232.3 38.6 %collective-permute-start.17 = (bf16[2,1024,384]{2,1,0:T(8,128)(2,1)}, bf16[2,1024,384]{2,1,0:T(8,128)(2,1)S(1)}, u32[]{:S(2)}, u32[]{:S(2)}) collective-permute-start(bf16[2,1024,384]{2,1,0:T(8,128)(2,1)} %gate.15.dep), channel_id=1, source_target_pairs={{0,2},{1,3},{2,0},{3,1},{4,6},{5,7},{6,4},{7,5},{8,10},{9,11},{10,... | collective-permute-start | bytes 4718600 | tf_op jit(solution)/shard_map/read/ppermute | solution.py:69
  233.9 42.7 %collective-permute-start = (bf16[1024,384]{1,0:T(8,128)(2,1)}, bf16[1024,384]{1,0:T(8,128)(2,1)}, u32[]{:S(2)}, u32[]{:S(2)}) collective-permute-start(bf16[1024,384]{1,0:T(8,128)(2,1)} %get-tuple-element.94), channel_id=1, source_target_pairs={{0,1},{1,0},{2,3},{3,2},{4,5},{5,4},{6,7},{7,6},{8,9},{9,8},{10,11... | collective-permute-start | bytes 2359304 | tf_op jit(solution)/shard_map/read/ppermute | solution.py:69
  368.6 23.7 %all-to-all-start.2 = ((bf16[8,16,4,768]{3,2,1,0:T(4,128)(2,1)}), bf16[8,16,4,768]{3,2,1,0:T(4,128)(2,1)S(1)}, u32[]{:S(2)}, u32[]{:S(2)}) async-start(bf16[8,16,4,768]{3,2,1,0:T(4,128)(2,1)} %broadcast_in_dim.26), calls=%async_computation.2 | async-start | bytes 1572864 | tf_op jit(solution)/shard_map/decode/all_to_all | solution.py:1131
  372.2 294.5 %all-gather.15.cloned.1.call-start = ((), (), s32[]{:S(2)}) async-start(), calls=%async_computation.11 | async-start | bytes 1327104 | tf_op jit(solution)/shard_map/latent_pairs/all_gather | solution.py:1208
  500.0 14.4 %collective-permute-start.35 = (bf16[16,3072]{1,0:T(8,128)(2,1)S(1)}, bf16[16,3072]{1,0:T(8,128)(2,1)S(1)}, u32[]{:S(2)}, u32[]{:S(2)}) collective-permute-start(bf16[16,3072]{1,0:T(8,128)(2,1)S(1)} %get-tuple-element.220), channel_id=1, source_target_pairs={{0,16},{4,20},{8,24},{12,28},{16,0},{20,4},{24,8},{28,12},{1,17},{... | collective-permute-start | bytes 294920 | tf_op jit(solution)/shard_map/latent_backward/ppermute | solution.py:69
  500.0 16.7 %collective-permute-start.36 = (bf16[16,3072]{1,0:T(8,128)(2,1)S(1)}, bf16[16,3072]{1,0:T(8,128)(2,1)S(1)}, u32[]{:S(2)}, u32[]{:S(2)}) collective-permute-start(bf16[16,3072]{1,0:T(8,128)(2,1)S(1)} %get-tuple-element.219), channel_id=1, source_target_pairs={{0,20},{4,16},{8,28},{12,24},{16,4},{20,0},{24,12},{28,8},{1,21},{... | collective-permute-start | bytes 294920 | tf_op jit(solution)/shard_map/latent_backward/ppermute | solution.py:69
  554.1 219.0 %all-gather.11.cloned.1.call-start = ((), (), s32[]{:S(2)}) async-start(), calls=%async_computation.9 | async-start | bytes 2654208 | tf_op jit(solution)/shard_map/row_gradients/all_gather | solution.py:1218
  554.9 224.1 %all-gather.13.cloned.1.call-start = ((), (), s32[]{:S(2)}) async-start(), calls=%async_computation.10 | async-start | bytes 2211840 | tf_op jit(solution)/shard_map/row_gradients/all_gather | solution.py:1215
  606.5 14.3 %collective-permute-start.43 = (bf16[2,384,1536]{2,1,0:T(8,128)(2,1)}, bf16[2,384,1536]{2,1,0:T(8,128)(2,1)}, u32[]{:S(2)}, u32[]{:S(2)}) collective-permute-start(bf16[2,384,1536]{2,1,0:T(8,128)(2,1)} %get-tuple-element.132), channel_id=1, source_target_pairs={{0,1},{1,0},{2,3},{3,2},{4,5},{5,4},{6,7},{7,6},{8,9},{9,8},{10,11... | collective-permute-start | bytes 7077896 | tf_op jit(solution)/shard_map/value_gradient/ppermute | solution.py:69
  612.0 160.0 %all-to-all-start.4 = ((bf16[8,4,64,192]{3,2,1,0:T(8,128)(2,1)}), bf16[8,4,64,192]{3,2,1,0:T(8,128)(2,1)S(1)}, u32[]{:S(2)}, u32[]{:S(2)}) async-start(bf16[8,4,64,192]{3,2,1,0:T(8,128)(2,1)} %maximum_bitcast_fusion), calls=%async_computation.4 | async-start | bytes 2097152 | tf_op jit(solution)/shard_map/row_gradients/all_to_all | solution.py:1225
  626.6 42.8 %collective-permute-start.46 = (bf16[384,1536]{1,0:T(8,128)(2,1)}, bf16[384,1536]{1,0:T(8,128)(2,1)}, u32[]{:S(2)}, u32[]{:S(2)}) collective-permute-start(bf16[384,1536]{1,0:T(8,128)(2,1)} %fusion.11.refs_1_), channel_id=1, source_target_pairs={{0,2},{1,3},{2,0},{3,1},{4,6},{5,7},{6,4},{7,5},{8,10},{9,11},{10,... | collective-permute-start | bytes 3538952 | tf_op jit(solution)/shard_map/value_gradient/ppermute | solution.py:69
  665.8 15.0 %collective-permute-start.44 = (bf16[384,1536]{1,0:T(8,128)(2,1)}, bf16[384,1536]{1,0:T(8,128)(2,1)}, u32[]{:S(2)}, u32[]{:S(2)}) collective-permute-start(bf16[384,1536]{1,0:T(8,128)(2,1)} %get-tuple-element.137), channel_id=1, source_target_pairs={{0,1},{1,0},{2,3},{3,2},{4,5},{5,4},{6,7},{7,6},{8,9},{9,8},{10,11... | collective-permute-start | bytes 3538952 | tf_op jit(solution)/shard_map/key_gradient/ppermute | solution.py:69
  678.7 49.7 %collective-permute-start.49 = (bf16[4,192,384]{2,1,0:T(8,128)(2,1)S(1)}, bf16[4,192,384]{2,1,0:T(8,128)(2,1)}, u32[]{:S(2)}, u32[]{:S(2)}) collective-permute-start(bf16[4,192,384]{2,1,0:T(8,128)(2,1)S(1)} %fusion.23.refs_3_), channel_id=1, source_target_pairs={{0,4},{4,0},{8,12},{12,8},{16,20},{20,16},{24,28},{28,24},{1,5},{5... | collective-permute-start | bytes 1769480 | tf_op jit(solution)/shard_map/value_gradient/ppermute | solution.py:69
  683.5 63.2 %collective-permute-start.48 = (bf16[384,1536]{1,0:T(8,128)(2,1)}, bf16[384,1536]{1,0:T(8,128)(2,1)}, u32[]{:S(2)}, u32[]{:S(2)}) collective-permute-start(bf16[384,1536]{1,0:T(8,128)(2,1)} %add_convert_fusion.refs_1_), channel_id=1, source_target_pairs={{0,2},{1,3},{2,0},{3,1},{4,6},{5,7},{6,4},{7,5},{8,10},{9,11},{10,... | collective-permute-start | bytes 3538952 | tf_op jit(solution)/shard_map/key_gradient/ppermute | solution.py:69
  723.9 22.7 %collective-permute-start.47 = (bf16[384,1536]{1,0:T(8,128)(2,1)}, bf16[384,1536]{1,0:T(8,128)(2,1)S(1)}, u32[]{:S(2)}, u32[]{:S(2)}) collective-permute-start(bf16[384,1536]{1,0:T(8,128)(2,1)} %get-tuple-element.143), channel_id=1, source_target_pairs={{0,1},{1,0},{2,3},{3,2},{4,5},{5,4},{6,7},{7,6},{8,9},{9,8},{10,11... | collective-permute-start | bytes 3538952 | tf_op jit(solution)/shard_map/key_gradient/ppermute | solution.py:69
  738.2 19.6 %collective-permute-start.62 = (f32[2,24,384]{2,1,0:T(8,128)S(1)}, f32[2,24,384]{2,1,0:T(8,128)S(1)}, u32[]{:S(2)}, u32[]{:S(2)}) collective-permute-start(f32[2,24,384]{2,1,0:T(8,128)S(1)} %slice.337), channel_id=1, source_target_pairs={{0,1},{1,0},{2,3},{3,2},{4,5},{5,4},{6,7},{7,6},{8,9},{9,8},{10,11... | collective-permute-start | bytes 221192 | tf_op jit(solution)/shard_map/patch_gradients/ppermute | solution.py:69
  766.9 19.1 %collective-permute-start.58 = (bf16[4,192,384]{2,1,0:T(8,128)(2,1)}, bf16[4,192,384]{2,1,0:T(8,128)(2,1)}, u32[]{:S(2)}, u32[]{:S(2)}) collective-permute-start(bf16[4,192,384]{2,1,0:T(8,128)(2,1)} %gate.20.refs_1_), channel_id=1, source_target_pairs={{0,4},{4,0},{8,12},{12,8},{16,20},{20,16},{24,28},{28,24},{1,5},{5... | collective-permute-start | bytes 1769480 | tf_op jit(solution)/shard_map/key_gradient/ppermute | solution.py:69
  768.7 16.6 %collective-permute-start.57 = (bf16[192,384]{1,0:T(8,128)(2,1)}, bf16[192,384]{1,0:T(8,128)(2,1)S(1)}, u32[]{:S(2)}, u32[]{:S(2)}) collective-permute-start(bf16[192,384]{1,0:T(8,128)(2,1)} %fusion.42), channel_id=1, source_target_pairs={{0,16},{4,20},{8,24},{12,28},{16,0},{20,4},{24,8},{28,12},{1,17},{... | collective-permute-start | bytes 442376 | tf_op jit(solution)/shard_map/patch_gradients/ppermute | solution.py:69
  810.1 24.6 %collective-permute-start.65 = (bf16[64,1536]{1,0:T(8,128)(2,1)}, bf16[64,1536]{1,0:T(8,128)(2,1)}, u32[]{:S(2)}, u32[]{:S(2)}) collective-permute-start(bf16[64,1536]{1,0:T(8,128)(2,1)} %fusion.47), channel_id=1, source_target_pairs={{0,2},{1,3},{2,0},{3,1},{4,6},{5,7},{6,4},{7,5},{8,10},{9,11},{10,... | collective-permute-start | bytes 589832 | tf_op jit(solution)/shard_map/patch_gradients/ppermute | solution.py:69
  (126 other events, 1327.5 us)
Sparse Core Ops, SparseCore 0:
  20.0 83.3 all-gather.6
  122.5 181.5 all-gather.8
  554.2 43.1 all-gather.14
  600.0 63.1 all-gather.10
  665.2 48.9 all-gather.12

commit v4 on v3

--- a/solution.py
+++ b/solution.py
@@ -1285,6 +1285,11 @@
         turned_down = ffn(6, 1, (own_cols, 2, wide_a, 0))
         key_half = key_near + swap(key_away, "frame", 1).astype(f32)
         key_half = gate(key_half, turned_up[1], turned_down[1])
+        key_low = key_half.astype(bf16)
+        key_sends = [
+            lax.dynamic_index_in_dim(key_low, (f >> 1) ^ d, 0, False)
+            for d in range(1, frame_size // 2)
+        ]
 
     with jax.named_scope("patch_gradients"):
         dq_pad = lax.dynamic_update_slice_in_dim(
@@ -1292,13 +1297,15 @@
         )
         dquery = own_dq[0] + swap(own_dq[1], "head", 1) + dq_far + dq_pad
         dquery = jnp.concatenate([dquery + zero_of(key_away).astype(f32), pairs], 0)
-        dquery = gate(sum_rounded(dquery, "frame").astype(bf16), key_half)
+        dquery = gate(sum_rounded(dquery, "frame").astype(bf16), *key_sends)
         dquery, dk_sum, dv_sum = (
             dquery[n * lat_count : (n + 1) * lat_count] for n in range(3)
         )
 
     with jax.named_scope("key_gradient"):
-        grad_key = scatter_deep(key_half)
+        grad_key = lax.dynamic_index_in_dim(key_half, f >> 1, 0, False)
+        for d, send in enumerate(key_sends):
+            grad_key = grad_key + swap(send, "frame", 2 * (d + 1)).astype(f32)
 
     with jax.named_scope("patch_gradients"):
         pack = sum_near(pack[:half], pack[half:])

time: 901 us -> 903 us (level)
  no operation moved by 1% of the time
where the time goes in v4:
time: 903 us; the launch traced here: 893 us
  Pallas kernels  367 us (41%)
  waiting for transfers between devices  179 us (20%)
  starting transfers between devices  85.3 us (9%)
  other arithmetic  77.2 us (9%)
  local copies, waits for them, and re-layouts  71.7 us (8%)
  blocking collectives  43.2 us (5%)
  matrix products  42.3 us (5%)
  between operations  27.1 us (3%)
    ppermute x74, waiting for transfers between devices, swap(): return lax.ppermute(x, axis, [(i, i ^ bit) for i in range(size)])  161 us
    pallas_call x4, Pallas kernels, read_pass(): pl.pallas_call(functools.partial(kernel_read, nf, before, c > 0, c == chu...  112 us
    pallas_call x1, Pallas kernels, decode_pass(): pl.pallas_call(functools.partial(kernel_decode, nf, scale), grid=(videos_...  98.7 us
    pallas_call x2, Pallas kernels, back_pass(): pl.pallas_call(functools.partial(kernel_back, nf, read_nf // nf, scale, v...  76.1 us
    ppermute x74, starting transfers between devices, swap(): return lax.ppermute(x, axis, [(i, i ^ bit) for i in range(size)])  74.2 us
    pallas_call x7, Pallas kernels, turn(): pl.pallas_call(body, grid=(cols // step,), in_specs=specs + [pl.BlockSpec...  25.4 us
    all_to_all x1, blocking collectives, to_tokens(): x = lax.all_to_all(x, 'frame', 0, 0, tiled=True)  23.2 us
    dot_general x8, matrix products, nt(): lax.dot_general(a, b, (((1,), (1,)), ((), ())), preferred_element_type=f32)  19.2 us
  transfers between devices with their start and end apart: 82, of which 35 were waited for; matrix products, arithmetic and copies ran while one was open for 15% of the time, Pallas kernels for 28%

profile of v4, /device:TPU:0, one launch (start us, length us, event | category | flops | bytes accessed | tf_op | source)
XLA Modules:
  0.0 892.7 jit_solution(7586981849087688582)
XLA Ops:
  11.8 7.0 collective-permute-done.1.refs_1_
  63.8 12.7 %collective-permute-done.4 = f32[64,384]{1,0:T(8,128)S(1)} collective-permute-done((f32[64,384]{1,0:T(8,128)S(1)}, f32[64,384]{1,0:T(8,128)S(1)}, u32[]{:S(2)}, u32[]{:S(2)}) %collective-permute-start.4) | collective-permute-done | bytes 98336 | tf_op jit(solution)/shard_map/weights/ppermute | solution.py:69
  77.3 12.7 %collective-permute-done.5 = f32[64,384]{1,0:T(8,128)S(1)} collective-permute-done((f32[64,384]{1,0:T(8,128)S(1)}, f32[64,384]{1,0:T(8,128)S(1)}, u32[]{:S(2)}, u32[]{:S(2)}) %collective-permute-start.5) | collective-permute-done | bytes 98336 | tf_op jit(solution)/shard_map/weights/ppermute | solution.py:69
  90.1 20.1 %collective-permute-done.9 = f32[12,768]{1,0:T(8,128)S(1)} collective-permute-done((f32[12,768]{1,0:T(8,128)S(1)}, f32[12,768]{1,0:T(8,128)S(1)}, u32[]{:S(2)}, u32[]{:S(2)}) %collective-permute-start.9) | collective-permute-done | bytes 36896 | tf_op jit(solution)/shard_map/weights/ppermute | solution.py:69
  124.1 6.6 collective-permute-done.11
  130.7 5.4 broadcast_select_fusion.1
  141.0 5.8 absorb.1.refs_2_.qw
  146.8 12.8 %collective-permute-done.10.refs_1_ = bf16[2,1024,384]{2,1,0:T(8,128)(2,1)} collective-permute-done((bf16[2,1024,384]{2,1,0:T(8,128)(2,1)}, bf16[2,1024,384]{2,1,0:T(8,128)(2,1)}, u32[]{:S(2)}, u32[]{:S(2)}) %collective-permute-start.10) | collective-permute-done | bytes 1572896 | tf_op jit(solution)/shard_map/read/ppermute | solution.py:69
  171.4 35.1 %read_pass.4 = (bf16[6144,1664]{1,0:T(8,128)(2,1)}, bf16[6144,1536]{1,0:T(8,128)(2,1)}, bf16[2048,3072]{1,0:T(8,128)(2,1)}, bf16[2048,1664]{1,0:T(8,128)(2,1)}, ...) custom-call(s32[13]{0:T(128)} %pad_add_fusion.2.place, bf16[24576,384]{1,0:T(8,128)(2,1)} %bitcast.289, ...), custom_call_target="tpu_custom_call" | custom-call | flops 1610612736 | bytes 3145728 | tf_op jit(solution)/shard_map/read/read_pass/pallas_call | solution.py:352
  206.5 21.4 %read_pass.5 = (bf16[6144,1664]{1,0:T(8,128)(2,1)}, bf16[6144,1536]{1,0:T(8,128)(2,1)}, bf16[2048,3072]{1,0:T(8,128)(2,1)}, bf16[2048,1664]{1,0:T(8,128)(2,1)}, ...) custom-call(s32[13]{0:T(128)} %pad_add_fusion.2.place, ...), custom_call_target="tpu_custom_call", output_to_operand_aliasing={{0}: (9, {}), {1}: (10, {}), {2}: (11, {}), {3}: (12, {}), ... | custom-call | flops 805306368 | bytes 1572864 | tf_op jit(solution)/shard_map/read/read_pass/pallas_call | solution.py:352
  236.1 34.9 %read_pass.6 = (bf16[6144,1664]{1,0:T(8,128)(2,1)}, bf16[6144,1536]{1,0:T(8,128)(2,1)}, bf16[2048,3072]{1,0:T(8,128)(2,1)}, bf16[2048,1664]{1,0:T(8,128)(2,1)}, ...) custom-call(s32[13]{0:T(128)} %pad_add_fusion.1.place, ...), custom_call_target="tpu_custom_call", output_to_operand_aliasing={{0}: (9, {}), {1}: (10, {}), {2}: (11, {}), {3}: (12, {}), ... | custom-call | flops 1610612736 | bytes 3145728 | tf_op jit(solution)/shard_map/read/read_pass/pallas_call | solution.py:352
  276.5 20.7 %read_pass.7 = (bf16[6144,1664]{1,0:T(8,128)(2,1)}, bf16[6144,1536]{1,0:T(8,128)(2,1)}, bf16[2048,3072]{1,0:T(8,128)(2,1)}, bf16[2048,1664]{1,0:T(8,128)(2,1)}, ...) custom-call(s32[13]{0:T(128)} %pad_add_fusion.1.place, ...), custom_call_target="tpu_custom_call", output_to_operand_aliasing={{0}: (9, {}), {1}: (10, {}), {2}: (11, {}), {3}: (12, {}), ... | custom-call | flops 805306368 | bytes 1572864 | tf_op jit(solution)/shard_map/read/read_pass/pallas_call | solution.py:352
  333.6 5.9 collective-permute-done.29
  350.3 6.7 collective-permute-done.31
  360.8 6.7 all_to_all.35
  378.4 13.9 %all-to-all-done.2 = bf16[8,16,4,768]{3,2,1,0:T(4,128)(2,1)S(1)} async-done(((bf16[8,16,4,768]{3,2,1,0:T(4,128)(2,1)}), bf16[8,16,4,768]{3,2,1,0:T(4,128)(2,1)S(1)}, u32[]{:S(2)}, u32[]{:S(2)}) %all-to-all-start.2) | async-done | bytes 786464 | tf_op jit(solution)/shard_map/decode/all_to_all | solution.py:1131
  394.1 98.7 %decode_pass.1 = (f32[128,1536]{1,0:T(8,128)}, f32[128,1536]{1,0:T(8,128)}, bf16[2048,1536]{1,0:T(8,128)(2,1)}, f32[2,40,1536]{2,1,0:T(8,128)}, f32[2,8,384]{2,1,0:T(8,128)}) custom-call(bf16[6144,1664]{1,0:T(8,128)(2,1)} %get-tuple-element.122.xn.refs_0_, bf16[6144,1536]{1,0:T(8,128)(2,1)} %get-tuple-element.123.feat, f32[6144,1]{1,0:T(8,128)} %reshape.381.msk, ...), custom_call_target="tpu_custom_call" | custom-call | flops 28991029248 | bytes 18874368 | tf_op jit(solution)/shard_map/decode/decode_pass/pallas_call | solution.py:492
  507.6 6.7 collective-permute-done.35
  516.8 6.9 all_to_all.36
  529.4 6.6 collective-permute-done.40
  546.2 6.5 collective-permute-done.42
  557.8 6.5 all_to_all.37
  564.4 23.2 %all_to_all.38 = bf16[8,16,4,408]{3,1,2,0:T(8,128)(2,1)S(1)} all-to-all(bf16[8,16,4,408]{3,1,2,0:T(8,128)(2,1)S(1)} %broadcast_in_dim.27), channel_id=1, replica_groups=mesh['frame'=8,'head'=4] {'frame'}, dimensions={0} | all-to-all | bytes 835584 | tf_op jit(solution)/shard_map/latent_backward/all_to_all | solution.py:1131
  589.3 17.0 %value_pass.1 = (bf16[2048,1536]{1,0:T(8,128)(2,1)}, bf16[2,384,1536]{2,1,0:T(8,128)(2,1)}, bf16[2,384,1536]{2,1,0:T(8,128)(2,1)}, f32[24,1536]{1,0:T(8,128)}) custom-call(s32[1]{0:T(128)} %bitcast.place, bf16[128,1536]{1,0:T(8,128)(2,1)} %bitcast.303, bf16[1536,1536]{1,0:T(8,128)(2,1)} %pad_maximum_fusion.1.wv, f32[128,128]{1,0:T(8,128)} %pad.8.ld, ...), custom_call_target="tpu_custom_call" | custom-call | flops 1 | bytes 1 | tf_op jit(solution)/shard_map/value/value_pass/pallas_call | solution.py:596
  626.5 37.8 %back_far.1 = (f32[2,64,384]{2,1,0:T(8,128)}, bf16[384,1536]{1,0:T(8,128)(2,1)}, bf16[384,1536]{1,0:T(8,128)(2,1)}, f32[40,1536]{1,0:T(8,128)}) custom-call(s32[1]{0:T(128)} %bitcast.place, bf16[6144,1664]{1,0:T(8,128)(2,1)} %gate.18.xn.refs_0_, bf16[2048,3072]{1,0:T(8,128)(2,1)} %get-tuple-element.133.e, f32[2048,128]{1,0:T(8,128)} %get-tuple-element.125.rest_1_.st, ...), custom_call_target="tpu_custom_call" | custom-call | flops 19327352832 | bytes 37748736 | tf_op jit(solution)/shard_map/back/back_far/pallas_call | solution.py:745
  685.5 38.3 %back_near.1 = (f32[2,64,384]{2,1,0:T(8,128)}, bf16[384,1536]{1,0:T(8,128)(2,1)}, bf16[384,1536]{1,0:T(8,128)(2,1)}, f32[4,24,384]{2,1,0:T(8,128)}) custom-call(s32[1]{0:T(128)} %bitcast.place, bf16[6144,1664]{1,0:T(8,128)(2,1)} %gate.19.xn, bf16[2048,3072]{1,0:T(8,128)(2,1)} %get-tuple-element.133.e, f32[2048,128]{1,0:T(8,128)} %get-tuple-element.125.rest_1_.st, ...), custom_call_target="tpu_custom_call" | custom-call | flops 19327352832 | bytes 37748736 | tf_op jit(solution)/shard_map/back/back_near/pallas_call | solution.py:745
  738.3 7.4 collective-permute-done.51
  773.4 6.0 turn.7
  779.4 6.2 turn.8
  813.6 5.3 collective-permute-done.60
  867.0 9.7 %update.3 = (f32[2,192,1536]{2,1,0:T(8,128)}, f32[2,192,1536]{2,1,0:T(8,128)}, f32[2,192,1536]{2,1,0:T(8,128)}, bf16[2,192,1536]{2,1,0:T(8,128)(2,1)}) custom-call(f32[1]{0:T(128)} %bitcast.117.factor, f32[2,192,1536]{2,1,0:T(8,128)} %weight.3, f32[2,192,1536]{2,1,0:T(8,128)} %one.3, f32[2,192,1536]{2,1,0:T(8,128)} %two.3, f32[7,192,192]{2,1,0:T(8,128)} %copy-done.2, ...), custom_call_target="tpu_custom_call" | custom-call | flops 1 | bytes 1 | tf_op jit(solution)/shard_map/update/update/pallas_call | solution.py:913
  876.7 8.1 update.2
  (619 shorter events, 346.5 us)
Async XLA Ops:
  7.2 110.4 %all-gather.7.cloned.1.call-start = ((), (), s32[]{:S(2)}) async-start(), calls=%async_computation.7 | async-start | bytes 5308416 | tf_op jit(solution)/shard_map/weights/all_gather | solution.py:1019
  19.8 309.0 %all-gather.9.cloned.1.call-start = ((), (), s32[]{:S(2)}) async-start(), calls=%async_computation.8 | async-start | bytes 14598144 | tf_op jit(solution)/shard_map/weights/all_gather | solution.py:1035
  23.8 37.4 %collective-permute-start.3 = (f32[64,384]{1,0:T(8,128)}, f32[64,384]{1,0:T(8,128)}, u32[]{:S(2)}, u32[]{:S(2)}) collective-permute-start(f32[64,384]{1,0:T(8,128)} %fusion.52), channel_id=1, source_target_pairs={{0,4},{4,0},{8,12},{12,8},{16,20},{20,16},{24,28},{28,24},{1,5},{5... | collective-permute-start | bytes 294920 | tf_op jit(solution)/shard_map/weights/ppermute | solution.py:69
  25.5 38.3 %collective-permute-start.8 = (f32[12,384]{1,0:T(8,128)S(1)}, f32[12,384]{1,0:T(8,128)S(1)}, u32[]{:S(2)}, u32[]{:S(2)}) collective-permute-start(f32[12,384]{1,0:T(8,128)S(1)} %copy-done.60), channel_id=1, source_target_pairs={{0,1},{1,0},{2,3},{3,2},{4,5},{5,4},{6,7},{7,6},{8,9},{9,8},{10,11... | collective-permute-start | bytes 55304 | tf_op jit(solution)/shard_map/weights/ppermute | solution.py:69
  38.5 77.2 %collective-permute-start.2 = (bf16[2,2048,384]{2,1,0:T(8,128)(2,1)}, bf16[2,2048,384]{2,1,0:T(8,128)(2,1)}, u32[]{:S(2)}, u32[]{:S(2)}) collective-permute-start(bf16[2,2048,384]{2,1,0:T(8,128)(2,1)} %gate.12), channel_id=1, source_target_pairs={{0,2},{1,3},{2,0},{3,1},{4,6},{5,7},{6,4},{7,5},{8,10},{9,11},{10,... | collective-permute-start | bytes 9437192 | tf_op jit(solution)/shard_map/exchange/ppermute | solution.py:69
  62.1 14.4 %collective-permute-start.4 = (f32[64,384]{1,0:T(8,128)S(1)}, f32[64,384]{1,0:T(8,128)S(1)}, u32[]{:S(2)}, u32[]{:S(2)}) collective-permute-start(f32[64,384]{1,0:T(8,128)S(1)} %add_add_fusion.1), channel_id=1, source_target_pairs={{0,8},{4,12},{8,0},{12,4},{16,24},{20,28},{24,16},{28,20},{1,9},{5... | collective-permute-start | bytes 294920 | tf_op jit(solution)/shard_map/weights/ppermute | solution.py:69
  76.6 33.6 %collective-permute-start.9 = (f32[12,768]{1,0:T(8,128)S(1)}, f32[12,768]{1,0:T(8,128)S(1)}, u32[]{:S(2)}, u32[]{:S(2)}) collective-permute-start(f32[12,768]{1,0:T(8,128)S(1)} %pad_maximum_fusion.12), channel_id=1, source_target_pairs={{0,2},{1,3},{2,0},{3,1},{4,6},{5,7},{6,4},{7,5},{8,10},{9,11},{10,... | collective-permute-start | bytes 110600 | tf_op jit(solution)/shard_map/weights/ppermute | solution.py:69
  90.0 20.2 %collective-permute-start.6 = (bf16[64,384]{1,0:T(8,128)(2,1)S(1)}, bf16[64,384]{1,0:T(8,128)(2,1)S(1)}, u32[]{:S(2)}, u32[]{:S(2)}) collective-permute-start(bf16[64,384]{1,0:T(8,128)(2,1)S(1)} %add_convert_fusion.2), channel_id=1, source_target_pairs={{0,1},{1,0},{2,3},{3,2},{4,5},{5,4},{6,7},{7,6},{8,9},{9,8},{10,11... | collective-permute-start | bytes 147464 | tf_op jit(solution)/shard_map/weights/ppermute | solution.py:69
  122.5 37.1 %collective-permute-start.10 = (bf16[2,1024,384]{2,1,0:T(8,128)(2,1)}, bf16[2,1024,384]{2,1,0:T(8,128)(2,1)}, u32[]{:S(2)}, u32[]{:S(2)}) collective-permute-start(bf16[2,1024,384]{2,1,0:T(8,128)(2,1)} %gate.13), channel_id=1, source_target_pairs={{0,2},{1,3},{2,0},{3,1},{4,6},{5,7},{6,4},{7,5},{8,10},{9,11},{10,... | collective-permute-start | bytes 4718600 | tf_op jit(solution)/shard_map/read/ppermute | solution.py:69
  159.6 70.0 %collective-permute-start.12 = (bf16[2,2048,384]{2,1,0:T(8,128)(2,1)}, bf16[2,2048,384]{2,1,0:T(8,128)(2,1)}, u32[]{:S(2)}, u32[]{:S(2)}) collective-permute-start(bf16[2,2048,384]{2,1,0:T(8,128)(2,1)} %gate.14.dep), channel_id=1, source_target_pairs={{0,2},{1,3},{2,0},{3,1},{4,6},{5,7},{6,4},{7,5},{8,10},{9,11},{10,... | collective-permute-start | bytes 9437192 | tf_op jit(solution)/shard_map/read/ppermute | solution.py:69
  164.4 42.1 %collective-permute-start.13 = (bf16[1024,384]{1,0:T(8,128)(2,1)}, bf16[1024,384]{1,0:T(8,128)(2,1)}, u32[]{:S(2)}, u32[]{:S(2)}) collective-permute-start(bf16[1024,384]{1,0:T(8,128)(2,1)} %get-tuple-element.99), channel_id=1, source_target_pairs={{0,1},{1,0},{2,3},{3,2},{4,5},{5,4},{6,7},{7,6},{8,9},{9,8},{10,11... | collective-permute-start | bytes 2359304 | tf_op jit(solution)/shard_map/read/ppermute | solution.py:69
  167.3 39.2 %collective-permute-start.14 = (bf16[1024,384]{1,0:T(8,128)(2,1)}, bf16[1024,384]{1,0:T(8,128)(2,1)}, u32[]{:S(2)}, u32[]{:S(2)}) collective-permute-start(bf16[1024,384]{1,0:T(8,128)(2,1)} %slice_bitcast_fusion.4), channel_id=1, source_target_pairs={{0,1},{1,0},{2,3},{3,2},{4,5},{5,4},{6,7},{7,6},{8,9},{9,8},{10,11... | collective-permute-start | bytes 2359304 | tf_op jit(solution)/shard_map/read/ppermute | solution.py:69
  170.0 65.4 %collective-permute-start.18 = (bf16[2048,384]{1,0:T(8,128)(2,1)}, bf16[2048,384]{1,0:T(8,128)(2,1)}, u32[]{:S(2)}, u32[]{:S(2)}) collective-permute-start(bf16[2048,384]{1,0:T(8,128)(2,1)} %get-tuple-element.100), channel_id=1, source_target_pairs={{0,1},{1,0},{2,3},{3,2},{4,5},{5,4},{6,7},{7,6},{8,9},{9,8},{10,11... | collective-permute-start | bytes 4718600 | tf_op jit(solution)/shard_map/read/ppermute | solution.py:69
  232.3 38.6 %collective-permute-start.17 = (bf16[2,1024,384]{2,1,0:T(8,128)(2,1)}, bf16[2,1024,384]{2,1,0:T(8,128)(2,1)S(1)}, u32[]{:S(2)}, u32[]{:S(2)}) collective-permute-start(bf16[2,1024,384]{2,1,0:T(8,128)(2,1)} %gate.15.dep), channel_id=1, source_target_pairs={{0,2},{1,3},{2,0},{3,1},{4,6},{5,7},{6,4},{7,5},{8,10},{9,11},{10,... | collective-permute-start | bytes 4718600 | tf_op jit(solution)/shard_map/read/ppermute | solution.py:69
  233.8 42.6 %collective-permute-start = (bf16[1024,384]{1,0:T(8,128)(2,1)}, bf16[1024,384]{1,0:T(8,128)(2,1)}, u32[]{:S(2)}, u32[]{:S(2)}) collective-permute-start(bf16[1024,384]{1,0:T(8,128)(2,1)} %get-tuple-element.94), channel_id=1, source_target_pairs={{0,1},{1,0},{2,3},{3,2},{4,5},{5,4},{6,7},{7,6},{8,9},{9,8},{10,11... | collective-permute-start | bytes 2359304 | tf_op jit(solution)/shard_map/read/ppermute | solution.py:69
  368.6 23.7 %all-to-all-start.2 = ((bf16[8,16,4,768]{3,2,1,0:T(4,128)(2,1)}), bf16[8,16,4,768]{3,2,1,0:T(4,128)(2,1)S(1)}, u32[]{:S(2)}, u32[]{:S(2)}) async-start(bf16[8,16,4,768]{3,2,1,0:T(4,128)(2,1)} %broadcast_in_dim.26), calls=%async_computation.2 | async-start | bytes 1572864 | tf_op jit(solution)/shard_map/decode/all_to_all | solution.py:1131
  372.1 294.5 %all-gather.15.cloned.1.call-start = ((), (), s32[]{:S(2)}) async-start(), calls=%async_computation.11 | async-start | bytes 1327104 | tf_op jit(solution)/shard_map/latent_pairs/all_gather | solution.py:1208
  499.9 14.4 %collective-permute-start.35 = (bf16[16,3072]{1,0:T(8,128)(2,1)S(1)}, bf16[16,3072]{1,0:T(8,128)(2,1)S(1)}, u32[]{:S(2)}, u32[]{:S(2)}) collective-permute-start(bf16[16,3072]{1,0:T(8,128)(2,1)S(1)} %get-tuple-element.220), channel_id=1, source_target_pairs={{0,16},{4,20},{8,24},{12,28},{16,0},{20,4},{24,8},{28,12},{1,17},{... | collective-permute-start | bytes 294920 | tf_op jit(solution)/shard_map/latent_backward/ppermute | solution.py:69
  499.9 16.7 %collective-permute-start.36 = (bf16[16,3072]{1,0:T(8,128)(2,1)S(1)}, bf16[16,3072]{1,0:T(8,128)(2,1)S(1)}, u32[]{:S(2)}, u32[]{:S(2)}) collective-permute-start(bf16[16,3072]{1,0:T(8,128)(2,1)S(1)} %get-tuple-element.219), channel_id=1, source_target_pairs={{0,20},{4,16},{8,28},{12,24},{16,4},{20,0},{24,12},{28,8},{1,21},{... | collective-permute-start | bytes 294920 | tf_op jit(solution)/shard_map/latent_backward/ppermute | solution.py:69
  554.0 219.3 %all-gather.11.cloned.1.call-start = ((), (), s32[]{:S(2)}) async-start(), calls=%async_computation.9 | async-start | bytes 2654208 | tf_op jit(solution)/shard_map/row_gradients/all_gather | solution.py:1218
  554.8 224.5 %all-gather.13.cloned.1.call-start = ((), (), s32[]{:S(2)}) async-start(), calls=%async_computation.10 | async-start | bytes 2211840 | tf_op jit(solution)/shard_map/row_gradients/all_gather | solution.py:1215
  611.9 160.5 %all-to-all-start.4 = ((bf16[8,4,64,192]{3,2,1,0:T(8,128)(2,1)}), bf16[8,4,64,192]{3,2,1,0:T(8,128)(2,1)S(1)}, u32[]{:S(2)}, u32[]{:S(2)}) async-start(bf16[8,4,64,192]{3,2,1,0:T(8,128)(2,1)} %maximum_bitcast_fusion), calls=%async_computation.4 | async-start | bytes 2097152 | tf_op jit(solution)/shard_map/row_gradients/all_to_all | solution.py:1225
  626.5 42.8 %collective-permute-start.46 = (bf16[384,1536]{1,0:T(8,128)(2,1)}, bf16[384,1536]{1,0:T(8,128)(2,1)}, u32[]{:S(2)}, u32[]{:S(2)}) collective-permute-start(bf16[384,1536]{1,0:T(8,128)(2,1)} %fusion.11.refs_1_), channel_id=1, source_target_pairs={{0,2},{1,3},{2,0},{3,1},{4,6},{5,7},{6,4},{7,5},{8,10},{9,11},{10,... | collective-permute-start | bytes 3538952 | tf_op jit(solution)/shard_map/value_gradient/ppermute | solution.py:69
  665.7 15.1 %collective-permute-start.44 = (bf16[384,1536]{1,0:T(8,128)(2,1)}, bf16[384,1536]{1,0:T(8,128)(2,1)}, u32[]{:S(2)}, u32[]{:S(2)}) collective-permute-start(bf16[384,1536]{1,0:T(8,128)(2,1)} %get-tuple-element.137), channel_id=1, source_target_pairs={{0,1},{1,0},{2,3},{3,2},{4,5},{5,4},{6,7},{7,6},{8,9},{9,8},{10,11... | collective-permute-start | bytes 3538952 | tf_op jit(solution)/shard_map/key_gradient/ppermute | solution.py:69
  678.7 49.6 %collective-permute-start.49 = (bf16[4,192,384]{2,1,0:T(8,128)(2,1)S(1)}, bf16[4,192,384]{2,1,0:T(8,128)(2,1)}, u32[]{:S(2)}, u32[]{:S(2)}) collective-permute-start(bf16[4,192,384]{2,1,0:T(8,128)(2,1)S(1)} %fusion.23.refs_3_), channel_id=1, source_target_pairs={{0,4},{4,0},{8,12},{12,8},{16,20},{20,16},{24,28},{28,24},{1,5},{5... | collective-permute-start | bytes 1769480 | tf_op jit(solution)/shard_map/value_gradient/ppermute | solution.py:69
  683.4 63.1 %collective-permute-start.48 = (bf16[384,1536]{1,0:T(8,128)(2,1)}, bf16[384,1536]{1,0:T(8,128)(2,1)}, u32[]{:S(2)}, u32[]{:S(2)}) collective-permute-start(bf16[384,1536]{1,0:T(8,128)(2,1)} %add_convert_fusion.refs_1_), channel_id=1, source_target_pairs={{0,2},{1,3},{2,0},{3,1},{4,6},{5,7},{6,4},{7,5},{8,10},{9,11},{10,... | collective-permute-start | bytes 3538952 | tf_op jit(solution)/shard_map/key_gradient/ppermute | solution.py:69
  723.8 22.7 %collective-permute-start.47 = (bf16[384,1536]{1,0:T(8,128)(2,1)}, bf16[384,1536]{1,0:T(8,128)(2,1)S(1)}, u32[]{:S(2)}, u32[]{:S(2)}) collective-permute-start(bf16[384,1536]{1,0:T(8,128)(2,1)} %get-tuple-element.143), channel_id=1, source_target_pairs={{0,1},{1,0},{2,3},{3,2},{4,5},{5,4},{6,7},{7,6},{8,9},{9,8},{10,11... | collective-permute-start | bytes 3538952 | tf_op jit(solution)/shard_map/key_gradient/ppermute | solution.py:69
  738.3 19.4 %collective-permute-start.62 = (f32[2,24,384]{2,1,0:T(8,128)S(1)}, f32[2,24,384]{2,1,0:T(8,128)S(1)}, u32[]{:S(2)}, u32[]{:S(2)}) collective-permute-start(f32[2,24,384]{2,1,0:T(8,128)S(1)} %slice.337), channel_id=1, source_target_pairs={{0,1},{1,0},{2,3},{3,2},{4,5},{5,4},{6,7},{7,6},{8,9},{9,8},{10,11... | collective-permute-start | bytes 221192 | tf_op jit(solution)/shard_map/patch_gradients/ppermute | solution.py:69
  766.8 19.6 %collective-permute-start.58 = (bf16[4,192,384]{2,1,0:T(8,128)(2,1)}, bf16[4,192,384]{2,1,0:T(8,128)(2,1)}, u32[]{:S(2)}, u32[]{:S(2)}) collective-permute-start(bf16[4,192,384]{2,1,0:T(8,128)(2,1)} %gate.20.refs_1_), channel_id=1, source_target_pairs={{0,4},{4,0},{8,12},{12,8},{16,20},{20,16},{24,28},{28,24},{1,5},{5... | collective-permute-start | bytes 1769480 | tf_op jit(solution)/shard_map/key_gradient/ppermute | solution.py:69
  768.6 16.9 %collective-permute-start.57 = (bf16[192,384]{1,0:T(8,128)(2,1)}, bf16[192,384]{1,0:T(8,128)(2,1)S(1)}, u32[]{:S(2)}, u32[]{:S(2)}) collective-permute-start(bf16[192,384]{1,0:T(8,128)(2,1)} %fusion.42), channel_id=1, source_target_pairs={{0,16},{4,20},{8,24},{12,28},{16,0},{20,4},{24,8},{28,12},{1,17},{... | collective-permute-start | bytes 442376 | tf_op jit(solution)/shard_map/patch_gradients/ppermute | solution.py:69
  771.8 25.6 %collective-permute-start.66 = (f32[1,384]{1,0:T(1,128)S(1)}, f32[1,384]{1,0:T(1,128)S(1)}, u32[]{:S(2)}, u32[]{:S(2)}) collective-permute-start(f32[1,384]{1,0:T(1,128)S(1)} %broadcast_in_dim.32), channel_id=1, source_target_pairs={{0,4},{4,0},{8,12},{12,8},{16,20},{20,16},{24,28},{28,24},{1,5},{5... | collective-permute-start | bytes 4616 | tf_op jit(solution)/shard_map/patch_gradients/ppermute | solution.py:69
  811.8 24.9 %collective-permute-start.65 = (bf16[64,1536]{1,0:T(8,128)(2,1)}, bf16[64,1536]{1,0:T(8,128)(2,1)}, u32[]{:S(2)}, u32[]{:S(2)}) collective-permute-start(bf16[64,1536]{1,0:T(8,128)(2,1)} %fusion.47), channel_id=1, source_target_pairs={{0,2},{1,3},{2,0},{3,1},{4,6},{5,7},{6,4},{7,5},{8,10},{9,11},{10,... | collective-permute-start | bytes 589832 | tf_op jit(solution)/shard_map/patch_gradients/ppermute | solution.py:69
  (128 other events, 1358.3 us)
Sparse Core Ops, SparseCore 0:
  20.0 83.3 all-gather.6
  122.5 181.5 all-gather.8
  554.1 43.1 all-gather.14
  599.9 63.1 all-gather.10
  665.2 48.8 all-gather.12
